TPU v7x, 128 devices: a whole 4x4x4 slice. The times are simulated.
128 devices in a mesh: row: 8 (over x, core), col: 16 (over z, y).
Axes of the slice: x: 4, y: 4, z: 4, core: 2. Of those that a mesh axis runs over, the one named last changes fastest.
Arguments:
- table: bfloat16 [131072, 256], P(('row', 'col')), may hold values from -6 to 6
- home: int32 [65536], P(('row', 'col')), may hold values from 0 to 65535, as said below
- degree: int32 [131072], P(('row', 'col')), may hold values from 2 to 8
- tile_rows: int32 [8, 16, 704], P('row', 'col'), may hold values from 0 to 63, as said below
- tile_cols: int32 [8, 16, 704], P('row', 'col'), may hold values from 0 to 127
- tile_count: int32 [8, 16], P('row', 'col'), may hold values from 88 to 704, as said below
- tile_values: bfloat16 [8, 16, 704, 128, 128], P('row', 'col'), may hold values from 0 to 1
- w_self: bfloat16 [256, 256], replicated, may hold values from -0.375 to 0.375
- w_neigh: bfloat16 [256, 256], replicated, may hold values from -0.375 to 0.375
- bias: bfloat16 [256], replicated, may hold values from -3 to 3
Outputs:
- layer_out: bfloat16 [131072, 256], P(('row', 'col'))
Inputs may be any that keep to these rules, and one draw needn't show every extreme that they name: home is a permutation of the node blocks. Device d in row-major order of (row, col) owns node blocks d * 512 to (d + 1) * 512 - 1. Of the hash blocks of one device's shard at most 6 belong to one owner, and some pair of devices reaches 6 in every draw. Within one grid cell the live slots name distinct (tile_rows, tile_cols) pairs. `tile_count`: one grid cell has exactly 704 live slots; the others have from 88 to 352.
All inputs are finite; a program needn't handle non-finite values.
Results may differ from a plain program's by a relative error of at most 0.02.
Values may be sent and summed in bfloat16 or wider, within the bound.
No kernel may reach another device: no remote copies, remote signals or barrier semaphores. Data moves between devices by JAX's collectives and lax.ppermute only.
A program may use at most 192 MiB of HBM per device.

v0:
```python
import functools

import jax
import jax.numpy as jnp
from jax import lax
from jax.experimental import pallas as pl
from jax.experimental.pallas import tpu as pltpu
from jax.sharding import PartitionSpec as P

SLOT_ROWS = 16
POS_ROW = 12
PAIRS = 8
BLOCK = 2 * PAIRS
BUFS = 8
LIST = 1152
LANES = 384
MB = 1 << 20
VMEM_TILES = 30 * MB


def iota(shape, dim):
    return lax.broadcasted_iota(jnp.int32, shape, dim)


def onehot(mask):
    return jnp.where(mask, 1.0, 0.0).astype(jnp.bfloat16)


def pack_kernel(home_ref, table_ref, out_ref):
    rows = table_ref.shape[0]
    blocks = home_ref.shape[1]
    parts = jnp.where(iota((16, blocks), 0) == 0, home_ref[...] >> 8, home_ref[...] & 255)
    twice = onehot(iota((blocks, rows), 0) == (iota((blocks, rows), 1) >> 1))
    parts = jnp.dot(
        parts.astype(jnp.float32).astype(jnp.bfloat16), twice, preferred_element_type=jnp.float32
    ).astype(jnp.int32)
    home = (parts[:1] << 8) + parts[1:2]
    dest = home >> 9
    pos = home & 511
    dest_f = dest.astype(jnp.float32)
    dest_col = jnp.broadcast_to(dest_f, (128, rows)).T[:, :1]
    before = (dest_col == dest_f) & (iota((rows, rows), 0) < iota((rows, rows), 1))
    rank = jnp.sum(jnp.where(before, 1.0, 0.0), axis=0, keepdims=True).astype(jnp.int32)
    place = dest * SLOT_ROWS + rank
    outs = out_ref.shape[0]
    spread = onehot(iota((outs, rows), 0) == place)
    data = jnp.dot(spread, table_ref[...], preferred_element_type=jnp.float32)
    lane = iota((256, rows), 0)
    high = jnp.broadcast_to(((pos >> 1) + 1).astype(jnp.float32), (256, rows))
    low = jnp.broadcast_to((pos & 1).astype(jnp.float32), (256, rows))
    marks = jnp.where(lane == rank, high, jnp.where(lane == rank + 128, low, 0.0)).astype(
        jnp.bfloat16
    )
    owner = onehot(iota((128, rows), 0) == dest)
    pos_rows = lax.dot_general(
        owner, marks, (((1,), (1,)), ((), ())), preferred_element_type=jnp.float32
    ).astype(jnp.bfloat16)
    lift = onehot(iota((outs, 128), 0) == iota((outs, 128), 1) * SLOT_ROWS + POS_ROW)
    data = data + jnp.dot(lift, pos_rows, preferred_element_type=jnp.float32)
    out_ref[...] = data.astype(jnp.bfloat16)


def unpack_kernel(in_ref, a_ref, b_ref):
    ins = in_ref.shape[0]
    rows = a_ref.shape[0] + b_ref.shape[0]
    data = in_ref[...]
    drop = onehot(iota((128, ins), 1) == iota((128, ins), 0) * SLOT_ROWS + POS_ROW)
    pos_rows = jnp.dot(drop, data, preferred_element_type=jnp.float32).astype(jnp.bfloat16)
    within = onehot(iota((128, ins), 0) == (iota((128, ins), 1) & (SLOT_ROWS - 1)))
    mine = (iota((128, ins), 1) >> 4) == iota((128, ins), 0)

    def lanes(part):
        spread = jnp.dot(part, within, preferred_element_type=jnp.float32)
        return jnp.sum(jnp.where(mine, spread, 0.0), axis=0, keepdims=True).astype(jnp.int32)

    high = lanes(pos_rows[:, :128])
    low = lanes(pos_rows[:, 128:])
    target = 4 * (high - 1) + 2 * low + (iota((1, ins), 1) & 1)
    pick = onehot(iota((rows, ins), 0) == target)
    owned = jnp.dot(pick, data, preferred_element_type=jnp.float32).astype(jnp.bfloat16)
    a_ref[...] = owned[: rows // 2]
    b_ref[...] = owned[rows // 2 :]


def ring_order(step):
    return jnp.where(step == 0, 0, jnp.where(step == 3, 1, jnp.where(step == 1, 2, 3)))


def plan_kernel(where_ref, count_ref, rows_ref, cols_ref, code_ref, start_ref):
    slots = rows_ref.shape[1]
    count = count_ref[0]
    x, core, z, y = where_ref[0], where_ref[1], where_ref[2], where_ref[3]
    row = rows_ref[...]
    col = cols_ref[...]
    source = col >> 3
    order_z = ring_order(((source >> 2) - z) & 3)
    order_y = ring_order(((source & 3) - y) & 3)
    half = (col >> 2) & 1
    outer = jnp.where(half == 0, order_z, order_y)
    inner = jnp.where(half == 0, order_y, order_z)
    stage = jnp.where((outer == 1) == (inner < 2), 1, 2)
    stage = jnp.where(outer == 3, 3, jnp.where(outer == 0, 0, stage))
    tile = half * 16 + inner * 4 + (col & 3)
    owner = row >> 3
    dx = ((owner >> 1) - x) & 3
    order_x = jnp.where(dx == 2, 0, jnp.where(dx == 1, 1, jnp.where(dx == 3, 2, 3)))
    own = (owner & 1) == core
    chunk = jnp.where(order_x == 0, jnp.where(own, 1, 0), jnp.where(own, 4, 1) + order_x)
    key = stage * 64 + chunk * 8 + (row & 7)
    slot = iota((1, slots), 1)
    key = jnp.where(slot < count, key, 511)
    code = ((chunk * 8 + (row & 7)) << 18) + (slot << 8) + tile + 1

    def column(v):
        return jnp.broadcast_to(v.astype(jnp.float32), (128, slots)).T

    key_row = key.astype(jnp.float32)
    key_col = column(key)[:, :1]
    code_col = column(code)[:, :1]
    same = (key_col == key_row) & (iota((slots, slots), 1) < iota((slots, slots), 0))
    rank = jnp.sum(jnp.where(same, 1.0, 0.0), axis=1, keepdims=True)
    bucket = iota((slots, LANES), 1).astype(jnp.float32)
    member = key_col == bucket
    cnt = jnp.sum(jnp.where(member, 1.0, 0.0), axis=0, keepdims=True).astype(jnp.int32)
    pairs = jnp.broadcast_to((cnt + 1) >> 1, (16, LANES)).astype(jnp.float32).astype(jnp.bfloat16)
    a, b = iota((LANES, LANES), 0), iota((LANES, LANES), 1)

    def region(k):
        late = jnp.where(k < 232, 4, jnp.where(k < 256, 5, 6))
        return jnp.where(k < 192, k >> 6, jnp.where(k < 208, 3, late))

    same_region = region(a) == region(b)
    opens = (a == 0) | (a == 64) | (a == 128) | (a == 192) | (a == 208) | (a == 232)
    inside = jnp.dot(pairs, onehot(same_region & (a < b)), preferred_element_type=jnp.float32)
    total = jnp.dot(pairs, onehot(same_region), preferred_element_type=jnp.float32)
    blocks = ((total.astype(jnp.int32) + (PAIRS - 1)) >> 3).astype(jnp.float32)
    blocks = blocks.astype(jnp.bfloat16)
    ahead = jnp.dot(
        blocks, onehot(opens & (region(a) < region(b))), preferred_element_type=jnp.float32
    )
    begin = (ahead * BLOCK + inside * 2.0)[:1]
    base = jnp.sum(jnp.where(member, begin, 0.0), axis=1, keepdims=True)
    live = iota((slots, 1), 0) < count
    place = jnp.where(live, base + rank, -1.0)
    lists = code_ref.shape[1]
    hit = place == iota((slots, lists), 1).astype(jnp.float32)
    code_ref[...] = jnp.sum(jnp.where(hit, code_col, 0.0), axis=0, keepdims=True).astype(jnp.int32)
    start_ref[...] = ahead[:1].astype(jnp.int32)


def tiles_kernel(buckets, opening, n_pieces, make_panel, outs, *refs):
    code_ref, start_ref, weights = refs[:3]
    k = 3
    pieces = refs[k : k + n_pieces]
    k += n_pieces
    if not n_pieces:
        panel = refs[k]
        k += 1
    if not opening:
        k += 2
    acc, wbuf = refs[k : k + 2]
    k += 2
    if make_panel:
        panel = refs[k]
        k += 1
    out_refs = refs[k : k + len(outs)]
    k += len(outs)
    if n_pieces and not make_panel:
        panel = refs[k]
        k += 1
    wsem = refs[k]
    first = start_ref[buckets[0]]
    last = start_ref[buckets[1]]
    total = start_ref[256]
    ahead = BUFS - 1

    copies = []
    if n_pieces:
        psem = refs[k + 1]
        offset = 1
        for i, piece in enumerate(pieces):
            n = piece.shape[0]
            copies.append(pltpu.make_async_copy(piece, panel.at[pl.ds(offset, n)], psem.at[i]))
            offset += n
        for c in copies:
            c.start()
        panel[0] = jnp.zeros(panel.shape[1:], panel.dtype)

    def fetch(block):
        slot = lax.rem(block, BUFS)
        for i in range(BLOCK):
            s = (code_ref[block * BLOCK + i] >> 8) & 1023
            pltpu.make_async_copy(weights.at[s], wbuf.at[slot, i], wsem.at[slot]).start()

    def arrive(block):
        slot = lax.rem(block, BUFS)
        pltpu.make_async_copy(weights.at[pl.ds(0, BLOCK)], wbuf.at[slot], wsem.at[slot]).wait()

    if opening:
        for i in range(ahead):
            pl.when(first + i < total)(functools.partial(fetch, first + i))

        def clear(i, _):
            acc[i] = jnp.zeros(acc.shape[1:], acc.dtype)
            return 0

        lax.fori_loop(0, acc.shape[0], clear, 0)
    fetched = first if opening else first + ahead
    for c in copies:
        c.wait()

    def run_block(block, _):
        pl.when(block + ahead < total)(functools.partial(fetch, block + ahead))
        pl.when(block >= fetched)(functools.partial(arrive, block))
        slot = lax.rem(block, BUFS)
        for u in range(PAIRS):
            c0 = code_ref[block * BLOCK + 2 * u]
            c1 = code_ref[block * BLOCK + 2 * u + 1]
            w = jnp.concatenate([wbuf[slot, 2 * u], wbuf[slot, 2 * u + 1]], axis=1)
            f = jnp.concatenate([panel[c0 & 255], panel[c1 & 255]], axis=0)
            acc[c0 >> 18] += jnp.dot(w, f, preferred_element_type=jnp.float32)
        return 0

    lax.fori_loop(first, last, run_block, 0)
    for out, (lo, n) in zip(out_refs, outs):

        def give(i, _, out=out, lo=lo):
            out[i] = acc[lo + i].astype(out.dtype)
            return 0

        lax.fori_loop(0, n, give, 0)
    for i in range(ahead):
        pl.when((last + i < total) & (last + i >= fetched))(functools.partial(arrive, last + i))


def run_tiles(buckets, code, start, weights, pieces=(), panel=None, state=None, make_panel=False, outs=()):
    any_spec = pl.BlockSpec(memory_space=pl.ANY)
    vmem = pl.BlockSpec(memory_space=pltpu.VMEM)
    smem = pl.BlockSpec(memory_space=pltpu.SMEM)
    t = weights.shape[1]
    pieces = [p.reshape(-1, t, p.shape[-1]) for p in pieces]
    n = len(pieces)
    tiles = sum(p.shape[0] for p in pieces) + 1
    f = (pieces[0] if n else panel).shape[2]
    args = [code, start, weights, *pieces]
    in_specs = [smem, smem, any_spec] + [any_spec] * n
    if panel is not None:
        args.append(panel)
        in_specs.append(vmem)
    aliases = {}
    if state is not None:
        aliases = {len(args): 0, len(args) + 1: 1}
        args += list(state)
        in_specs += [vmem, vmem]
    out_shape = [
        pltpu.VMEM((64, t, f), jnp.float32),
        pltpu.VMEM((BUFS, BLOCK, t, t), jnp.bfloat16),
    ]
    if make_panel:
        out_shape.append(pltpu.VMEM((tiles, t, f), jnp.bfloat16))
    out_shape += [pltpu.VMEM((k, t, f), jnp.bfloat16) for _, k in outs]
    scratch = [pltpu.VMEM((tiles, t, f), jnp.bfloat16)] if n and not make_panel else []
    scratch.append(pltpu.SemaphoreType.DMA((BUFS,)))
    if n:
        scratch.append(pltpu.SemaphoreType.DMA((n,)))
    share = 352 * (buckets[1] - buckets[0]) // 256
    return pl.pallas_call(
        functools.partial(tiles_kernel, buckets, state is None, n, make_panel, outs),
        out_shape=out_shape,
        in_specs=in_specs,
        out_specs=[vmem] * len(out_shape),
        scratch_shapes=scratch,
        input_output_aliases=aliases,
        compiler_params=pltpu.CompilerParams(vmem_limit_bytes=VMEM_TILES),
        cost_estimate=pl.CostEstimate(
            flops=share * 4 * t * t * f, bytes_accessed=share * 4 * t * t, transcendentals=0
        ),
        name=f"tiles_{buckets[0]}",
    )(*args)


def col_perm(dz, dy):
    return [(z * 4 + y, (z + dz) % 4 * 4 + (y + dy) % 4) for z in range(4) for y in range(4)]


def row_perm(dx, flip=0):
    return [(x * 2 + c, (x + dx) % 4 * 2 + (c ^ flip)) for x in range(4) for c in range(2)]


def per_device(
    table, home, degree, tile_rows, tile_cols, tile_count, tile_values, w_self, w_neigh, bias
):
    rows, width = table.shape
    devices = lax.axis_size("row") * lax.axis_size("col")
    slots, tile = tile_values.shape[2:4]
    row_index = lax.axis_index("row")
    col_index = lax.axis_index("col")
    where = jnp.stack([row_index // 2, row_index % 2, col_index // 4, col_index % 4]).astype(
        jnp.int32
    )
    vmem = pl.BlockSpec(memory_space=pltpu.VMEM)
    smem = pl.BlockSpec(memory_space=pltpu.SMEM)
    big = pltpu.CompilerParams(vmem_limit_bytes=48 * MB)

    outgoing = pl.pallas_call(
        pack_kernel,
        out_shape=jax.ShapeDtypeStruct((devices * SLOT_ROWS, width), jnp.bfloat16),
        in_specs=[vmem, vmem],
        out_specs=vmem,
        compiler_params=big,
        name="pack",
    )(home.reshape(1, -1), table)
    incoming = lax.all_to_all(
        outgoing.reshape(devices, SLOT_ROWS, width),
        ("row", "col"),
        split_axis=0,
        concat_axis=0,
        tiled=True,
    )
    half = rows // 2
    quarter = half // 2
    a0, b0 = pl.pallas_call(
        unpack_kernel,
        out_shape=(jax.ShapeDtypeStruct((half, width), jnp.bfloat16),) * 2,
        in_specs=[vmem],
        out_specs=(vmem, vmem),
        compiler_params=big,
        name="unpack",
    )(incoming.reshape(devices * SLOT_ROWS, width))

    code, start = pl.pallas_call(
        plan_kernel,
        out_shape=(
            jax.ShapeDtypeStruct((1, LIST), jnp.int32),
            jax.ShapeDtypeStruct((1, LANES), jnp.int32),
        ),
        in_specs=[smem, smem, vmem, vmem],
        out_specs=(vmem, vmem),
        compiler_params=big,
        name="plan",
    )(where, tile_count.reshape(1), tile_rows.reshape(1, slots), tile_cols.reshape(1, slots))
    code = code.reshape(LIST)
    start = start.reshape(LANES)
    weights = tile_values.reshape(slots, tile, tile)

    def send(v, dz, dy):
        return lax.ppermute(v, "col", col_perm(dz, dy))

    def cat(*parts):
        return jnp.concatenate(parts, axis=0)

    ap, am = send(a0, 0, 1), send(a0, 0, -1)
    bp, bm = send(b0, 1, 0), send(b0, -1, 0)
    a_hi = cat(am, send(ap[:quarter], 0, 1), send(am[quarter:], 0, -1))
    b_hi = cat(bm, send(bp[:quarter], 1, 0), send(bm[quarter:], -1, 0))
    a_hi, b_hi, ap, bp, code, start = lax.optimization_barrier((a_hi, b_hi, ap, bp, code, start))
    a_lo, b_lo = cat(a0, ap), cat(b0, bp)
    lists = (code, start, weights)
    a_lo_p, a_hi_m = send(a_lo, 1, 0), send(a_hi, -1, 0)
    b_lo_p, b_hi_m = send(b_lo, 0, 1), send(b_hi, 0, -1)
    state = run_tiles((0, 64), *lists, [a_lo, a_hi, b_lo, b_hi])
    a_lo, a_hi, b_lo, b_hi, *state = lax.optimization_barrier((a_lo, a_hi, b_lo, b_hi, *state))
    a_hi_p, a_lo_m = send(a_hi, 1, 0), send(a_lo, -1, 0)
    b_hi_p, b_lo_m = send(b_hi, 0, 1), send(b_lo, 0, -1)
    state = run_tiles((64, 128), *lists, [a_lo_p, a_hi_m, b_lo_p, b_hi_m], state=state)
    a_lo_p, a_hi_m, b_lo_p, b_hi_m, *state = lax.optimization_barrier(
        (a_lo_p, a_hi_m, b_lo_p, b_hi_m, *state)
    )
    far = [send(a_lo_p, 1, 0), send(a_hi_m, -1, 0), send(b_lo_p, 0, 1), send(b_hi_m, 0, -1)]
    state = run_tiles((128, 192), *lists, [a_lo_m, a_hi_p, b_lo_m, b_hi_p], state=state)
    f32 = jnp.float32

    def over(v, dx, flip=0):
        return lax.ppermute(v, "row", row_perm(dx, flip))

    *state, panel, other_far, mine_far = run_tiles(
        (192, 208), *lists, far, state=state, make_panel=True, outs=((0, 8), (8, 8))
    )
    got_far = over(other_far.reshape(rows, width), 0, 1)
    *state, other_rest = run_tiles((208, 232), *lists, panel=panel, state=state, outs=((16, 24),))
    across = (mine_far.reshape(rows, width).astype(f32) + got_far.astype(f32)).astype(jnp.bfloat16)
    across, *state = lax.optimization_barrier((across, *state))
    from_minus, from_plus = over(across[:half], 1), over(across[half:], -1)
    got_rest = over(other_rest.reshape(3, rows, width), 0, 1)
    *state, mine_rest = run_tiles((232, 256), *lists, panel=panel, state=state, outs=((40, 24),))
    mine_rest = mine_rest.reshape(3, rows, width)
    both = [mine_rest[i].astype(f32) + got_rest[i].astype(f32) for i in range(3)]
    to_plus = cat(both[0][:half] + from_minus.astype(f32), both[0][half:]).astype(jnp.bfloat16)
    to_minus = cat(both[1][:half], both[1][half:] + from_plus.astype(f32)).astype(jnp.bfloat16)
    summed = both[2] + over(to_plus, 1).astype(f32) + over(to_minus, -1).astype(f32)

    neighbor_mean = (summed / degree.astype(f32)[:, None]).astype(jnp.bfloat16)
    total = jnp.dot(cat(a0, b0), w_self, preferred_element_type=f32)
    total = total + jnp.dot(neighbor_mean, w_neigh, preferred_element_type=f32)
    total = total + bias.astype(f32)[None, :]
    return jnp.maximum(total, f32(0.0)).astype(jnp.bfloat16)


def solution(mesh):
    in_specs = (
        P(("row", "col"), None),
        P(("row", "col")),
        P(("row", "col")),
        P("row", "col", None),
        P("row", "col", None),
        P("row", "col"),
        P("row", "col", None, None, None),
        P(),
        P(),
        P(),
    )
    out_specs = P(("row", "col"), None)
    return jax.shard_map(
        per_device, mesh=mesh, in_specs=in_specs, out_specs=out_specs, check_vma=False
    )
```

profile of v0, /device:TPU:6, one launch (start us, length us, event | category | flops | bytes accessed | tf_op | source)
XLA Modules:
  0.0 128.7 jit_solution(13895811235867131778)
XLA Ops:
  0.0 1.1 copy-done.1
  1.1 0.7 copy-done.4
  1.8 2.7 %pack.1 = bf16[2048,256]{1,0:T(8,128)(2,1)S(1)} custom-call(s32[1,512]{1,0:T(1,128)S(1)} %bitcast.79, bf16[1024,256]{1,0:T(8,128)(2,1)S(1)} %copy-done.1), custom_call_target="tpu_custom_call" | custom-call | tf_op jit(solution)/shard_map/pack/pallas_call | solution.py:305
  4.5 28.4 %all_to_all.5 = bf16[128,16,256]{2,1,0:T(8,128)(2,1)S(1)} all-to-all(bf16[128,16,256]{2,1,0:T(8,128)(2,1)S(1)} %bitcast.60), channel_id=1, replica_groups=mesh['row'=8,'col'=16] {'row','col'}, dimensions={0} | all-to-all | bytes 2097152 | tf_op jit(solution)/shard_map/all_to_all | solution.py:313
  32.9 2.1 %unpack.1 = (bf16[512,256]{1,0:T(8,128)(2,1)S(1)}, bf16[512,256]{1,0:T(8,128)(2,1)S(1)}) custom-call(bf16[2048,256]{1,0:T(8,128)(2,1)S(1)} %bitcast.59), custom_call_target="tpu_custom_call" | custom-call | tf_op jit(solution)/shard_map/unpack/pallas_call | solution.py:322
  35.0 0.9 collective-permute-start.5
  35.9 2.4 %collective-permute-start.4 = (bf16[512,256]{1,0:T(8,128)(2,1)S(1)}, bf16[512,256]{1,0:T(8,128)(2,1)S(1)}, u32[]{:S(2)}, u32[]{:S(2)}) collective-permute-start(bf16[512,256]{1,0:T(8,128)(2,1)S(1)} %get-tuple-element.46), channel_id=1, source_target_pairs={{0,12},{1,13},{2,14},{3,15},{4,0},{5,1},{6,2},{7,3},{8,4},{9,5},{1... | collective-permute-start | bytes 786440 | tf_op jit(solution)/shard_map/ppermute | solution.py:347
  38.3 0.6 collective-permute-start.1
  38.9 2.6 %collective-permute-start = (bf16[512,256]{1,0:T(8,128)(2,1)S(1)}, bf16[512,256]{1,0:T(8,128)(2,1)S(1)}, u32[]{:S(2)}, u32[]{:S(2)}) collective-permute-start(bf16[512,256]{1,0:T(8,128)(2,1)S(1)} %get-tuple-element.45), channel_id=1, source_target_pairs={{0,3},{1,0},{2,1},{3,2},{4,7},{5,4},{6,5},{7,6},{8,11},{9,8},{10,9... | collective-permute-start | bytes 786440 | tf_op jit(solution)/shard_map/ppermute | solution.py:347
  42.3 1.8 %plan.1 = (s32[1,1152]{1,0:T(1,128)S(1)}, s32[1,384]{1,0:T(1,128)S(1)}) custom-call(s32[4]{0:T(128)S(1)} %pad_add_fusion.where_ref, s32[1]{0:T(128)} %bitcast.58.count_ref, s32[1,704]{1,0:T(1,128)S(1)} %bitcast.77, s32[1,704]{1,0:T(1,128)S(1)} %bitcast.78), custom_call_target="tpu_custom_call" | custom-call | tf_op jit(solution)/shard_map/plan/pallas_call | solution.py:331
  44.1 0.1 collective-permute-done.5
  44.4 3.3 %collective-permute-start.7 = (bf16[256,256]{1,0:T(8,128)(2,1)S(1)}, bf16[256,256]{1,0:T(8,128)(2,1)S(1)}, u32[]{:S(2)}, u32[]{:S(2)}) collective-permute-start(bf16[256,256]{1,0:T(8,128)(2,1)S(1)} %slice.72), channel_id=1, source_target_pairs={{0,12},{1,13},{2,14},{3,15},{4,0},{5,1},{6,2},{7,3},{8,4},{9,5},{1... | collective-permute-start | bytes 393224 | tf_op jit(solution)/shard_map/ppermute | solution.py:347
  47.7 0.7 collective-permute-start.2
  48.4 2.7 %collective-permute-start.3 = (bf16[256,256]{1,0:T(8,128)(2,1)S(1)}, bf16[256,256]{1,0:T(8,128)(2,1)S(1)}, u32[]{:S(2)}, u32[]{:S(2)}) collective-permute-start(bf16[256,256]{1,0:T(8,128)(2,1)S(1)} %slice.70), channel_id=1, source_target_pairs={{0,3},{1,0},{2,1},{3,2},{4,7},{5,4},{6,5},{7,6},{8,11},{9,8},{10,9... | collective-permute-start | bytes 393224 | tf_op jit(solution)/shard_map/ppermute | solution.py:347
  51.2 2.8 %collective-permute-done.2 = bf16[256,256]{1,0:T(8,128)(2,1)S(1)} collective-permute-done((bf16[256,256]{1,0:T(8,128)(2,1)S(1)}, bf16[256,256]{1,0:T(8,128)(2,1)S(1)}, u32[]{:S(2)}, u32[]{:S(2)}) %collective-permute-start.2) | collective-permute-done | bytes 131104 | tf_op jit(solution)/shard_map/ppermute | solution.py:347
  54.0 0.3 collective-permute-start.10
  54.4 3.2 %collective-permute-start.9 = (bf16[1024,256]{1,0:T(8,128)(2,1)S(1)}, bf16[1024,256]{1,0:T(8,128)(2,1)S(1)}, u32[]{:S(2)}, u32[]{:S(2)}) collective-permute-start(bf16[1024,256]{1,0:T(8,128)(2,1)S(1)} %pad_maximum_fusion), channel_id=1, source_target_pairs={{0,12},{1,13},{2,14},{3,15},{4,0},{5,1},{6,2},{7,3},{8,4},{9,5},{1... | collective-permute-start | bytes 1572872 | tf_op jit(solution)/shard_map/ppermute | solution.py:347
  57.7 3.1 %collective-permute-start.11 = (bf16[1024,256]{1,0:T(8,128)(2,1)S(1)}, bf16[1024,256]{1,0:T(8,128)(2,1)S(1)}, u32[]{:S(2)}, u32[]{:S(2)}) collective-permute-start(bf16[1024,256]{1,0:T(8,128)(2,1)S(1)} %pad_maximum_fusion.1), channel_id=1, source_target_pairs={{0,3},{1,0},{2,1},{3,2},{4,7},{5,4},{6,5},{7,6},{8,11},{9,8},{10,9... | collective-permute-start | bytes 1572872 | tf_op jit(solution)/shard_map/ppermute | solution.py:347
  60.7 6.0 %tiles_0.1 = (f32[64,128,256]{2,1,0:T(8,128)S(1)}, bf16[8,16,128,128]{3,2,1,0:T(8,128)(2,1)S(1)}) custom-call(s32[1152]{0:T(1024)S(1)} %reduce.refs_0_, s32[384]{0:T(512)S(1)} %reduce.1.refs_1_, bf16[704,128,128]{2,1,0:T(8,128)(2,1)} %bitcast.82, bf16[8,128,256]{2,1,0:T(8,128)(2,1)S(1)} %bitcast.64, bf16[8,128,256]{2,1,0:T(8,128)(2,1)S(1)} %bitcast.62, ...), custom_call_target="tpu_custom_call" | custom-call | flops 1476395008 | bytes 5767168 | tf_op jit(solution)/shard_map/tiles_0/pallas_call | solution.py:267
  66.8 0.3 collective-permute-start.16
  67.0 2.0 %collective-permute-start.17 = (bf16[1024,256]{1,0:T(8,128)(2,1)S(1)}, bf16[1024,256]{1,0:T(8,128)(2,1)S(1)}, u32[]{:S(2)}, u32[]{:S(2)}) collective-permute-start(bf16[1024,256]{1,0:T(8,128)(2,1)S(1)} %pad_maximum_fusion), channel_id=1, source_target_pairs={{0,4},{1,5},{2,6},{3,7},{4,8},{5,9},{6,10},{7,11},{8,12},{9,13},{1... | collective-permute-start | bytes 1572872 | tf_op jit(solution)/shard_map/ppermute | solution.py:347
  69.0 1.7 %collective-permute-start.18 = (bf16[1024,256]{1,0:T(8,128)(2,1)S(1)}, bf16[1024,256]{1,0:T(8,128)(2,1)S(1)}, u32[]{:S(2)}, u32[]{:S(2)}) collective-permute-start(bf16[1024,256]{1,0:T(8,128)(2,1)S(1)} %constant_dynamic-update-slice_fusion.2), channel_id=1, source_target_pairs={{0,3},{1,0},{2,1},{3,2},{4,7},{5,4},{6,5},{7,6},{8,11},{9,8},{10,9... | collective-permute-start | bytes 1572872 | tf_op jit(solution)/shard_map/ppermute | solution.py:347
  70.7 0.3 collective-permute-start.19
  71.1 4.6 %tiles_64.1 = (f32[64,128,256]{2,1,0:T(8,128)S(1)}, bf16[8,16,128,128]{3,2,1,0:T(8,128)(2,1)S(1)}) custom-call(s32[1152]{0:T(1024)S(1)} %reduce.refs_0_, s32[384]{0:T(512)S(1)} %reduce.1.refs_1_, bf16[704,128,128]{2,1,0:T(8,128)(2,1)} %bitcast.83, bf16[8,128,256]{2,1,0:T(8,128)(2,1)S(1)} %bitcast.67, ...), custom_call_target="tpu_custom_call", output_to_operand_aliasing={{0}: (7, {}), {1}: (8, {})} | custom-call | flops 1476395008 | bytes 5767168 | tf_op jit(solution)/shard_map/tiles_64/pallas_call | solution.py:267
  75.8 2.2 %collective-permute-done.16 = bf16[1024,256]{1,0:T(8,128)(2,1)S(1)} collective-permute-done((bf16[1024,256]{1,0:T(8,128)(2,1)S(1)}, bf16[1024,256]{1,0:T(8,128)(2,1)S(1)}, u32[]{:S(2)}, u32[]{:S(2)}) %collective-permute-start.16) | collective-permute-done | bytes 524320 | tf_op jit(solution)/shard_map/ppermute | solution.py:347
  77.9 3.7 %collective-permute-start.13 = (bf16[1024,256]{1,0:T(8,128)(2,1)S(1)}, bf16[1024,256]{1,0:T(8,128)(2,1)S(1)}, u32[]{:S(2)}, u32[]{:S(2)}) collective-permute-start(bf16[1024,256]{1,0:T(8,128)(2,1)S(1)} %collective-permute-done.9), channel_id=1, source_target_pairs={{0,12},{1,13},{2,14},{3,15},{4,0},{5,1},{6,2},{7,3},{8,4},{9,5},{1... | collective-permute-start | bytes 1572872 | tf_op jit(solution)/shard_map/ppermute | solution.py:347
  81.6 1.5 %collective-permute-done.17 = bf16[1024,256]{1,0:T(8,128)(2,1)S(1)} collective-permute-done((bf16[1024,256]{1,0:T(8,128)(2,1)S(1)}, bf16[1024,256]{1,0:T(8,128)(2,1)S(1)}, u32[]{:S(2)}, u32[]{:S(2)}) %collective-permute-start.17) | collective-permute-done | bytes 524320 | tf_op jit(solution)/shard_map/ppermute | solution.py:347
  83.2 3.2 %collective-permute-start.15 = (bf16[1024,256]{1,0:T(8,128)(2,1)S(1)}, bf16[1024,256]{1,0:T(8,128)(2,1)S(1)}, u32[]{:S(2)}, u32[]{:S(2)}) collective-permute-start(bf16[1024,256]{1,0:T(8,128)(2,1)S(1)} %collective-permute-done.11), channel_id=1, source_target_pairs={{0,3},{1,0},{2,1},{3,2},{4,7},{5,4},{6,5},{7,6},{8,11},{9,8},{10,9... | collective-permute-start | bytes 1572872 | tf_op jit(solution)/shard_map/ppermute | solution.py:347
  86.4 4.8 %tiles_128.1 = (f32[64,128,256]{2,1,0:T(8,128)S(1)}, bf16[8,16,128,128]{3,2,1,0:T(8,128)(2,1)S(1)}) custom-call(s32[1152]{0:T(1024)S(1)} %reduce.refs_0_, s32[384]{0:T(512)S(1)} %reduce.1.refs_1_, bf16[704,128,128]{2,1,0:T(8,128)(2,1)} %bitcast.84, bf16[8,128,256]{2,1,0:T(8,128)(2,1)S(1)} %bitcast.69, ...), custom_call_target="tpu_custom_call", output_to_operand_aliasing={{0}: (7, {}), {1}: (8, {})} | custom-call | flops 1476395008 | bytes 5767168 | tf_op jit(solution)/shard_map/tiles_128/pallas_call | solution.py:267
  91.2 2.4 %collective-permute-done.14 = bf16[1024,256]{1,0:T(8,128)(2,1)S(1)} collective-permute-done((bf16[1024,256]{1,0:T(8,128)(2,1)S(1)}, bf16[1024,256]{1,0:T(8,128)(2,1)S(1)}, u32[]{:S(2)}, u32[]{:S(2)}) %collective-permute-start.14) | collective-permute-done | bytes 524320 | tf_op jit(solution)/shard_map/ppermute | solution.py:347
  93.6 2.3 %tiles_192.1 = (f32[64,128,256]{2,1,0:T(8,128)S(1)}, bf16[8,16,128,128]{3,2,1,0:T(8,128)(2,1)S(1)}, bf16[33,128,256]{2,1,0:T(8,128)(2,1)S(1)}, bf16[8,128,256]{2,1,0:T(8,128)(2,1)S(1)}, bf16[8,128,256]{2,1,0:T(8,128)(2,1)S(1)}) custom-call(s32[1152]{0:T(1024)S(1)} %reduce.refs_0_, ...), custom_call_target="tpu_custom_call", output_to_operand_aliasing={{0}: (7, {}), {1}: (8, {})} | custom-call | flops 369098752 | bytes 1441792 | tf_op jit(solution)/shard_map/tiles_192/pallas_call | solution.py:267
  95.9 2.4 %tiles_208.1 = (f32[64,128,256]{2,1,0:T(8,128)S(1)}, bf16[8,16,128,128]{3,2,1,0:T(8,128)(2,1)S(1)}, bf16[24,128,256]{2,1,0:T(8,128)(2,1)S(1)}) custom-call(s32[1152]{0:T(1024)S(1)} %reduce.refs_0_, s32[384]{0:T(512)S(1)} %reduce.1.refs_1_, bf16[704,128,128]{2,1,0:T(8,128)(2,1)} %bitcast.86, ...), custom_call_target="tpu_custom_call", output_to_operand_aliasing={{0}: (4, {}), {1}: (5, {})} | custom-call | flops 553648128 | bytes 2162688 | tf_op jit(solution)/shard_map/tiles_208/pallas_call | solution.py:267
  98.3 0.1 collective-permute-start.21
  98.4 0.5 collective-permute-start.20
  98.8 3.6 %collective-permute-done.20 = bf16[1024,256]{1,0:T(8,128)(2,1)S(1)} collective-permute-done((bf16[1024,256]{1,0:T(8,128)(2,1)S(1)}, bf16[1024,256]{1,0:T(8,128)(2,1)S(1)}, u32[]{:S(2)}, u32[]{:S(2)}) %collective-permute-start.20) | collective-permute-done | bytes 524320 | tf_op jit(solution)/shard_map/ppermute | solution.py:374
  102.5 0.2 fusion.6
  102.7 0.2 collective-permute-start.22
  102.9 1.9 %collective-permute-start.24 = (bf16[512,256]{1,0:T(8,128)(2,1)S(1)}, bf16[512,256]{1,0:T(8,128)(2,1)S(1)}, u32[]{:S(2)}, u32[]{:S(2)}) collective-permute-start(bf16[512,256]{1,0:T(8,128)(2,1)S(1)} %get-tuple-element.91), channel_id=1, source_target_pairs={{0,96},{16,112},{32,0},{48,16},{64,32},{80,48},{96,64},{112,80},{1... | collective-permute-start | bytes 786440 | tf_op jit(solution)/shard_map/ppermute | solution.py:374
  104.8 2.3 %tiles_232.1 = (f32[64,128,256]{2,1,0:T(8,128)S(1)}, bf16[8,16,128,128]{3,2,1,0:T(8,128)(2,1)S(1)}, bf16[24,128,256]{2,1,0:T(8,128)(2,1)S(1)}) custom-call(s32[1152]{0:T(1024)S(1)} %reduce.refs_0_, s32[384]{0:T(512)S(1)} %reduce.1.refs_1_, bf16[704,128,128]{2,1,0:T(8,128)(2,1)} %bitcast.87, ...), custom_call_target="tpu_custom_call", output_to_operand_aliasing={{0}: (4, {}), {1}: (5, {})} | custom-call | flops 553648128 | bytes 2162688 | tf_op jit(solution)/shard_map/tiles_232/pallas_call | solution.py:267
  107.2 0.1 fusion.17
  107.4 0.3 convert_add_fusion.1
  107.8 3.4 %collective-permute-done.22 = bf16[512,256]{1,0:T(8,128)(2,1)S(1)} collective-permute-done((bf16[512,256]{1,0:T(8,128)(2,1)S(1)}, bf16[512,256]{1,0:T(8,128)(2,1)S(1)}, u32[]{:S(2)}, u32[]{:S(2)}) %collective-permute-start.22) | collective-permute-done | bytes 262176 | tf_op jit(solution)/shard_map/ppermute | solution.py:374
  111.3 1.6 %collective-permute-start.23 = (bf16[1024,256]{1,0:T(8,128)(2,1)S(1)}, bf16[1024,256]{1,0:T(8,128)(2,1)S(1)}, u32[]{:S(2)}, u32[]{:S(2)}) collective-permute-start(bf16[1024,256]{1,0:T(8,128)(2,1)S(1)} %pad_maximum_fusion.2), channel_id=1, source_target_pairs={{0,32},{16,48},{32,64},{48,80},{64,96},{80,112},{96,0},{112,16},{1... | collective-permute-start | bytes 1572872 | tf_op jit(solution)/shard_map/ppermute | solution.py:374
  113.0 0.6 collective-permute-start.25
  113.6 0.3 fusion.11
  113.9 10.6 %collective-permute-done.23 = bf16[1024,256]{1,0:T(8,128)(2,1)S(1)} collective-permute-done((bf16[1024,256]{1,0:T(8,128)(2,1)S(1)}, bf16[1024,256]{1,0:T(8,128)(2,1)S(1)}, u32[]{:S(2)}, u32[]{:S(2)}) %collective-permute-start.23) | collective-permute-done | bytes 524320 | tf_op jit(solution)/shard_map/ppermute | solution.py:374
  124.5 2.9 %collective-permute-done.25 = bf16[1024,256]{1,0:T(8,128)(2,1)S(1)} collective-permute-done((bf16[1024,256]{1,0:T(8,128)(2,1)S(1)}, bf16[1024,256]{1,0:T(8,128)(2,1)S(1)}, u32[]{:S(2)}, u32[]{:S(2)}) %collective-permute-start.25) | collective-permute-done | bytes 524320 | tf_op jit(solution)/shard_map/ppermute | solution.py:374
  127.4 1.3 %fusion.2 = bf16[1024,256]{1,0:T(8,128)(2,1)} fusion(f32[1024,256]{1,0:T(8,128)S(1)} %fusion.11, bf16[256,256]{1,0:T(8,128)(2,1)S(1)} %copy-done.6, bf16[1024,256]{1,0:T(8,128)(2,1)S(1)} %collective-permute-done.25, bf16[1024,256]{1,0:T(8,128)(2,1)S(1)} %collective-permute-done.23, bf16[1024,256]{1,0:T(8,128)(2,1)S(1)} %bitcast.88, ...), kind=kOutput, calls=%fused_computation.3 | convolution fusion | flops 137625600 | bytes 3806208 | tf_op jit(solution)/shard_map/dot_general | solution.py:394
  (57 shorter events, 0.9 us)
Async XLA Ops:
  0.0 113.6 %copy-start = (bf16[256,256]{1,0:T(8,128)(2,1)S(1)}, bf16[256,256]{1,0:T(8,128)(2,1)}, u32[]{:S(2)}) copy-start(bf16[256,256]{1,0:T(8,128)(2,1)} %param.17) | copy-start | bytes 393220
  0.0 1.1 copy-start.1
  1.1 0.7 copy-start.4
  1.8 40.5 %copy-start.2 = (s32[1,1,704]{2,1,0:T(1,128)S(1)}, s32[1,1,704]{2,1,0:T(1,128)}, u32[]{:S(2)}) copy-start(s32[1,1,704]{2,1,0:T(1,128)} %param.13) | copy-start | bytes 8452
  1.8 40.5 %copy-start.3 = (s32[1,1,704]{2,1,0:T(1,128)S(1)}, s32[1,1,704]{2,1,0:T(1,128)}, u32[]{:S(2)}) copy-start(s32[1,1,704]{2,1,0:T(1,128)} %param.14) | copy-start | bytes 8452
  35.0 9.3 %collective-permute-start.5 = (bf16[512,256]{1,0:T(8,128)(2,1)S(1)}, bf16[512,256]{1,0:T(8,128)(2,1)S(1)}, u32[]{:S(2)}, u32[]{:S(2)}) collective-permute-start(bf16[512,256]{1,0:T(8,128)(2,1)S(1)} %get-tuple-element.46), channel_id=1, source_target_pairs={{0,4},{1,5},{2,6},{3,7},{4,8},{5,9},{6,10},{7,11},{8,12},{9,13},{1... | collective-permute-start | bytes 786440 | tf_op jit(solution)/shard_map/ppermute | solution.py:347
  35.9 8.5 %collective-permute-start.4 = (bf16[512,256]{1,0:T(8,128)(2,1)S(1)}, bf16[512,256]{1,0:T(8,128)(2,1)S(1)}, u32[]{:S(2)}, u32[]{:S(2)}) collective-permute-start(bf16[512,256]{1,0:T(8,128)(2,1)S(1)} %get-tuple-element.46), channel_id=1, source_target_pairs={{0,12},{1,13},{2,14},{3,15},{4,0},{5,1},{6,2},{7,3},{8,4},{9,5},{1... | collective-permute-start | bytes 786440 | tf_op jit(solution)/shard_map/ppermute | solution.py:347
  38.3 9.4 %collective-permute-start.1 = (bf16[512,256]{1,0:T(8,128)(2,1)S(1)}, bf16[512,256]{1,0:T(8,128)(2,1)S(1)}, u32[]{:S(2)}, u32[]{:S(2)}) collective-permute-start(bf16[512,256]{1,0:T(8,128)(2,1)S(1)} %get-tuple-element.45), channel_id=1, source_target_pairs={{0,1},{1,2},{2,3},{3,0},{4,5},{5,6},{6,7},{7,4},{8,9},{9,10},{10,1... | collective-permute-start | bytes 786440 | tf_op jit(solution)/shard_map/ppermute | solution.py:347
  38.9 9.5 %collective-permute-start = (bf16[512,256]{1,0:T(8,128)(2,1)S(1)}, bf16[512,256]{1,0:T(8,128)(2,1)S(1)}, u32[]{:S(2)}, u32[]{:S(2)}) collective-permute-start(bf16[512,256]{1,0:T(8,128)(2,1)S(1)} %get-tuple-element.45), channel_id=1, source_target_pairs={{0,3},{1,0},{2,1},{3,2},{4,7},{5,4},{6,5},{7,6},{8,11},{9,8},{10,9... | collective-permute-start | bytes 786440 | tf_op jit(solution)/shard_map/ppermute | solution.py:347
  44.2 6.9 %collective-permute-start.6 = (bf16[256,256]{1,0:T(8,128)(2,1)S(1)}, bf16[256,256]{1,0:T(8,128)(2,1)S(1)}, u32[]{:S(2)}, u32[]{:S(2)}) collective-permute-start(bf16[256,256]{1,0:T(8,128)(2,1)S(1)} %slice.71), channel_id=1, source_target_pairs={{0,4},{1,5},{2,6},{3,7},{4,8},{5,9},{6,10},{7,11},{8,12},{9,13},{1... | collective-permute-start | bytes 393224 | tf_op jit(solution)/shard_map/ppermute | solution.py:347
  44.4 6.8 %collective-permute-start.7 = (bf16[256,256]{1,0:T(8,128)(2,1)S(1)}, bf16[256,256]{1,0:T(8,128)(2,1)S(1)}, u32[]{:S(2)}, u32[]{:S(2)}) collective-permute-start(bf16[256,256]{1,0:T(8,128)(2,1)S(1)} %slice.72), channel_id=1, source_target_pairs={{0,12},{1,13},{2,14},{3,15},{4,0},{5,1},{6,2},{7,3},{8,4},{9,5},{1... | collective-permute-start | bytes 393224 | tf_op jit(solution)/shard_map/ppermute | solution.py:347
  47.7 6.2 %collective-permute-start.2 = (bf16[256,256]{1,0:T(8,128)(2,1)S(1)}, bf16[256,256]{1,0:T(8,128)(2,1)S(1)}, u32[]{:S(2)}, u32[]{:S(2)}) collective-permute-start(bf16[256,256]{1,0:T(8,128)(2,1)S(1)} %slice.69), channel_id=1, source_target_pairs={{0,1},{1,2},{2,3},{3,0},{4,5},{5,6},{6,7},{7,4},{8,9},{9,10},{10,1... | collective-permute-start | bytes 393224 | tf_op jit(solution)/shard_map/ppermute | solution.py:347
  48.4 5.5 %collective-permute-start.3 = (bf16[256,256]{1,0:T(8,128)(2,1)S(1)}, bf16[256,256]{1,0:T(8,128)(2,1)S(1)}, u32[]{:S(2)}, u32[]{:S(2)}) collective-permute-start(bf16[256,256]{1,0:T(8,128)(2,1)S(1)} %slice.70), channel_id=1, source_target_pairs={{0,3},{1,0},{2,1},{3,2},{4,7},{5,4},{6,5},{7,6},{8,11},{9,8},{10,9... | collective-permute-start | bytes 393224 | tf_op jit(solution)/shard_map/ppermute | solution.py:347
  54.0 13.0 %collective-permute-start.10 = (bf16[1024,256]{1,0:T(8,128)(2,1)S(1)}, bf16[1024,256]{1,0:T(8,128)(2,1)S(1)}, u32[]{:S(2)}, u32[]{:S(2)}) collective-permute-start(bf16[1024,256]{1,0:T(8,128)(2,1)S(1)} %constant_dynamic-update-slice_fusion.2), channel_id=1, source_target_pairs={{0,1},{1,2},{2,3},{3,0},{4,5},{5,6},{6,7},{7,4},{8,9},{9,10},{10,1... | collective-permute-start | bytes 1572872 | tf_op jit(solution)/shard_map/ppermute | solution.py:347
  54.4 14.7 %collective-permute-start.8 = (bf16[1024,256]{1,0:T(8,128)(2,1)S(1)}, bf16[1024,256]{1,0:T(8,128)(2,1)S(1)}, u32[]{:S(2)}, u32[]{:S(2)}) collective-permute-start(bf16[1024,256]{1,0:T(8,128)(2,1)S(1)} %constant_dynamic-update-slice_fusion), channel_id=1, source_target_pairs={{0,4},{1,5},{2,6},{3,7},{4,8},{5,9},{6,10},{7,11},{8,12},{9,13},{1... | collective-permute-start | bytes 1572872 | tf_op jit(solution)/shard_map/ppermute | solution.py:347
  54.4 16.3 %collective-permute-start.9 = (bf16[1024,256]{1,0:T(8,128)(2,1)S(1)}, bf16[1024,256]{1,0:T(8,128)(2,1)S(1)}, u32[]{:S(2)}, u32[]{:S(2)}) collective-permute-start(bf16[1024,256]{1,0:T(8,128)(2,1)S(1)} %pad_maximum_fusion), channel_id=1, source_target_pairs={{0,12},{1,13},{2,14},{3,15},{4,0},{5,1},{6,2},{7,3},{8,4},{9,5},{1... | collective-permute-start | bytes 1572872 | tf_op jit(solution)/shard_map/ppermute | solution.py:347
  57.7 13.4 %collective-permute-start.11 = (bf16[1024,256]{1,0:T(8,128)(2,1)S(1)}, bf16[1024,256]{1,0:T(8,128)(2,1)S(1)}, u32[]{:S(2)}, u32[]{:S(2)}) collective-permute-start(bf16[1024,256]{1,0:T(8,128)(2,1)S(1)} %pad_maximum_fusion.1), channel_id=1, source_target_pairs={{0,3},{1,0},{2,1},{3,2},{4,7},{5,4},{6,5},{7,6},{8,11},{9,8},{10,9... | collective-permute-start | bytes 1572872 | tf_op jit(solution)/shard_map/ppermute | solution.py:347
  66.8 11.2 %collective-permute-start.16 = (bf16[1024,256]{1,0:T(8,128)(2,1)S(1)}, bf16[1024,256]{1,0:T(8,128)(2,1)S(1)}, u32[]{:S(2)}, u32[]{:S(2)}) collective-permute-start(bf16[1024,256]{1,0:T(8,128)(2,1)S(1)} %constant_dynamic-update-slice_fusion), channel_id=1, source_target_pairs={{0,12},{1,13},{2,14},{3,15},{4,0},{5,1},{6,2},{7,3},{8,4},{9,5},{1... | collective-permute-start | bytes 1572872 | tf_op jit(solution)/shard_map/ppermute | solution.py:347
  67.0 16.1 %collective-permute-start.17 = (bf16[1024,256]{1,0:T(8,128)(2,1)S(1)}, bf16[1024,256]{1,0:T(8,128)(2,1)S(1)}, u32[]{:S(2)}, u32[]{:S(2)}) collective-permute-start(bf16[1024,256]{1,0:T(8,128)(2,1)S(1)} %pad_maximum_fusion), channel_id=1, source_target_pairs={{0,4},{1,5},{2,6},{3,7},{4,8},{5,9},{6,10},{7,11},{8,12},{9,13},{1... | collective-permute-start | bytes 1572872 | tf_op jit(solution)/shard_map/ppermute | solution.py:347
  69.0 14.1 %collective-permute-start.18 = (bf16[1024,256]{1,0:T(8,128)(2,1)S(1)}, bf16[1024,256]{1,0:T(8,128)(2,1)S(1)}, u32[]{:S(2)}, u32[]{:S(2)}) collective-permute-start(bf16[1024,256]{1,0:T(8,128)(2,1)S(1)} %constant_dynamic-update-slice_fusion.2), channel_id=1, source_target_pairs={{0,3},{1,0},{2,1},{3,2},{4,7},{5,4},{6,5},{7,6},{8,11},{9,8},{10,9... | collective-permute-start | bytes 1572872 | tf_op jit(solution)/shard_map/ppermute | solution.py:347
  70.7 15.7 %collective-permute-start.19 = (bf16[1024,256]{1,0:T(8,128)(2,1)S(1)}, bf16[1024,256]{1,0:T(8,128)(2,1)S(1)}, u32[]{:S(2)}, u32[]{:S(2)}) collective-permute-start(bf16[1024,256]{1,0:T(8,128)(2,1)S(1)} %pad_maximum_fusion.1), channel_id=1, source_target_pairs={{0,1},{1,2},{2,3},{3,0},{4,5},{5,6},{6,7},{7,4},{8,9},{9,10},{10,1... | collective-permute-start | bytes 1572872 | tf_op jit(solution)/shard_map/ppermute | solution.py:347
  75.7 15.5 %collective-permute-start.12 = (bf16[1024,256]{1,0:T(8,128)(2,1)S(1)}, bf16[1024,256]{1,0:T(8,128)(2,1)S(1)}, u32[]{:S(2)}, u32[]{:S(2)}) collective-permute-start(bf16[1024,256]{1,0:T(8,128)(2,1)S(1)} %collective-permute-done.8), channel_id=1, source_target_pairs={{0,4},{1,5},{2,6},{3,7},{4,8},{5,9},{6,10},{7,11},{8,12},{9,13},{1... | collective-permute-start | bytes 1572872 | tf_op jit(solution)/shard_map/ppermute | solution.py:347
  77.9 13.3 %collective-permute-start.13 = (bf16[1024,256]{1,0:T(8,128)(2,1)S(1)}, bf16[1024,256]{1,0:T(8,128)(2,1)S(1)}, u32[]{:S(2)}, u32[]{:S(2)}) collective-permute-start(bf16[1024,256]{1,0:T(8,128)(2,1)S(1)} %collective-permute-done.9), channel_id=1, source_target_pairs={{0,12},{1,13},{2,14},{3,15},{4,0},{5,1},{6,2},{7,3},{8,4},{9,5},{1... | collective-permute-start | bytes 1572872 | tf_op jit(solution)/shard_map/ppermute | solution.py:347
  83.2 10.4 %collective-permute-start.14 = (bf16[1024,256]{1,0:T(8,128)(2,1)S(1)}, bf16[1024,256]{1,0:T(8,128)(2,1)S(1)}, u32[]{:S(2)}, u32[]{:S(2)}) collective-permute-start(bf16[1024,256]{1,0:T(8,128)(2,1)S(1)} %collective-permute-done.10), channel_id=1, source_target_pairs={{0,1},{1,2},{2,3},{3,0},{4,5},{5,6},{6,7},{7,4},{8,9},{9,10},{10,1... | collective-permute-start | bytes 1572872 | tf_op jit(solution)/shard_map/ppermute | solution.py:347
  83.2 10.4 %collective-permute-start.15 = (bf16[1024,256]{1,0:T(8,128)(2,1)S(1)}, bf16[1024,256]{1,0:T(8,128)(2,1)S(1)}, u32[]{:S(2)}, u32[]{:S(2)}) collective-permute-start(bf16[1024,256]{1,0:T(8,128)(2,1)S(1)} %collective-permute-done.11), channel_id=1, source_target_pairs={{0,3},{1,0},{2,1},{3,2},{4,7},{5,4},{6,5},{7,6},{8,11},{9,8},{10,9... | collective-permute-start | bytes 1572872 | tf_op jit(solution)/shard_map/ppermute | solution.py:347
  98.3 9.1 %collective-permute-start.21 = (bf16[3,1024,256]{2,1,0:T(8,128)(2,1)S(1)}, bf16[3,1024,256]{2,1,0:T(8,128)(2,1)S(1)}, u32[]{:S(2)}, u32[]{:S(2)}) collective-permute-start(bf16[3,1024,256]{2,1,0:T(8,128)(2,1)S(1)} %bitcast.80), channel_id=1, source_target_pairs={{0,16},{16,0},{32,48},{48,32},{64,80},{80,64},{96,112},{112,96},{1... | collective-permute-start | bytes 4718600 | tf_op jit(solution)/shard_map/ppermute | solution.py:374
  98.4 4.1 %collective-permute-start.20 = (bf16[1024,256]{1,0:T(8,128)(2,1)S(1)}, bf16[1024,256]{1,0:T(8,128)(2,1)S(1)}, u32[]{:S(2)}, u32[]{:S(2)}) collective-permute-start(bf16[1024,256]{1,0:T(8,128)(2,1)S(1)} %bitcast.81), channel_id=1, source_target_pairs={{0,16},{16,0},{32,48},{48,32},{64,80},{80,64},{96,112},{112,96},{1... | collective-permute-start | bytes 1572872 | tf_op jit(solution)/shard_map/ppermute | solution.py:374
  102.7 8.4 %collective-permute-start.22 = (bf16[512,256]{1,0:T(8,128)(2,1)S(1)}, bf16[512,256]{1,0:T(8,128)(2,1)S(1)}, u32[]{:S(2)}, u32[]{:S(2)}) collective-permute-start(bf16[512,256]{1,0:T(8,128)(2,1)S(1)} %get-tuple-element.90), channel_id=1, source_target_pairs={{0,32},{16,48},{32,64},{48,80},{64,96},{80,112},{96,0},{112,16},{1... | collective-permute-start | bytes 786440 | tf_op jit(solution)/shard_map/ppermute | solution.py:374
  102.9 10.0 %collective-permute-start.24 = (bf16[512,256]{1,0:T(8,128)(2,1)S(1)}, bf16[512,256]{1,0:T(8,128)(2,1)S(1)}, u32[]{:S(2)}, u32[]{:S(2)}) collective-permute-start(bf16[512,256]{1,0:T(8,128)(2,1)S(1)} %get-tuple-element.91), channel_id=1, source_target_pairs={{0,96},{16,112},{32,0},{48,16},{64,32},{80,48},{96,64},{112,80},{1... | collective-permute-start | bytes 786440 | tf_op jit(solution)/shard_map/ppermute | solution.py:374
  107.3 6.3 %copy-start.5 = (s32[1024]{0:T(1024)S(1)}, s32[1024]{0:T(1024)}, u32[]{:S(2)}) copy-start(s32[1024]{0:T(1024)} %param.12) | copy-start | bytes 12292
  107.3 6.2 %copy-start.7 = (bf16[256]{0:T(256)(128)(2,1)S(1)}, bf16[256]{0:T(256)(128)(2,1)}, u32[]{:S(2)}) copy-start(bf16[256]{0:T(256)(128)(2,1)} %param.19) | copy-start | bytes 1540
  107.7 19.6 %copy-start.6 = (bf16[256,256]{1,0:T(8,128)(2,1)S(1)}, bf16[256,256]{1,0:T(8,128)(2,1)}, u32[]{:S(2)}) copy-start(bf16[256,256]{1,0:T(8,128)(2,1)} %param.18) | copy-start | bytes 393220
  111.3 13.2 %collective-permute-start.23 = (bf16[1024,256]{1,0:T(8,128)(2,1)S(1)}, bf16[1024,256]{1,0:T(8,128)(2,1)S(1)}, u32[]{:S(2)}, u32[]{:S(2)}) collective-permute-start(bf16[1024,256]{1,0:T(8,128)(2,1)S(1)} %pad_maximum_fusion.2), channel_id=1, source_target_pairs={{0,32},{16,48},{32,64},{48,80},{64,96},{80,112},{96,0},{112,16},{1... | collective-permute-start | bytes 1572872 | tf_op jit(solution)/shard_map/ppermute | solution.py:374
  113.0 14.4 %collective-permute-start.25 = (bf16[1024,256]{1,0:T(8,128)(2,1)S(1)}, bf16[1024,256]{1,0:T(8,128)(2,1)S(1)}, u32[]{:S(2)}, u32[]{:S(2)}) collective-permute-start(bf16[1024,256]{1,0:T(8,128)(2,1)S(1)} %pad_maximum_fusion.3), channel_id=1, source_target_pairs={{0,96},{16,112},{32,0},{48,16},{64,32},{80,48},{96,64},{112,80},{1... | collective-permute-start | bytes 1572872 | tf_op jit(solution)/shard_map/ppermute | solution.py:374
where the time goes:
time: 130 us; the launch traced here: 129 us
  starting transfers between devices  36.1 us (28%)
  waiting for transfers between devices  29.5 us (23%)
  Pallas kernels  29 us (22%)
  blocking collectives  28.4 us (22%)
  local copies, waits for them, and re-layouts  2.14 us (2%)
  matrix products  1.59 us (1%)
    ppermute x20, starting transfers between devices, send(): return lax.ppermute(v, 'col', col_perm(dz, dy))  31.3 us
    all_to_all x1, blocking collectives, per_device(): lax.all_to_all(outgoing.reshape(devices, SLOT_ROWS, width), ('row', 'col'...  28.4 us
    pallas_call x6, Pallas kernels, run_tiles(): pl.pallas_call(functools.partial(tiles_kernel, buckets, state is None, n,...  22.4 us
    ppermute x6, waiting for transfers between devices, over(): return lax.ppermute(v, 'row', row_perm(dx, flip))  20.5 us
    ppermute x20, waiting for transfers between devices, send(): return lax.ppermute(v, 'col', col_perm(dz, dy))  9 us
    ppermute x6, starting transfers between devices, over(): return lax.ppermute(v, 'row', row_perm(dx, flip))  4.84 us
    pallas_call x1, Pallas kernels, per_device(): pl.pallas_call(pack_kernel, out_shape=jax.ShapeDtypeStruct((devices * SLO...  2.74 us
  transfers between devices with their start and end apart: 26, of which 9 were waited for; matrix products, arithmetic and copies ran while one was open for 1% of the time, Pallas kernels for 15%

commit v1 on v0

--- a/solution.py
+++ b/solution.py
@@ -12,7 +12,7 @@
 PAIRS = 8
 BLOCK = 2 * PAIRS
 BUFS = 8
-LIST = 1152
+LIST = 1024
 LANES = 384
 MB = 1 << 20
 VMEM_TILES = 30 * MB
@@ -60,9 +60,9 @@
     out_ref[...] = data.astype(jnp.bfloat16)
 
 
-def unpack_kernel(in_ref, a_ref, b_ref):
+def unpack_kernel(in_ref, out_ref):
     ins = in_ref.shape[0]
-    rows = a_ref.shape[0] + b_ref.shape[0]
+    rows = out_ref.shape[0]
     data = in_ref[...]
     drop = onehot(iota((128, ins), 1) == iota((128, ins), 0) * SLOT_ROWS + POS_ROW)
     pos_rows = jnp.dot(drop, data, preferred_element_type=jnp.float32).astype(jnp.bfloat16)
@@ -77,13 +77,7 @@
     low = lanes(pos_rows[:, 128:])
     target = 4 * (high - 1) + 2 * low + (iota((1, ins), 1) & 1)
     pick = onehot(iota((rows, ins), 0) == target)
-    owned = jnp.dot(pick, data, preferred_element_type=jnp.float32).astype(jnp.bfloat16)
-    a_ref[...] = owned[: rows // 2]
-    b_ref[...] = owned[rows // 2 :]
-
-
-def ring_order(step):
-    return jnp.where(step == 0, 0, jnp.where(step == 3, 1, jnp.where(step == 1, 2, 3)))
+    out_ref[...] = jnp.dot(pick, data, preferred_element_type=jnp.float32).astype(jnp.bfloat16)
 
 
 def plan_kernel(where_ref, count_ref, rows_ref, cols_ref, code_ref, start_ref):
@@ -93,14 +87,19 @@
     row = rows_ref[...]
     col = cols_ref[...]
     source = col >> 3
-    order_z = ring_order(((source >> 2) - z) & 3)
-    order_y = ring_order(((source & 3) - y) & 3)
-    half = (col >> 2) & 1
-    outer = jnp.where(half == 0, order_z, order_y)
-    inner = jnp.where(half == 0, order_y, order_z)
-    stage = jnp.where((outer == 1) == (inner < 2), 1, 2)
-    stage = jnp.where(outer == 3, 3, jnp.where(outer == 0, 0, stage))
-    tile = half * 16 + inner * 4 + (col & 3)
+    dz = ((source >> 2) - z) & 3
+    dy = ((source & 3) - y) & 3
+    steps = jnp.where(dz == 3, 1, dz) + jnp.where(dy == 3, 1, dy)
+    stage = jnp.maximum(steps - 1, 0)
+    part, rest = (col & 7) >> 2, col & 3
+    side_z, side_y = jnp.where(dz == 3, 0, 4), jnp.where(dy == 3, 0, 4)
+    tile_0 = jnp.where(dz == 0, jnp.where(dy == 0, 0, side_y * 2 + 8), side_z * 2 + 24) + (col & 7)
+    corner = jnp.where(part == 0, side_y * 3 + side_z, side_z * 3 + side_y + 24)
+    tile_1 = jnp.where(dz == 0, part * 12 + 8, jnp.where(dy == 0, part * 12 + 32, corner)) + rest
+    on_y = jnp.where(part == 0, 4 - side_z, side_z + 8)
+    on_z = jnp.where(part == 1, 20 - side_y, side_y + 24)
+    tile_2 = jnp.where(dy == 2, on_y, on_z) + rest
+    tile = jnp.where(stage == 0, tile_0, jnp.where(stage == 1, tile_1, jnp.where(stage == 2, tile_2, col & 7)))
     owner = row >> 3
     dx = ((owner >> 1) - x) & 3
     order_x = jnp.where(dx == 2, 0, jnp.where(dx == 1, 1, jnp.where(dx == 3, 2, 3)))
@@ -125,18 +124,14 @@
     pairs = jnp.broadcast_to((cnt + 1) >> 1, (16, LANES)).astype(jnp.float32).astype(jnp.bfloat16)
     a, b = iota((LANES, LANES), 0), iota((LANES, LANES), 1)
 
-    def region(k):
-        late = jnp.where(k < 232, 4, jnp.where(k < 256, 5, 6))
-        return jnp.where(k < 192, k >> 6, jnp.where(k < 208, 3, late))
-
-    same_region = region(a) == region(b)
-    opens = (a == 0) | (a == 64) | (a == 128) | (a == 192) | (a == 208) | (a == 232)
-    inside = jnp.dot(pairs, onehot(same_region & (a < b)), preferred_element_type=jnp.float32)
-    total = jnp.dot(pairs, onehot(same_region), preferred_element_type=jnp.float32)
+    same_stage = (a >> 6) == (b >> 6)
+    opens = ((a & 63) == 0) & ((a >> 6) < (b >> 6))
+    inside = jnp.dot(pairs, onehot(same_stage & (a < b)), preferred_element_type=jnp.float32)
+    total = jnp.dot(pairs, onehot(same_stage), preferred_element_type=jnp.float32)
     blocks = ((total.astype(jnp.int32) + (PAIRS - 1)) >> 3).astype(jnp.float32)
     blocks = blocks.astype(jnp.bfloat16)
     ahead = jnp.dot(
-        blocks, onehot(opens & (region(a) < region(b))), preferred_element_type=jnp.float32
+        blocks, onehot(opens), preferred_element_type=jnp.float32
     )
     begin = (ahead * BLOCK + inside * 2.0)[:1]
     base = jnp.sum(jnp.where(member, begin, 0.0), axis=1, keepdims=True)
@@ -148,43 +143,30 @@
     start_ref[...] = ahead[:1].astype(jnp.int32)
 
 
-def tiles_kernel(buckets, opening, n_pieces, make_panel, outs, *refs):
+def tiles_kernel(stage, n_pieces, outs, *refs):
+    opening = stage == 0
     code_ref, start_ref, weights = refs[:3]
-    k = 3
-    pieces = refs[k : k + n_pieces]
-    k += n_pieces
-    if not n_pieces:
-        panel = refs[k]
-        k += 1
+    pieces = refs[3 : 3 + n_pieces]
+    k = 3 + n_pieces
     if not opening:
         k += 2
     acc, wbuf = refs[k : k + 2]
-    k += 2
-    if make_panel:
-        panel = refs[k]
-        k += 1
-    out_refs = refs[k : k + len(outs)]
-    k += len(outs)
-    if n_pieces and not make_panel:
-        panel = refs[k]
-        k += 1
-    wsem = refs[k]
-    first = start_ref[buckets[0]]
-    last = start_ref[buckets[1]]
+    out_refs = refs[k + 2 : k + 2 + len(outs)]
+    panel, wsem, psem = refs[k + 2 + len(outs) :]
+    first = start_ref[64 * stage]
+    last = start_ref[64 * stage + 64]
     total = start_ref[256]
     ahead = BUFS - 1
 
     copies = []
-    if n_pieces:
-        psem = refs[k + 1]
-        offset = 1
-        for i, piece in enumerate(pieces):
-            n = piece.shape[0]
-            copies.append(pltpu.make_async_copy(piece, panel.at[pl.ds(offset, n)], psem.at[i]))
-            offset += n
-        for c in copies:
-            c.start()
-        panel[0] = jnp.zeros(panel.shape[1:], panel.dtype)
+    offset = 1
+    for i, piece in enumerate(pieces):
+        n = piece.shape[0]
+        copies.append(pltpu.make_async_copy(piece, panel.at[pl.ds(offset, n)], psem.at[i]))
+        offset += n
+    for c in copies:
+        c.start()
+    panel[0] = jnp.zeros(panel.shape[1:], panel.dtype)
 
     def fetch(block):
         slot = lax.rem(block, BUFS)
@@ -233,7 +215,7 @@
         pl.when((last + i < total) & (last + i >= fetched))(functools.partial(arrive, last + i))
 
 
-def run_tiles(buckets, code, start, weights, pieces=(), panel=None, state=None, make_panel=False, outs=()):
+def run_tiles(stage, code, start, weights, pieces, state=(), outs=()):
     any_spec = pl.BlockSpec(memory_space=pl.ANY)
     vmem = pl.BlockSpec(memory_space=pltpu.VMEM)
     smem = pl.BlockSpec(memory_space=pltpu.SMEM)
@@ -241,42 +223,32 @@
     pieces = [p.reshape(-1, t, p.shape[-1]) for p in pieces]
     n = len(pieces)
     tiles = sum(p.shape[0] for p in pieces) + 1
-    f = (pieces[0] if n else panel).shape[2]
+    f = pieces[0].shape[2]
     args = [code, start, weights, *pieces]
-    in_specs = [smem, smem, any_spec] + [any_spec] * n
-    if panel is not None:
-        args.append(panel)
-        in_specs.append(vmem)
-    aliases = {}
-    if state is not None:
-        aliases = {len(args): 0, len(args) + 1: 1}
-        args += list(state)
-        in_specs += [vmem, vmem]
+    in_specs = [smem, smem] + [any_spec] * (n + 1)
+    aliases = {len(args) + i: i for i in range(len(state))}
     out_shape = [
         pltpu.VMEM((64, t, f), jnp.float32),
         pltpu.VMEM((BUFS, BLOCK, t, t), jnp.bfloat16),
-    ]
-    if make_panel:
-        out_shape.append(pltpu.VMEM((tiles, t, f), jnp.bfloat16))
-    out_shape += [pltpu.VMEM((k, t, f), jnp.bfloat16) for _, k in outs]
-    scratch = [pltpu.VMEM((tiles, t, f), jnp.bfloat16)] if n and not make_panel else []
-    scratch.append(pltpu.SemaphoreType.DMA((BUFS,)))
-    if n:
-        scratch.append(pltpu.SemaphoreType.DMA((n,)))
-    share = 352 * (buckets[1] - buckets[0]) // 256
+    ] + [pltpu.VMEM((k, t, f), jnp.bfloat16) for _, k in outs]
+    share = 352 * (tiles - 1) // 128
     return pl.pallas_call(
-        functools.partial(tiles_kernel, buckets, state is None, n, make_panel, outs),
+        functools.partial(tiles_kernel, stage, n, outs),
         out_shape=out_shape,
-        in_specs=in_specs,
+        in_specs=in_specs + [vmem] * len(state),
         out_specs=[vmem] * len(out_shape),
-        scratch_shapes=scratch,
+        scratch_shapes=[
+            pltpu.VMEM((tiles, t, f), jnp.bfloat16),
+            pltpu.SemaphoreType.DMA((BUFS,)),
+            pltpu.SemaphoreType.DMA((n,)),
+        ],
         input_output_aliases=aliases,
         compiler_params=pltpu.CompilerParams(vmem_limit_bytes=VMEM_TILES),
         cost_estimate=pl.CostEstimate(
             flops=share * 4 * t * t * f, bytes_accessed=share * 4 * t * t, transcendentals=0
         ),
-        name=f"tiles_{buckets[0]}",
-    )(*args)
+        name=f"tiles_{stage}",
+    )(*args, *state)
 
 
 def col_perm(dz, dy):
@@ -319,11 +291,11 @@
     )
     half = rows // 2
     quarter = half // 2
-    a0, b0 = pl.pallas_call(
+    owned = pl.pallas_call(
         unpack_kernel,
-        out_shape=(jax.ShapeDtypeStruct((half, width), jnp.bfloat16),) * 2,
+        out_shape=jax.ShapeDtypeStruct((rows, width), jnp.bfloat16),
         in_specs=[vmem],
-        out_specs=(vmem, vmem),
+        out_specs=vmem,
         compiler_params=big,
         name="unpack",
     )(incoming.reshape(devices * SLOT_ROWS, width))
@@ -346,43 +318,54 @@
     def send(v, dz, dy):
         return lax.ppermute(v, "col", col_perm(dz, dy))
 
+    def spread(to_yp, to_ym, to_zp, to_zm):
+        return [send(to_yp, 0, 1), send(to_ym, 0, -1), send(to_zp, 1, 0), send(to_zm, -1, 0)]
+
     def cat(*parts):
         return jnp.concatenate(parts, axis=0)
 
-    ap, am = send(a0, 0, 1), send(a0, 0, -1)
-    bp, bm = send(b0, 1, 0), send(b0, -1, 0)
-    a_hi = cat(am, send(ap[:quarter], 0, 1), send(am[quarter:], 0, -1))
-    b_hi = cat(bm, send(bp[:quarter], 1, 0), send(bm[quarter:], -1, 0))
-    a_hi, b_hi, ap, bp, code, start = lax.optimization_barrier((a_hi, b_hi, ap, bp, code, start))
-    a_lo, b_lo = cat(a0, ap), cat(b0, bp)
+    def one(v):
+        return v[:half]
+
+    def two(v):
+        return v[half:]
+
+    near = spread(owned, owned, owned, owned)
+    *near, code, start = lax.optimization_barrier((*near, code, start))
+    ym, yp, zm, zp = near
     lists = (code, start, weights)
-    a_lo_p, a_hi_m = send(a_lo, 1, 0), send(a_hi, -1, 0)
-    b_lo_p, b_hi_m = send(b_lo, 0, 1), send(b_hi, 0, -1)
-    state = run_tiles((0, 64), *lists, [a_lo, a_hi, b_lo, b_hi])
-    a_lo, a_hi, b_lo, b_hi, *state = lax.optimization_barrier((a_lo, a_hi, b_lo, b_hi, *state))
-    a_hi_p, a_lo_m = send(a_hi, 1, 0), send(a_lo, -1, 0)
-    b_hi_p, b_lo_m = send(b_hi, 0, 1), send(b_lo, 0, -1)
-    state = run_tiles((64, 128), *lists, [a_lo_p, a_hi_m, b_lo_p, b_hi_m], state=state)
-    a_lo_p, a_hi_m, b_lo_p, b_hi_m, *state = lax.optimization_barrier(
-        (a_lo_p, a_hi_m, b_lo_p, b_hi_m, *state)
-    )
-    far = [send(a_lo_p, 1, 0), send(a_hi_m, -1, 0), send(b_lo_p, 0, 1), send(b_hi_m, 0, -1)]
-    state = run_tiles((128, 192), *lists, [a_lo_m, a_hi_p, b_lo_m, b_hi_p], state=state)
+    diagonal = spread(
+        cat(one(zm), one(zp), one(ym)),
+        cat(one(zm), one(zp), two(yp)),
+        cat(two(ym), two(yp), one(zm)),
+        cat(two(ym), two(yp), two(zp)),
+    )
+    state = run_tiles(0, *lists, [owned, *near])
+    (ym, yp, zm, zp), state = lax.optimization_barrier((diagonal, state))
+    third = spread(
+        cat(ym[half:rows], one(ym)),
+        cat(zm[half:rows], zp[half:rows]),
+        cat(zm[half:rows], one(zm)),
+        cat(ym[half:rows], yp[half:rows]),
+    )
+    state = run_tiles(1, *lists, [ym, yp, zm, zp], state)
+    (ym, yp, zm, zp), state = lax.optimization_barrier((third, state))
+    last = spread(zp[:quarter], zp[-quarter:], yp[:quarter], yp[-quarter:])
+    state = run_tiles(2, *lists, [ym, yp, zm, zp], state)
+    *_, other_far, mine_far, other_rest, mine_rest = run_tiles(
+        3, *lists, last, state, ((0, 8), (8, 8), (16, 24), (40, 24))
+    )
+
     f32 = jnp.float32
 
     def over(v, dx, flip=0):
         return lax.ppermute(v, "row", row_perm(dx, flip))
 
-    *state, panel, other_far, mine_far = run_tiles(
-        (192, 208), *lists, far, state=state, make_panel=True, outs=((0, 8), (8, 8))
-    )
     got_far = over(other_far.reshape(rows, width), 0, 1)
-    *state, other_rest = run_tiles((208, 232), *lists, panel=panel, state=state, outs=((16, 24),))
     across = (mine_far.reshape(rows, width).astype(f32) + got_far.astype(f32)).astype(jnp.bfloat16)
-    across, *state = lax.optimization_barrier((across, *state))
+    across, other_rest = lax.optimization_barrier((across, other_rest))
     from_minus, from_plus = over(across[:half], 1), over(across[half:], -1)
     got_rest = over(other_rest.reshape(3, rows, width), 0, 1)
-    *state, mine_rest = run_tiles((232, 256), *lists, panel=panel, state=state, outs=((40, 24),))
     mine_rest = mine_rest.reshape(3, rows, width)
     both = [mine_rest[i].astype(f32) + got_rest[i].astype(f32) for i in range(3)]
     to_plus = cat(both[0][:half] + from_minus.astype(f32), both[0][half:]).astype(jnp.bfloat16)
@@ -390,7 +373,7 @@
     summed = both[2] + over(to_plus, 1).astype(f32) + over(to_minus, -1).astype(f32)
 
     neighbor_mean = (summed / degree.astype(f32)[:, None]).astype(jnp.bfloat16)
-    total = jnp.dot(cat(a0, b0), w_self, preferred_element_type=f32)
+    total = jnp.dot(owned, w_self, preferred_element_type=f32)
     total = total + jnp.dot(neighbor_mean, w_neigh, preferred_element_type=f32)
     total = total + bias.astype(f32)[None, :]
     return jnp.maximum(total, f32(0.0)).astype(jnp.bfloat16)

time: 130 us -> 133 us (1.023)
  waiting for transfers between devices: 29.5 us -> 46.3 us
  Pallas kernels: 29 us -> 22.2 us
  starting transfers between devices: 36.1 us -> 30.1 us
    ppermute x20 -> x16, waiting for transfers between devices: 9 us -> 24.2 us  [send(): return lax.ppermute(v, 'col', col_perm(dz, dy))]
    pallas_call x7 -> x5, Pallas kernels: 24.4 us -> 17.6 us  [the longest x4 15.5 us: run_tiles(): pl.pallas_call(functools.partial(tiles_kernel, stage, n, outs), out_shape...]
    ppermute x20 -> x16, starting transfers between devices: 31.3 us -> 25.3 us  [send(): return lax.ppermute(v, 'col', col_perm(dz, dy))]
    ppermute x6, waiting for transfers between devices: 20.5 us -> 22 us  [over(): return lax.ppermute(v, 'row', row_perm(dx, flip))]
  transfers between devices with their start and end apart: 26 -> 22, of which waited for: 9 -> 12; matrix products, arithmetic and copies ran while one was open for 1% -> 1% of each run, Pallas kernels for 15% -> 11%
where the time goes in v1:
time: 133 us
  waiting for transfers between devices  46.3 us (35%)
  starting transfers between devices  30.1 us (23%)
  blocking collectives  28.4 us (21%)
  Pallas kernels  22.2 us (17%)
  local copies, waits for them, and re-layouts  2.28 us (2%)
  matrix products  1.58 us (1%)
    all_to_all x1, blocking collectives, per_device(): lax.all_to_all(outgoing.reshape(devices, SLOT_ROWS, width), ('row', 'col'...  28.4 us
    ppermute x16, starting transfers between devices, send(): return lax.ppermute(v, 'col', col_perm(dz, dy))  25.3 us
    ppermute x16, waiting for transfers between devices, send(): return lax.ppermute(v, 'col', col_perm(dz, dy))  24.2 us
    ppermute x6, waiting for transfers between devices, over(): return lax.ppermute(v, 'row', row_perm(dx, flip))  22 us
    pallas_call x4, Pallas kernels, run_tiles(): pl.pallas_call(functools.partial(tiles_kernel, stage, n, outs), out_shape...  15.5 us
    ppermute x6, starting transfers between devices, over(): return lax.ppermute(v, 'row', row_perm(dx, flip))  4.8 us
    pallas_call x1, Pallas kernels, per_device(): pl.pallas_call(pack_kernel, out_shape=jax.ShapeDtypeStruct((devices * SLO...  2.74 us
  transfers between devices with their start and end apart: 22, of which 12 were waited for; matrix products, arithmetic and copies ran while one was open for 1% of the time, Pallas kernels for 11%

profile of v1, /device:TPU:6, one launch (start us, length us, event | category | flops | bytes accessed | tf_op | source)
XLA Modules:
  0.0 132.9 jit_solution(3851563743780001311)
XLA Ops:
  0.0 1.1 copy-done.1
  1.1 0.7 copy-done.4
  1.8 2.7 %pack.1 = bf16[2048,256]{1,0:T(8,128)(2,1)S(1)} custom-call(s32[1,512]{1,0:T(1,128)S(1)} %bitcast.87, bf16[1024,256]{1,0:T(8,128)(2,1)S(1)} %copy-done.1), custom_call_target="tpu_custom_call" | custom-call | tf_op jit(solution)/shard_map/pack/pallas_call | solution.py:277
  4.5 28.4 %all_to_all.5 = bf16[128,16,256]{2,1,0:T(8,128)(2,1)S(1)} all-to-all(bf16[128,16,256]{2,1,0:T(8,128)(2,1)S(1)} %bitcast.64), channel_id=1, replica_groups=mesh['row'=8,'col'=16] {'row','col'}, dimensions={0} | all-to-all | bytes 2097152 | tf_op jit(solution)/shard_map/all_to_all | solution.py:285
  32.9 2.1 %unpack.1 = bf16[1024,256]{1,0:T(8,128)(2,1)S(1)} custom-call(bf16[2048,256]{1,0:T(8,128)(2,1)S(1)} %bitcast.63), custom_call_target="tpu_custom_call" | custom-call | tf_op jit(solution)/shard_map/unpack/pallas_call | solution.py:294
  35.0 0.7 collective-permute-start
  35.7 2.6 %collective-permute-start.1 = (bf16[1024,256]{1,0:T(8,128)(2,1)S(1)}, bf16[1024,256]{1,0:T(8,128)(2,1)S(1)}, u32[]{:S(2)}, u32[]{:S(2)}) collective-permute-start(bf16[1024,256]{1,0:T(8,128)(2,1)S(1)} %unpack.1), channel_id=1, source_target_pairs={{0,3},{1,0},{2,1},{3,2},{4,7},{5,4},{6,5},{7,6},{8,11},{9,8},{10,9... | collective-permute-start | bytes 1572872 | tf_op jit(solution)/shard_map/ppermute | solution.py:319
  38.3 0.8 collective-permute-start.2
  39.1 2.4 %collective-permute-start.3 = (bf16[1024,256]{1,0:T(8,128)(2,1)S(1)}, bf16[1024,256]{1,0:T(8,128)(2,1)S(1)}, u32[]{:S(2)}, u32[]{:S(2)}) collective-permute-start(bf16[1024,256]{1,0:T(8,128)(2,1)S(1)} %unpack.1), channel_id=1, source_target_pairs={{0,12},{1,13},{2,14},{3,15},{4,0},{5,1},{6,2},{7,3},{8,4},{9,5},{1... | collective-permute-start | bytes 1572872 | tf_op jit(solution)/shard_map/ppermute | solution.py:319
  42.2 0.1 pad_add_fusion.where_ref
  42.3 1.9 %plan.1 = (s32[1,1024]{1,0:T(1,128)S(1)}, s32[1,384]{1,0:T(1,128)S(1)}) custom-call(s32[4]{0:T(128)S(1)} %pad_add_fusion.where_ref, s32[1]{0:T(128)} %bitcast.61.count_ref, s32[1,704]{1,0:T(1,128)S(1)} %bitcast.85, s32[1,704]{1,0:T(1,128)S(1)} %bitcast.86), custom_call_target="tpu_custom_call" | custom-call | tf_op jit(solution)/shard_map/plan/pallas_call | solution.py:303
  44.2 5.7 %collective-permute-done = bf16[1024,256]{1,0:T(8,128)(2,1)S(1)} collective-permute-done((bf16[1024,256]{1,0:T(8,128)(2,1)S(1)}, bf16[1024,256]{1,0:T(8,128)(2,1)S(1)}, u32[]{:S(2)}, u32[]{:S(2)}) %collective-permute-start) | collective-permute-done | bytes 524320 | tf_op jit(solution)/shard_map/ppermute | solution.py:319
  49.9 2.7 %collective-permute-done.2 = bf16[1024,256]{1,0:T(8,128)(2,1)S(1)} collective-permute-done((bf16[1024,256]{1,0:T(8,128)(2,1)S(1)}, bf16[1024,256]{1,0:T(8,128)(2,1)S(1)}, u32[]{:S(2)}, u32[]{:S(2)}) %collective-permute-start.2) | collective-permute-done | bytes 524320 | tf_op jit(solution)/shard_map/ppermute | solution.py:319
  52.7 0.2 pad_maximum_fusion.5
  53.0 3.2 %collective-permute-start.5 = (bf16[1536,256]{1,0:T(8,128)(2,1)S(1)}, bf16[1536,256]{1,0:T(8,128)(2,1)S(1)}, u32[]{:S(2)}, u32[]{:S(2)}) collective-permute-start(bf16[1536,256]{1,0:T(8,128)(2,1)S(1)} %get-tuple-element.86), channel_id=1, source_target_pairs={{0,3},{1,0},{2,1},{3,2},{4,7},{5,4},{6,5},{7,6},{8,11},{9,8},{10,9... | collective-permute-start | bytes 2359304 | tf_op jit(solution)/shard_map/ppermute | solution.py:319
  56.2 3.2 %collective-permute-start.7 = (bf16[1536,256]{1,0:T(8,128)(2,1)S(1)}, bf16[1536,256]{1,0:T(8,128)(2,1)S(1)}, u32[]{:S(2)}, u32[]{:S(2)}) collective-permute-start(bf16[1536,256]{1,0:T(8,128)(2,1)S(1)} %get-tuple-element.84), channel_id=1, source_target_pairs={{0,12},{1,13},{2,14},{3,15},{4,0},{5,1},{6,2},{7,3},{8,4},{9,5},{1... | collective-permute-start | bytes 2359304 | tf_op jit(solution)/shard_map/ppermute | solution.py:319
  59.5 5.0 %tiles_0.1 = (f32[64,128,256]{2,1,0:T(8,128)S(1)}, bf16[8,16,128,128]{3,2,1,0:T(8,128)(2,1)S(1)}) custom-call(s32[1024]{0:T(1024)S(1)} %bitcast.81, s32[384]{0:T(512)S(1)} %reduce.refs_1_, bf16[704,128,128]{2,1,0:T(8,128)(2,1)} %bitcast.90, bf16[8,128,256]{2,1,0:T(8,128)(2,1)S(1)} %bitcast.62, bf16[8,128,256]{2,1,0:T(8,128)(2,1)S(1)} %bitcast.67, ...), custom_call_target="tpu_custom_call" | custom-call | flops 1845493760 | bytes 7208960 | tf_op jit(solution)/shard_map/tiles_0/pallas_call | solution.py:235
  64.5 7.5 %collective-permute-done.4 = bf16[1536,256]{1,0:T(8,128)(2,1)S(1)} collective-permute-done((bf16[1536,256]{1,0:T(8,128)(2,1)S(1)}, bf16[1536,256]{1,0:T(8,128)(2,1)S(1)}, u32[]{:S(2)}, u32[]{:S(2)}) %collective-permute-start.4) | collective-permute-done | bytes 786464 | tf_op jit(solution)/shard_map/ppermute | solution.py:319
  71.9 2.7 %collective-permute-done.6 = bf16[1536,256]{1,0:T(8,128)(2,1)S(1)} collective-permute-done((bf16[1536,256]{1,0:T(8,128)(2,1)S(1)}, bf16[1536,256]{1,0:T(8,128)(2,1)S(1)}, u32[]{:S(2)}, u32[]{:S(2)}) %collective-permute-start.6) | collective-permute-done | bytes 786464 | tf_op jit(solution)/shard_map/ppermute | solution.py:319
  74.8 0.9 collective-permute-start.10
  75.7 0.3 collective-permute-start.9
  76.1 2.6 %collective-permute-start.11 = (bf16[1024,256]{1,0:T(8,128)(2,1)S(1)}, bf16[1024,256]{1,0:T(8,128)(2,1)S(1)}, u32[]{:S(2)}, u32[]{:S(2)}) collective-permute-start(bf16[1024,256]{1,0:T(8,128)(2,1)S(1)} %get-tuple-element.92), channel_id=1, source_target_pairs={{0,12},{1,13},{2,14},{3,15},{4,0},{5,1},{6,2},{7,3},{8,4},{9,5},{1... | collective-permute-start | bytes 1572872 | tf_op jit(solution)/shard_map/ppermute | solution.py:319
  78.7 1.7 %collective-permute-start.8 = (bf16[1024,256]{1,0:T(8,128)(2,1)S(1)}, bf16[1024,256]{1,0:T(8,128)(2,1)S(1)}, u32[]{:S(2)}, u32[]{:S(2)}) collective-permute-start(bf16[1024,256]{1,0:T(8,128)(2,1)S(1)} %get-tuple-element.93), channel_id=1, source_target_pairs={{0,1},{1,2},{2,3},{3,0},{4,5},{5,6},{6,7},{7,4},{8,9},{9,10},{10,1... | collective-permute-start | bytes 1572872 | tf_op jit(solution)/shard_map/ppermute | solution.py:319
  80.5 4.8 %tiles_1.1 = (f32[64,128,256]{2,1,0:T(8,128)S(1)}, bf16[8,16,128,128]{3,2,1,0:T(8,128)(2,1)S(1)}) custom-call(s32[1024]{0:T(1024)S(1)} %bitcast.82, s32[384]{0:T(512)S(1)} %reduce.refs_1_, bf16[704,128,128]{2,1,0:T(8,128)(2,1)} %bitcast.91, bf16[12,128,256]{2,1,0:T(8,128)(2,1)S(1)} %bitcast.65, ...), custom_call_target="tpu_custom_call", output_to_operand_aliasing={{0}: (7, {}), {1}: (8, {})} | custom-call | flops 2214592512 | bytes 8650752 | tf_op jit(solution)/shard_map/tiles_1/pallas_call | solution.py:235
  85.3 1.4 %collective-permute-done.10 = bf16[1024,256]{1,0:T(8,128)(2,1)S(1)} collective-permute-done((bf16[1024,256]{1,0:T(8,128)(2,1)S(1)}, bf16[1024,256]{1,0:T(8,128)(2,1)S(1)}, u32[]{:S(2)}, u32[]{:S(2)}) %collective-permute-start.10) | collective-permute-done | bytes 524320 | tf_op jit(solution)/shard_map/ppermute | solution.py:319
  86.7 4.1 %collective-permute-done.8 = bf16[1024,256]{1,0:T(8,128)(2,1)S(1)} collective-permute-done((bf16[1024,256]{1,0:T(8,128)(2,1)S(1)}, bf16[1024,256]{1,0:T(8,128)(2,1)S(1)}, u32[]{:S(2)}, u32[]{:S(2)}) %collective-permute-start.8) | collective-permute-done | bytes 524320 | tf_op jit(solution)/shard_map/ppermute | solution.py:319
  90.8 1.0 collective-permute-start.12
  91.8 2.3 %collective-permute-start.13 = (bf16[256,256]{1,0:T(8,128)(2,1)S(1)}, bf16[256,256]{1,0:T(8,128)(2,1)S(1)}, u32[]{:S(2)}, u32[]{:S(2)}) collective-permute-start(bf16[256,256]{1,0:T(8,128)(2,1)S(1)} %get-tuple-element.82), channel_id=1, source_target_pairs={{0,3},{1,0},{2,1},{3,2},{4,7},{5,4},{6,5},{7,6},{8,11},{9,8},{10,9... | collective-permute-start | bytes 393224 | tf_op jit(solution)/shard_map/ppermute | solution.py:319
  94.1 0.1 collective-permute-start.14
  94.2 3.2 %collective-permute-start.15 = (bf16[256,256]{1,0:T(8,128)(2,1)S(1)}, bf16[256,256]{1,0:T(8,128)(2,1)S(1)}, u32[]{:S(2)}, u32[]{:S(2)}) collective-permute-start(bf16[256,256]{1,0:T(8,128)(2,1)S(1)} %get-tuple-element.80), channel_id=1, source_target_pairs={{0,12},{1,13},{2,14},{3,15},{4,0},{5,1},{6,2},{7,3},{8,4},{9,5},{1... | collective-permute-start | bytes 393224 | tf_op jit(solution)/shard_map/ppermute | solution.py:319
  97.4 2.7 %tiles_2.1 = (f32[64,128,256]{2,1,0:T(8,128)S(1)}, bf16[8,16,128,128]{3,2,1,0:T(8,128)(2,1)S(1)}) custom-call(s32[1024]{0:T(1024)S(1)} %bitcast.83, s32[384]{0:T(512)S(1)} %reduce.refs_1_, bf16[704,128,128]{2,1,0:T(8,128)(2,1)} %bitcast.92, bf16[8,128,256]{2,1,0:T(8,128)(2,1)S(1)} %bitcast.76, ...), custom_call_target="tpu_custom_call", output_to_operand_aliasing={{0}: (7, {}), {1}: (8, {})} | custom-call | flops 1476395008 | bytes 5767168 | tf_op jit(solution)/shard_map/tiles_2/pallas_call | solution.py:235
  100.1 0.3 collective-permute-done.14
  100.3 3.1 %tiles_3.1 = (f32[64,128,256]{2,1,0:T(8,128)S(1)}, bf16[8,16,128,128]{3,2,1,0:T(8,128)(2,1)S(1)}, bf16[8,128,256]{2,1,0:T(8,128)(2,1)S(1)}, bf16[8,128,256]{2,1,...) custom-call(s32[1024]{0:T(1024)S(1)} %bitcast.84, ...), custom_call_target="tpu_custom_call", output_to_operand_aliasing={{0}: (7, {}), {1}: (8, {})} | custom-call | flops 369098752 | bytes 1441792 | tf_op jit(solution)/shard_map/tiles_3/pallas_call | solution.py:235
  103.4 0.1 collective-permute-start.16
  103.5 1.9 %collective-permute-done.16 = bf16[1024,256]{1,0:T(8,128)(2,1)S(1)} collective-permute-done((bf16[1024,256]{1,0:T(8,128)(2,1)S(1)}, bf16[1024,256]{1,0:T(8,128)(2,1)S(1)}, u32[]{:S(2)}, u32[]{:S(2)}) %collective-permute-start.16) | collective-permute-done | bytes 524320 | tf_op jit(solution)/shard_map/ppermute | solution.py:362
  105.4 0.2 fusion.6
  105.6 0.2 collective-permute-start.17
  105.8 0.1 fusion.12
  106.0 1.1 collective-permute-start.18
  107.1 1.0 collective-permute-start.20
  108.1 1.0 collective-permute-done.17
  109.1 0.3 convert_add_fusion.1
  109.5 5.2 %collective-permute-done.18 = bf16[512,256]{1,0:T(8,128)(2,1)S(1)} collective-permute-done((bf16[512,256]{1,0:T(8,128)(2,1)S(1)}, bf16[512,256]{1,0:T(8,128)(2,1)S(1)}, u32[]{:S(2)}, u32[]{:S(2)}) %collective-permute-start.18) | collective-permute-done | bytes 262176 | tf_op jit(solution)/shard_map/ppermute | solution.py:362
  114.8 2.3 %collective-permute-start.19 = (bf16[1024,256]{1,0:T(8,128)(2,1)S(1)}, bf16[1024,256]{1,0:T(8,128)(2,1)S(1)}, u32[]{:S(2)}, u32[]{:S(2)}) collective-permute-start(bf16[1024,256]{1,0:T(8,128)(2,1)S(1)} %pad_maximum_fusion.10), channel_id=1, source_target_pairs={{0,32},{16,48},{32,64},{48,80},{64,96},{80,112},{96,0},{112,16},{1... | collective-permute-start | bytes 1572872 | tf_op jit(solution)/shard_map/ppermute | solution.py:362
  117.4 0.3 fusion.20
  117.7 10.5 %collective-permute-done.19 = bf16[1024,256]{1,0:T(8,128)(2,1)S(1)} collective-permute-done((bf16[1024,256]{1,0:T(8,128)(2,1)S(1)}, bf16[1024,256]{1,0:T(8,128)(2,1)S(1)}, u32[]{:S(2)}, u32[]{:S(2)}) %collective-permute-start.19) | collective-permute-done | bytes 524320 | tf_op jit(solution)/shard_map/ppermute | solution.py:362
  128.2 3.4 %collective-permute-done.21 = bf16[1024,256]{1,0:T(8,128)(2,1)S(1)} collective-permute-done((bf16[1024,256]{1,0:T(8,128)(2,1)S(1)}, bf16[1024,256]{1,0:T(8,128)(2,1)S(1)}, u32[]{:S(2)}, u32[]{:S(2)}) %collective-permute-start.21) | collective-permute-done | bytes 524320 | tf_op jit(solution)/shard_map/ppermute | solution.py:362
  131.7 1.3 fusion.2
  (48 shorter events, 0.9 us)
Async XLA Ops:
  0.0 117.4 %copy-start = (bf16[256,256]{1,0:T(8,128)(2,1)S(1)}, bf16[256,256]{1,0:T(8,128)(2,1)}, u32[]{:S(2)}) copy-start(bf16[256,256]{1,0:T(8,128)(2,1)} %param.17) | copy-start | bytes 393220
  0.0 1.1 copy-start.1
  1.1 0.7 copy-start.4
  4.5 37.8 %copy-start.2 = (s32[1,1,704]{2,1,0:T(1,128)S(1)}, s32[1,1,704]{2,1,0:T(1,128)}, u32[]{:S(2)}) copy-start(s32[1,1,704]{2,1,0:T(1,128)} %param.13) | copy-start | bytes 8452
  4.5 37.8 %copy-start.3 = (s32[1,1,704]{2,1,0:T(1,128)S(1)}, s32[1,1,704]{2,1,0:T(1,128)}, u32[]{:S(2)}) copy-start(s32[1,1,704]{2,1,0:T(1,128)} %param.14) | copy-start | bytes 8452
  35.0 14.9 %collective-permute-start = (bf16[1024,256]{1,0:T(8,128)(2,1)S(1)}, bf16[1024,256]{1,0:T(8,128)(2,1)S(1)}, u32[]{:S(2)}, u32[]{:S(2)}) collective-permute-start(bf16[1024,256]{1,0:T(8,128)(2,1)S(1)} %unpack.1), channel_id=1, source_target_pairs={{0,1},{1,2},{2,3},{3,0},{4,5},{5,6},{6,7},{7,4},{8,9},{9,10},{10,1... | collective-permute-start | bytes 1572872 | tf_op jit(solution)/shard_map/ppermute | solution.py:319
  35.7 14.2 %collective-permute-start.1 = (bf16[1024,256]{1,0:T(8,128)(2,1)S(1)}, bf16[1024,256]{1,0:T(8,128)(2,1)S(1)}, u32[]{:S(2)}, u32[]{:S(2)}) collective-permute-start(bf16[1024,256]{1,0:T(8,128)(2,1)S(1)} %unpack.1), channel_id=1, source_target_pairs={{0,3},{1,0},{2,1},{3,2},{4,7},{5,4},{6,5},{7,6},{8,11},{9,8},{10,9... | collective-permute-start | bytes 1572872 | tf_op jit(solution)/shard_map/ppermute | solution.py:319
  38.3 14.3 %collective-permute-start.2 = (bf16[1024,256]{1,0:T(8,128)(2,1)S(1)}, bf16[1024,256]{1,0:T(8,128)(2,1)S(1)}, u32[]{:S(2)}, u32[]{:S(2)}) collective-permute-start(bf16[1024,256]{1,0:T(8,128)(2,1)S(1)} %unpack.1), channel_id=1, source_target_pairs={{0,4},{1,5},{2,6},{3,7},{4,8},{5,9},{6,10},{7,11},{8,12},{9,13},{1... | collective-permute-start | bytes 1572872 | tf_op jit(solution)/shard_map/ppermute | solution.py:319
  39.1 13.4 %collective-permute-start.3 = (bf16[1024,256]{1,0:T(8,128)(2,1)S(1)}, bf16[1024,256]{1,0:T(8,128)(2,1)S(1)}, u32[]{:S(2)}, u32[]{:S(2)}) collective-permute-start(bf16[1024,256]{1,0:T(8,128)(2,1)S(1)} %unpack.1), channel_id=1, source_target_pairs={{0,12},{1,13},{2,14},{3,15},{4,0},{5,1},{6,2},{7,3},{8,4},{9,5},{1... | collective-permute-start | bytes 1572872 | tf_op jit(solution)/shard_map/ppermute | solution.py:319
  52.9 19.0 %collective-permute-start.4 = (bf16[1536,256]{1,0:T(8,128)(2,1)S(1)}, bf16[1536,256]{1,0:T(8,128)(2,1)S(1)}, u32[]{:S(2)}, u32[]{:S(2)}) collective-permute-start(bf16[1536,256]{1,0:T(8,128)(2,1)S(1)} %get-tuple-element.87), channel_id=1, source_target_pairs={{0,1},{1,2},{2,3},{3,0},{4,5},{5,6},{6,7},{7,4},{8,9},{9,10},{10,1... | collective-permute-start | bytes 2359304 | tf_op jit(solution)/shard_map/ppermute | solution.py:319
  53.0 18.9 %collective-permute-start.5 = (bf16[1536,256]{1,0:T(8,128)(2,1)S(1)}, bf16[1536,256]{1,0:T(8,128)(2,1)S(1)}, u32[]{:S(2)}, u32[]{:S(2)}) collective-permute-start(bf16[1536,256]{1,0:T(8,128)(2,1)S(1)} %get-tuple-element.86), channel_id=1, source_target_pairs={{0,3},{1,0},{2,1},{3,2},{4,7},{5,4},{6,5},{7,6},{8,11},{9,8},{10,9... | collective-permute-start | bytes 2359304 | tf_op jit(solution)/shard_map/ppermute | solution.py:319
  56.2 18.4 %collective-permute-start.6 = (bf16[1536,256]{1,0:T(8,128)(2,1)S(1)}, bf16[1536,256]{1,0:T(8,128)(2,1)S(1)}, u32[]{:S(2)}, u32[]{:S(2)}) collective-permute-start(bf16[1536,256]{1,0:T(8,128)(2,1)S(1)} %get-tuple-element.85), channel_id=1, source_target_pairs={{0,4},{1,5},{2,6},{3,7},{4,8},{5,9},{6,10},{7,11},{8,12},{9,13},{1... | collective-permute-start | bytes 2359304 | tf_op jit(solution)/shard_map/ppermute | solution.py:319
  56.2 18.4 %collective-permute-start.7 = (bf16[1536,256]{1,0:T(8,128)(2,1)S(1)}, bf16[1536,256]{1,0:T(8,128)(2,1)S(1)}, u32[]{:S(2)}, u32[]{:S(2)}) collective-permute-start(bf16[1536,256]{1,0:T(8,128)(2,1)S(1)} %get-tuple-element.84), channel_id=1, source_target_pairs={{0,12},{1,13},{2,14},{3,15},{4,0},{5,1},{6,2},{7,3},{8,4},{9,5},{1... | collective-permute-start | bytes 2359304 | tf_op jit(solution)/shard_map/ppermute | solution.py:319
  74.8 11.9 %collective-permute-start.10 = (bf16[1024,256]{1,0:T(8,128)(2,1)S(1)}, bf16[1024,256]{1,0:T(8,128)(2,1)S(1)}, u32[]{:S(2)}, u32[]{:S(2)}) collective-permute-start(bf16[1024,256]{1,0:T(8,128)(2,1)S(1)} %get-tuple-element.94), channel_id=1, source_target_pairs={{0,4},{1,5},{2,6},{3,7},{4,8},{5,9},{6,10},{7,11},{8,12},{9,13},{1... | collective-permute-start | bytes 1572872 | tf_op jit(solution)/shard_map/ppermute | solution.py:319
  75.7 11.0 %collective-permute-start.9 = (bf16[1024,256]{1,0:T(8,128)(2,1)S(1)}, bf16[1024,256]{1,0:T(8,128)(2,1)S(1)}, u32[]{:S(2)}, u32[]{:S(2)}) collective-permute-start(bf16[1024,256]{1,0:T(8,128)(2,1)S(1)} %get-tuple-element.95), channel_id=1, source_target_pairs={{0,3},{1,0},{2,1},{3,2},{4,7},{5,4},{6,5},{7,6},{8,11},{9,8},{10,9... | collective-permute-start | bytes 1572872 | tf_op jit(solution)/shard_map/ppermute | solution.py:319
  76.1 10.6 %collective-permute-start.11 = (bf16[1024,256]{1,0:T(8,128)(2,1)S(1)}, bf16[1024,256]{1,0:T(8,128)(2,1)S(1)}, u32[]{:S(2)}, u32[]{:S(2)}) collective-permute-start(bf16[1024,256]{1,0:T(8,128)(2,1)S(1)} %get-tuple-element.92), channel_id=1, source_target_pairs={{0,12},{1,13},{2,14},{3,15},{4,0},{5,1},{6,2},{7,3},{8,4},{9,5},{1... | collective-permute-start | bytes 1572872 | tf_op jit(solution)/shard_map/ppermute | solution.py:319
  78.7 12.0 %collective-permute-start.8 = (bf16[1024,256]{1,0:T(8,128)(2,1)S(1)}, bf16[1024,256]{1,0:T(8,128)(2,1)S(1)}, u32[]{:S(2)}, u32[]{:S(2)}) collective-permute-start(bf16[1024,256]{1,0:T(8,128)(2,1)S(1)} %get-tuple-element.93), channel_id=1, source_target_pairs={{0,1},{1,2},{2,3},{3,0},{4,5},{5,6},{6,7},{7,4},{8,9},{9,10},{10,1... | collective-permute-start | bytes 1572872 | tf_op jit(solution)/shard_map/ppermute | solution.py:319
  90.8 9.3 %collective-permute-start.12 = (bf16[256,256]{1,0:T(8,128)(2,1)S(1)}, bf16[256,256]{1,0:T(8,128)(2,1)S(1)}, u32[]{:S(2)}, u32[]{:S(2)}) collective-permute-start(bf16[256,256]{1,0:T(8,128)(2,1)S(1)} %get-tuple-element.83), channel_id=1, source_target_pairs={{0,1},{1,2},{2,3},{3,0},{4,5},{5,6},{6,7},{7,4},{8,9},{9,10},{10,1... | collective-permute-start | bytes 393224 | tf_op jit(solution)/shard_map/ppermute | solution.py:319
  91.8 8.3 %collective-permute-start.13 = (bf16[256,256]{1,0:T(8,128)(2,1)S(1)}, bf16[256,256]{1,0:T(8,128)(2,1)S(1)}, u32[]{:S(2)}, u32[]{:S(2)}) collective-permute-start(bf16[256,256]{1,0:T(8,128)(2,1)S(1)} %get-tuple-element.82), channel_id=1, source_target_pairs={{0,3},{1,0},{2,1},{3,2},{4,7},{5,4},{6,5},{7,6},{8,11},{9,8},{10,9... | collective-permute-start | bytes 393224 | tf_op jit(solution)/shard_map/ppermute | solution.py:319
  94.1 6.2 %collective-permute-start.14 = (bf16[256,256]{1,0:T(8,128)(2,1)S(1)}, bf16[256,256]{1,0:T(8,128)(2,1)S(1)}, u32[]{:S(2)}, u32[]{:S(2)}) collective-permute-start(bf16[256,256]{1,0:T(8,128)(2,1)S(1)} %get-tuple-element.81), channel_id=1, source_target_pairs={{0,4},{1,5},{2,6},{3,7},{4,8},{5,9},{6,10},{7,11},{8,12},{9,13},{1... | collective-permute-start | bytes 393224 | tf_op jit(solution)/shard_map/ppermute | solution.py:319
  94.2 6.2 %collective-permute-start.15 = (bf16[256,256]{1,0:T(8,128)(2,1)S(1)}, bf16[256,256]{1,0:T(8,128)(2,1)S(1)}, u32[]{:S(2)}, u32[]{:S(2)}) collective-permute-start(bf16[256,256]{1,0:T(8,128)(2,1)S(1)} %get-tuple-element.80), channel_id=1, source_target_pairs={{0,12},{1,13},{2,14},{3,15},{4,0},{5,1},{6,2},{7,3},{8,4},{9,5},{1... | collective-permute-start | bytes 393224 | tf_op jit(solution)/shard_map/ppermute | solution.py:319
  103.4 2.0 %collective-permute-start.16 = (bf16[1024,256]{1,0:T(8,128)(2,1)S(1)}, bf16[1024,256]{1,0:T(8,128)(2,1)S(1)}, u32[]{:S(2)}, u32[]{:S(2)}) collective-permute-start(bf16[1024,256]{1,0:T(8,128)(2,1)S(1)} %bitcast.89), channel_id=1, source_target_pairs={{0,16},{16,0},{32,48},{48,32},{64,80},{80,64},{96,112},{112,96},{1... | collective-permute-start | bytes 1572872 | tf_op jit(solution)/shard_map/ppermute | solution.py:362
  105.6 3.5 %collective-permute-start.17 = (bf16[3,1024,256]{2,1,0:T(8,128)(2,1)S(1)}, bf16[3,1024,256]{2,1,0:T(8,128)(2,1)S(1)}, u32[]{:S(2)}, u32[]{:S(2)}) collective-permute-start(bf16[3,1024,256]{2,1,0:T(8,128)(2,1)S(1)} %bitcast.88), channel_id=1, source_target_pairs={{0,16},{16,0},{32,48},{48,32},{64,80},{80,64},{96,112},{112,96},{1... | collective-permute-start | bytes 4718600 | tf_op jit(solution)/shard_map/ppermute | solution.py:362
  106.0 8.7 %collective-permute-start.18 = (bf16[512,256]{1,0:T(8,128)(2,1)S(1)}, bf16[512,256]{1,0:T(8,128)(2,1)S(1)}, u32[]{:S(2)}, u32[]{:S(2)}) collective-permute-start(bf16[512,256]{1,0:T(8,128)(2,1)S(1)} %get-tuple-element.78), channel_id=1, source_target_pairs={{0,32},{16,48},{32,64},{48,80},{64,96},{80,112},{96,0},{112,16},{1... | collective-permute-start | bytes 786440 | tf_op jit(solution)/shard_map/ppermute | solution.py:362
  107.1 10.0 %collective-permute-start.20 = (bf16[512,256]{1,0:T(8,128)(2,1)S(1)}, bf16[512,256]{1,0:T(8,128)(2,1)S(1)}, u32[]{:S(2)}, u32[]{:S(2)}) collective-permute-start(bf16[512,256]{1,0:T(8,128)(2,1)S(1)} %get-tuple-element.79), channel_id=1, source_target_pairs={{0,96},{16,112},{32,0},{48,16},{64,32},{80,48},{96,64},{112,80},{1... | collective-permute-start | bytes 786440 | tf_op jit(solution)/shard_map/ppermute | solution.py:362
  114.8 2.6 %copy-start.5 = (s32[1024]{0:T(1024)S(1)}, s32[1024]{0:T(1024)}, u32[]{:S(2)}) copy-start(s32[1024]{0:T(1024)} %param.12) | copy-start | bytes 12292
  114.8 2.6 %copy-start.7 = (bf16[256]{0:T(256)(128)(2,1)S(1)}, bf16[256]{0:T(256)(128)(2,1)}, u32[]{:S(2)}) copy-start(bf16[256]{0:T(256)(128)(2,1)} %param.19) | copy-start | bytes 1540
  114.8 13.5 %collective-permute-start.19 = (bf16[1024,256]{1,0:T(8,128)(2,1)S(1)}, bf16[1024,256]{1,0:T(8,128)(2,1)S(1)}, u32[]{:S(2)}, u32[]{:S(2)}) collective-permute-start(bf16[1024,256]{1,0:T(8,128)(2,1)S(1)} %pad_maximum_fusion.10), channel_id=1, source_target_pairs={{0,32},{16,48},{32,64},{48,80},{64,96},{80,112},{96,0},{112,16},{1... | collective-permute-start | bytes 1572872 | tf_op jit(solution)/shard_map/ppermute | solution.py:362
  117.2 14.4 %copy-start.6 = (bf16[256,256]{1,0:T(8,128)(2,1)S(1)}, bf16[256,256]{1,0:T(8,128)(2,1)}, u32[]{:S(2)}) copy-start(bf16[256,256]{1,0:T(8,128)(2,1)} %param.18) | copy-start | bytes 393220
  117.3 14.4 %collective-permute-start.21 = (bf16[1024,256]{1,0:T(8,128)(2,1)S(1)}, bf16[1024,256]{1,0:T(8,128)(2,1)S(1)}, u32[]{:S(2)}, u32[]{:S(2)}) collective-permute-start(bf16[1024,256]{1,0:T(8,128)(2,1)S(1)} %pad_maximum_fusion.11), channel_id=1, source_target_pairs={{0,96},{16,112},{32,0},{48,16},{64,32},{80,48},{96,64},{112,80},{1... | collective-permute-start | bytes 1572872 | tf_op jit(solution)/shard_map/ppermute | solution.py:362

commit v2 on v1

--- a/solution.py
+++ b/solution.py
@@ -60,9 +60,9 @@
     out_ref[...] = data.astype(jnp.bfloat16)
 
 
-def unpack_kernel(in_ref, out_ref):
+def unpack_kernel(in_ref, a_ref, b_ref):
     ins = in_ref.shape[0]
-    rows = out_ref.shape[0]
+    rows = a_ref.shape[0] + b_ref.shape[0]
     data = in_ref[...]
     drop = onehot(iota((128, ins), 1) == iota((128, ins), 0) * SLOT_ROWS + POS_ROW)
     pos_rows = jnp.dot(drop, data, preferred_element_type=jnp.float32).astype(jnp.bfloat16)
@@ -77,7 +77,13 @@
     low = lanes(pos_rows[:, 128:])
     target = 4 * (high - 1) + 2 * low + (iota((1, ins), 1) & 1)
     pick = onehot(iota((rows, ins), 0) == target)
-    out_ref[...] = jnp.dot(pick, data, preferred_element_type=jnp.float32).astype(jnp.bfloat16)
+    owned = jnp.dot(pick, data, preferred_element_type=jnp.float32).astype(jnp.bfloat16)
+    a_ref[...] = owned[: rows // 2]
+    b_ref[...] = owned[rows // 2 :]
+
+
+def ring_order(step):
+    return jnp.where(step == 0, 0, jnp.where(step == 3, 1, jnp.where(step == 1, 2, 3)))
 
 
 def plan_kernel(where_ref, count_ref, rows_ref, cols_ref, code_ref, start_ref):
@@ -87,19 +93,14 @@
     row = rows_ref[...]
     col = cols_ref[...]
     source = col >> 3
-    dz = ((source >> 2) - z) & 3
-    dy = ((source & 3) - y) & 3
-    steps = jnp.where(dz == 3, 1, dz) + jnp.where(dy == 3, 1, dy)
-    stage = jnp.maximum(steps - 1, 0)
-    part, rest = (col & 7) >> 2, col & 3
-    side_z, side_y = jnp.where(dz == 3, 0, 4), jnp.where(dy == 3, 0, 4)
-    tile_0 = jnp.where(dz == 0, jnp.where(dy == 0, 0, side_y * 2 + 8), side_z * 2 + 24) + (col & 7)
-    corner = jnp.where(part == 0, side_y * 3 + side_z, side_z * 3 + side_y + 24)
-    tile_1 = jnp.where(dz == 0, part * 12 + 8, jnp.where(dy == 0, part * 12 + 32, corner)) + rest
-    on_y = jnp.where(part == 0, 4 - side_z, side_z + 8)
-    on_z = jnp.where(part == 1, 20 - side_y, side_y + 24)
-    tile_2 = jnp.where(dy == 2, on_y, on_z) + rest
-    tile = jnp.where(stage == 0, tile_0, jnp.where(stage == 1, tile_1, jnp.where(stage == 2, tile_2, col & 7)))
+    order_z = ring_order(((source >> 2) - z) & 3)
+    order_y = ring_order(((source & 3) - y) & 3)
+    half = (col >> 2) & 1
+    outer = jnp.where(half == 0, order_z, order_y)
+    inner = jnp.where(half == 0, order_y, order_z)
+    stage = jnp.where((outer == 1) == (inner < 2), 1, 2)
+    stage = jnp.where(outer == 3, 3, jnp.where(outer == 0, 0, stage))
+    tile = half * 16 + inner * 4 + (col & 3)
     owner = row >> 3
     dx = ((owner >> 1) - x) & 3
     order_x = jnp.where(dx == 2, 0, jnp.where(dx == 1, 1, jnp.where(dx == 3, 2, 3)))
@@ -291,11 +292,11 @@
     )
     half = rows // 2
     quarter = half // 2
-    owned = pl.pallas_call(
+    a0, b0 = pl.pallas_call(
         unpack_kernel,
-        out_shape=jax.ShapeDtypeStruct((rows, width), jnp.bfloat16),
+        out_shape=(jax.ShapeDtypeStruct((half, width), jnp.bfloat16),) * 2,
         in_specs=[vmem],
-        out_specs=vmem,
+        out_specs=(vmem, vmem),
         compiler_params=big,
         name="unpack",
     )(incoming.reshape(devices * SLOT_ROWS, width))
@@ -318,42 +319,33 @@
     def send(v, dz, dy):
         return lax.ppermute(v, "col", col_perm(dz, dy))
 
-    def spread(to_yp, to_ym, to_zp, to_zm):
-        return [send(to_yp, 0, 1), send(to_ym, 0, -1), send(to_zp, 1, 0), send(to_zm, -1, 0)]
-
     def cat(*parts):
         return jnp.concatenate(parts, axis=0)
 
-    def one(v):
-        return v[:half]
-
-    def two(v):
-        return v[half:]
-
-    near = spread(owned, owned, owned, owned)
-    *near, code, start = lax.optimization_barrier((*near, code, start))
-    ym, yp, zm, zp = near
+    ap, am = send(a0, 0, 1), send(a0, 0, -1)
+    bp, bm = send(b0, 1, 0), send(b0, -1, 0)
+    bp, bm, code, start = lax.optimization_barrier((bp, bm, code, start))
+    a_far = (send(ap[:quarter], 0, 1), send(am[quarter:], 0, -1))
+    b_far = (send(bp[:quarter], 1, 0), send(bm[quarter:], -1, 0))
+    ap, b_far = lax.optimization_barrier((ap, b_far))
+    bp, a_far = lax.optimization_barrier((bp, a_far))
+    a_lo, b_lo = cat(a0, ap), cat(b0, bp)
+    a_hi, b_hi = cat(am, *a_far), cat(bm, *b_far)
     lists = (code, start, weights)
-    diagonal = spread(
-        cat(one(zm), one(zp), one(ym)),
-        cat(one(zm), one(zp), two(yp)),
-        cat(two(ym), two(yp), one(zm)),
-        cat(two(ym), two(yp), two(zp)),
-    )
-    state = run_tiles(0, *lists, [owned, *near])
-    (ym, yp, zm, zp), state = lax.optimization_barrier((diagonal, state))
-    third = spread(
-        cat(ym[half:rows], one(ym)),
-        cat(zm[half:rows], zp[half:rows]),
-        cat(zm[half:rows], one(zm)),
-        cat(ym[half:rows], yp[half:rows]),
-    )
-    state = run_tiles(1, *lists, [ym, yp, zm, zp], state)
-    (ym, yp, zm, zp), state = lax.optimization_barrier((third, state))
-    last = spread(zp[:quarter], zp[-quarter:], yp[:quarter], yp[-quarter:])
-    state = run_tiles(2, *lists, [ym, yp, zm, zp], state)
+    a_lo_p, a_hi_m = send(a_lo, 1, 0), send(a_hi, -1, 0)
+    b_lo_p, b_hi_m = send(b_lo, 0, 1), send(b_hi, 0, -1)
+    state = run_tiles(0, *lists, [a_lo, a_hi, b_lo, b_hi])
+    a_lo, a_hi, b_lo, b_hi, *state = lax.optimization_barrier((a_lo, a_hi, b_lo, b_hi, *state))
+    a_hi_p, a_lo_m = send(a_hi, 1, 0), send(a_lo, -1, 0)
+    b_hi_p, b_lo_m = send(b_hi, 0, 1), send(b_lo, 0, -1)
+    state = run_tiles(1, *lists, [a_lo_p, a_hi_m, b_lo_p, b_hi_m], state)
+    a_lo_p, a_hi_m, b_lo_p, b_hi_m, *state = lax.optimization_barrier(
+        (a_lo_p, a_hi_m, b_lo_p, b_hi_m, *state)
+    )
+    far = [send(a_lo_p, 1, 0), send(a_hi_m, -1, 0), send(b_lo_p, 0, 1), send(b_hi_m, 0, -1)]
+    state = run_tiles(2, *lists, [a_lo_m, a_hi_p, b_lo_m, b_hi_p], state)
     *_, other_far, mine_far, other_rest, mine_rest = run_tiles(
-        3, *lists, last, state, ((0, 8), (8, 8), (16, 24), (40, 24))
+        3, *lists, far, state, ((0, 8), (8, 8), (16, 24), (40, 24))
     )
 
     f32 = jnp.float32
@@ -373,7 +365,7 @@
     summed = both[2] + over(to_plus, 1).astype(f32) + over(to_minus, -1).astype(f32)
 
     neighbor_mean = (summed / degree.astype(f32)[:, None]).astype(jnp.bfloat16)
-    total = jnp.dot(owned, w_self, preferred_element_type=f32)
+    total = jnp.dot(cat(a0, b0), w_self, preferred_element_type=f32)
     total = total + jnp.dot(neighbor_mean, w_neigh, preferred_element_type=f32)
     total = total + bias.astype(f32)[None, :]
     return jnp.maximum(total, f32(0.0)).astype(jnp.bfloat16)

time: 133 us -> 130 us (0.977)
  waiting for transfers between devices: 46.3 us -> 34.1 us
  starting transfers between devices: 30.1 us -> 35.5 us
  Pallas kernels: 22.2 us -> 25.5 us
    ppermute x16 -> x20, waiting for transfers between devices: 24.2 us -> 12.1 us  [send(): return lax.ppermute(v, 'col', col_perm(dz, dy))]
    ppermute x16 -> x20, starting transfers between devices: 25.3 us -> 30.6 us  [send(): return lax.ppermute(v, 'col', col_perm(dz, dy))]
    pallas_call x4, Pallas kernels: 15.5 us -> 18.9 us  [run_tiles(): pl.pallas_call(functools.partial(tiles_kernel, stage, n, outs), out_shape...]
  transfers between devices with their start and end apart: 22 -> 26, of which waited for: 12 -> 12; matrix products, arithmetic and copies ran while one was open for 1% -> 1% of each run, Pallas kernels for 11% -> 13%
where the time goes in v2:
time: 130 us; the launch traced here: 129 us
  starting transfers between devices  35.5 us (27%)
  waiting for transfers between devices  34.1 us (26%)
  blocking collectives  28.4 us (22%)
  Pallas kernels  25.5 us (20%)
  local copies, waits for them, and re-layouts  2.21 us (2%)
  matrix products  1.58 us (1%)
    ppermute x20, starting transfers between devices, send(): return lax.ppermute(v, 'col', col_perm(dz, dy))  30.6 us
    all_to_all x1, blocking collectives, per_device(): lax.all_to_all(outgoing.reshape(devices, SLOT_ROWS, width), ('row', 'col'...  28.4 us
    ppermute x6, waiting for transfers between devices, over(): return lax.ppermute(v, 'row', row_perm(dx, flip))  22 us
    pallas_call x4, Pallas kernels, run_tiles(): pl.pallas_call(functools.partial(tiles_kernel, stage, n, outs), out_shape...  18.9 us
    ppermute x20, waiting for transfers between devices, send(): return lax.ppermute(v, 'col', col_perm(dz, dy))  12.1 us
    ppermute x6, starting transfers between devices, over(): return lax.ppermute(v, 'row', row_perm(dx, flip))  4.9 us
    pallas_call x1, Pallas kernels, per_device(): pl.pallas_call(pack_kernel, out_shape=jax.ShapeDtypeStruct((devices * SLO...  2.74 us
  transfers between devices with their start and end apart: 26, of which 12 were waited for; matrix products, arithmetic and copies ran while one was open for 1% of the time, Pallas kernels for 13%

profile of v2, /device:TPU:6, one launch (start us, length us, event | category | flops | bytes accessed | tf_op | source)
XLA Modules:
  0.0 129.2 jit_solution(1561789156388776001)
XLA Ops:
  0.0 1.1 copy-done.1
  1.1 0.7 copy-done.4
  1.8 2.7 %pack.1 = bf16[2048,256]{1,0:T(8,128)(2,1)S(1)} custom-call(s32[1,512]{1,0:T(1,128)S(1)} %bitcast.84, bf16[1024,256]{1,0:T(8,128)(2,1)S(1)} %copy-done.1), custom_call_target="tpu_custom_call" | custom-call | tf_op jit(solution)/shard_map/pack/pallas_call | solution.py:278
  4.5 28.4 %all_to_all.5 = bf16[128,16,256]{2,1,0:T(8,128)(2,1)S(1)} all-to-all(bf16[128,16,256]{2,1,0:T(8,128)(2,1)S(1)} %bitcast.61), channel_id=1, replica_groups=mesh['row'=8,'col'=16] {'row','col'}, dimensions={0} | all-to-all | bytes 2097152 | tf_op jit(solution)/shard_map/all_to_all | solution.py:286
  32.9 2.1 %unpack.1 = (bf16[512,256]{1,0:T(8,128)(2,1)S(1)}, bf16[512,256]{1,0:T(8,128)(2,1)S(1)}) custom-call(bf16[2048,256]{1,0:T(8,128)(2,1)S(1)} %bitcast.60), custom_call_target="tpu_custom_call" | custom-call | tf_op jit(solution)/shard_map/unpack/pallas_call | solution.py:295
  35.0 0.9 collective-permute-start
  35.9 2.4 %collective-permute-start.1 = (bf16[512,256]{1,0:T(8,128)(2,1)S(1)}, bf16[512,256]{1,0:T(8,128)(2,1)S(1)}, u32[]{:S(2)}, u32[]{:S(2)}) collective-permute-start(bf16[512,256]{1,0:T(8,128)(2,1)S(1)} %get-tuple-element.44), channel_id=1, source_target_pairs={{0,12},{1,13},{2,14},{3,15},{4,0},{5,1},{6,2},{7,3},{8,4},{9,5},{1... | collective-permute-start | bytes 786440 | tf_op jit(solution)/shard_map/ppermute | solution.py:320
  38.3 0.6 collective-permute-start.2
  38.9 2.6 %collective-permute-start.6 = (bf16[512,256]{1,0:T(8,128)(2,1)S(1)}, bf16[512,256]{1,0:T(8,128)(2,1)S(1)}, u32[]{:S(2)}, u32[]{:S(2)}) collective-permute-start(bf16[512,256]{1,0:T(8,128)(2,1)S(1)} %get-tuple-element.43), channel_id=1, source_target_pairs={{0,3},{1,0},{2,1},{3,2},{4,7},{5,4},{6,5},{7,6},{8,11},{9,8},{10,9... | collective-permute-start | bytes 786440 | tf_op jit(solution)/shard_map/ppermute | solution.py:320
  42.3 1.9 %plan.1 = (s32[1,1024]{1,0:T(1,128)S(1)}, s32[1,384]{1,0:T(1,128)S(1)}) custom-call(s32[4]{0:T(128)S(1)} %pad_add_fusion.where_ref, s32[1]{0:T(128)} %bitcast.59.count_ref, s32[1,704]{1,0:T(1,128)S(1)} %bitcast.82, s32[1,704]{1,0:T(1,128)S(1)} %bitcast.83), custom_call_target="tpu_custom_call" | custom-call | tf_op jit(solution)/shard_map/plan/pallas_call | solution.py:304
  44.4 3.3 %collective-permute-start.4 = (bf16[256,256]{1,0:T(8,128)(2,1)S(1)}, bf16[256,256]{1,0:T(8,128)(2,1)S(1)}, u32[]{:S(2)}, u32[]{:S(2)}) collective-permute-start(bf16[256,256]{1,0:T(8,128)(2,1)S(1)} %slice.54), channel_id=1, source_target_pairs={{0,12},{1,13},{2,14},{3,15},{4,0},{5,1},{6,2},{7,3},{8,4},{9,5},{1... | collective-permute-start | bytes 393224 | tf_op jit(solution)/shard_map/ppermute | solution.py:320
  47.7 0.7 collective-permute-start.7
  48.4 2.7 %collective-permute-start.8 = (bf16[256,256]{1,0:T(8,128)(2,1)S(1)}, bf16[256,256]{1,0:T(8,128)(2,1)S(1)}, u32[]{:S(2)}, u32[]{:S(2)}) collective-permute-start(bf16[256,256]{1,0:T(8,128)(2,1)S(1)} %slice.70), channel_id=1, source_target_pairs={{0,3},{1,0},{2,1},{3,2},{4,7},{5,4},{6,5},{7,6},{8,11},{9,8},{10,9... | collective-permute-start | bytes 393224 | tf_op jit(solution)/shard_map/ppermute | solution.py:320
  51.1 2.8 %collective-permute-done.7 = bf16[256,256]{1,0:T(8,128)(2,1)S(1)} collective-permute-done((bf16[256,256]{1,0:T(8,128)(2,1)S(1)}, bf16[256,256]{1,0:T(8,128)(2,1)S(1)}, u32[]{:S(2)}, u32[]{:S(2)}) %collective-permute-start.7) | collective-permute-done | bytes 131104 | tf_op jit(solution)/shard_map/ppermute | solution.py:320
  53.9 3.4 %collective-permute-start.11 = (bf16[1024,256]{1,0:T(8,128)(2,1)S(1)}, bf16[1024,256]{1,0:T(8,128)(2,1)S(1)}, u32[]{:S(2)}, u32[]{:S(2)}) collective-permute-start(bf16[1024,256]{1,0:T(8,128)(2,1)S(1)} %constant_dynamic-update-slice_fusion.7), channel_id=1, source_target_pairs={{0,3},{1,0},{2,1},{3,2},{4,7},{5,4},{6,5},{7,6},{8,11},{9,8},{10,9... | collective-permute-start | bytes 1572872 | tf_op jit(solution)/shard_map/ppermute | solution.py:320
  57.5 1.8 %collective-permute-start.9 = (bf16[1024,256]{1,0:T(8,128)(2,1)S(1)}, bf16[1024,256]{1,0:T(8,128)(2,1)S(1)}, u32[]{:S(2)}, u32[]{:S(2)}) collective-permute-start(bf16[1024,256]{1,0:T(8,128)(2,1)S(1)} %constant_dynamic-update-slice_fusion.2), channel_id=1, source_target_pairs={{0,12},{1,13},{2,14},{3,15},{4,0},{5,1},{6,2},{7,3},{8,4},{9,5},{1... | collective-permute-start | bytes 1572872 | tf_op jit(solution)/shard_map/ppermute | solution.py:320
  59.3 0.4 collective-permute-start.5
  59.7 5.7 %tiles_0.1 = (f32[64,128,256]{2,1,0:T(8,128)S(1)}, bf16[8,16,128,128]{3,2,1,0:T(8,128)(2,1)S(1)}) custom-call(s32[1024]{0:T(1024)S(1)} %bitcast.78, s32[384]{0:T(512)S(1)} %reduce.refs_1_, bf16[704,128,128]{2,1,0:T(8,128)(2,1)} %bitcast.87, bf16[8,128,256]{2,1,0:T(8,128)(2,1)S(1)} %bitcast.63, bf16[8,128,256]{2,1,0:T(8,128)(2,1)S(1)} %bitcast.65, ...), custom_call_target="tpu_custom_call" | custom-call | flops 1476395008 | bytes 5767168 | tf_op jit(solution)/shard_map/tiles_0/pallas_call | solution.py:236
  65.4 3.0 %collective-permute-start.16 = (bf16[1024,256]{1,0:T(8,128)(2,1)S(1)}, bf16[1024,256]{1,0:T(8,128)(2,1)S(1)}, u32[]{:S(2)}, u32[]{:S(2)}) collective-permute-start(bf16[1024,256]{1,0:T(8,128)(2,1)S(1)} %constant_dynamic-update-slice_fusion), channel_id=1, source_target_pairs={{0,12},{1,13},{2,14},{3,15},{4,0},{5,1},{6,2},{7,3},{8,4},{9,5},{1... | collective-permute-start | bytes 1572872 | tf_op jit(solution)/shard_map/ppermute | solution.py:320
  68.4 0.7 collective-permute-done.10
  69.1 3.0 %collective-permute-start.18 = (bf16[1024,256]{1,0:T(8,128)(2,1)S(1)}, bf16[1024,256]{1,0:T(8,128)(2,1)S(1)}, u32[]{:S(2)}, u32[]{:S(2)}) collective-permute-start(bf16[1024,256]{1,0:T(8,128)(2,1)S(1)} %constant_dynamic-update-slice_fusion.5), channel_id=1, source_target_pairs={{0,3},{1,0},{2,1},{3,2},{4,7},{5,4},{6,5},{7,6},{8,11},{9,8},{10,9... | collective-permute-start | bytes 1572872 | tf_op jit(solution)/shard_map/ppermute | solution.py:320
  72.1 1.0 collective-permute-done.5
  73.1 4.2 %tiles_1.1 = (f32[64,128,256]{2,1,0:T(8,128)S(1)}, bf16[8,16,128,128]{3,2,1,0:T(8,128)(2,1)S(1)}) custom-call(s32[1024]{0:T(1024)S(1)} %bitcast.79, s32[384]{0:T(512)S(1)} %reduce.refs_1_, bf16[704,128,128]{2,1,0:T(8,128)(2,1)} %bitcast.88, bf16[8,128,256]{2,1,0:T(8,128)(2,1)S(1)} %bitcast.69, ...), custom_call_target="tpu_custom_call", output_to_operand_aliasing={{0}: (7, {}), {1}: (8, {})} | custom-call | flops 1476395008 | bytes 5767168 | tf_op jit(solution)/shard_map/tiles_1/pallas_call | solution.py:236
  77.3 0.1 collective-permute-start.12
  77.4 2.5 %collective-permute-done.16 = bf16[1024,256]{1,0:T(8,128)(2,1)S(1)} collective-permute-done((bf16[1024,256]{1,0:T(8,128)(2,1)S(1)}, bf16[1024,256]{1,0:T(8,128)(2,1)S(1)}, u32[]{:S(2)}, u32[]{:S(2)}) %collective-permute-start.16) | collective-permute-done | bytes 524320 | tf_op jit(solution)/shard_map/ppermute | solution.py:320
  79.9 2.0 %collective-permute-start.13 = (bf16[1024,256]{1,0:T(8,128)(2,1)S(1)}, bf16[1024,256]{1,0:T(8,128)(2,1)S(1)}, u32[]{:S(2)}, u32[]{:S(2)}) collective-permute-start(bf16[1024,256]{1,0:T(8,128)(2,1)S(1)} %collective-permute-done.9), channel_id=1, source_target_pairs={{0,12},{1,13},{2,14},{3,15},{4,0},{5,1},{6,2},{7,3},{8,4},{9,5},{1... | collective-permute-start | bytes 1572872 | tf_op jit(solution)/shard_map/ppermute | solution.py:320
  81.9 2.6 %collective-permute-done.17 = bf16[1024,256]{1,0:T(8,128)(2,1)S(1)} collective-permute-done((bf16[1024,256]{1,0:T(8,128)(2,1)S(1)}, bf16[1024,256]{1,0:T(8,128)(2,1)S(1)}, u32[]{:S(2)}, u32[]{:S(2)}) %collective-permute-start.17) | collective-permute-done | bytes 524320 | tf_op jit(solution)/shard_map/ppermute | solution.py:320
  84.5 3.6 %collective-permute-start.15 = (bf16[1024,256]{1,0:T(8,128)(2,1)S(1)}, bf16[1024,256]{1,0:T(8,128)(2,1)S(1)}, u32[]{:S(2)}, u32[]{:S(2)}) collective-permute-start(bf16[1024,256]{1,0:T(8,128)(2,1)S(1)} %collective-permute-done.11), channel_id=1, source_target_pairs={{0,3},{1,0},{2,1},{3,2},{4,7},{5,4},{6,5},{7,6},{8,11},{9,8},{10,9... | collective-permute-start | bytes 1572872 | tf_op jit(solution)/shard_map/ppermute | solution.py:320
  88.1 4.6 %tiles_2.1 = (f32[64,128,256]{2,1,0:T(8,128)S(1)}, bf16[8,16,128,128]{3,2,1,0:T(8,128)(2,1)S(1)}) custom-call(s32[1024]{0:T(1024)S(1)} %bitcast.80, s32[384]{0:T(512)S(1)} %reduce.refs_1_, bf16[704,128,128]{2,1,0:T(8,128)(2,1)} %bitcast.89, bf16[8,128,256]{2,1,0:T(8,128)(2,1)S(1)} %bitcast.70, ...), custom_call_target="tpu_custom_call", output_to_operand_aliasing={{0}: (7, {}), {1}: (8, {})} | custom-call | flops 1476395008 | bytes 5767168 | tf_op jit(solution)/shard_map/tiles_2/pallas_call | solution.py:236
  92.7 0.2 collective-permute-done.12
  92.9 2.3 %collective-permute-done.14 = bf16[1024,256]{1,0:T(8,128)(2,1)S(1)} collective-permute-done((bf16[1024,256]{1,0:T(8,128)(2,1)S(1)}, bf16[1024,256]{1,0:T(8,128)(2,1)S(1)}, u32[]{:S(2)}, u32[]{:S(2)}) %collective-permute-start.14) | collective-permute-done | bytes 524320 | tf_op jit(solution)/shard_map/ppermute | solution.py:320
  95.2 4.3 %tiles_3.1 = (f32[64,128,256]{2,1,0:T(8,128)S(1)}, bf16[8,16,128,128]{3,2,1,0:T(8,128)(2,1)S(1)}, bf16[8,128,256]{2,1,0:T(8,128)(2,1)S(1)}, bf16[8,128,256]{2,1,...) custom-call(s32[1024]{0:T(1024)S(1)} %bitcast.81, ...), custom_call_target="tpu_custom_call", output_to_operand_aliasing={{0}: (7, {}), {1}: (8, {})} | custom-call | flops 1476395008 | bytes 5767168 | tf_op jit(solution)/shard_map/tiles_3/pallas_call | solution.py:236
  99.5 0.1 collective-permute-start.20
  99.6 1.9 %collective-permute-done.20 = bf16[1024,256]{1,0:T(8,128)(2,1)S(1)} collective-permute-done((bf16[1024,256]{1,0:T(8,128)(2,1)S(1)}, bf16[1024,256]{1,0:T(8,128)(2,1)S(1)}, u32[]{:S(2)}, u32[]{:S(2)}) %collective-permute-start.20) | collective-permute-done | bytes 524320 | tf_op jit(solution)/shard_map/ppermute | solution.py:354
  101.5 0.2 fusion.6
  101.7 0.2 collective-permute-start.21
  101.9 0.1 fusion.17
  102.1 1.2 collective-permute-start.22
  103.3 0.9 collective-permute-start.24
  104.2 1.0 collective-permute-done.21
  105.2 0.3 convert_add_fusion.1
  105.6 5.2 %collective-permute-done.22 = bf16[512,256]{1,0:T(8,128)(2,1)S(1)} collective-permute-done((bf16[512,256]{1,0:T(8,128)(2,1)S(1)}, bf16[512,256]{1,0:T(8,128)(2,1)S(1)}, u32[]{:S(2)}, u32[]{:S(2)}) %collective-permute-start.22) | collective-permute-done | bytes 262176 | tf_op jit(solution)/shard_map/ppermute | solution.py:354
  110.9 2.4 %collective-permute-start.23 = (bf16[1024,256]{1,0:T(8,128)(2,1)S(1)}, bf16[1024,256]{1,0:T(8,128)(2,1)S(1)}, u32[]{:S(2)}, u32[]{:S(2)}) collective-permute-start(bf16[1024,256]{1,0:T(8,128)(2,1)S(1)} %pad_maximum_fusion), channel_id=1, source_target_pairs={{0,32},{16,48},{32,64},{48,80},{64,96},{80,112},{96,0},{112,16},{1... | collective-permute-start | bytes 1572872 | tf_op jit(solution)/shard_map/ppermute | solution.py:354
  113.4 0.1 fusion.9
  113.6 0.3 fusion.11
  113.9 10.4 %collective-permute-done.23 = bf16[1024,256]{1,0:T(8,128)(2,1)S(1)} collective-permute-done((bf16[1024,256]{1,0:T(8,128)(2,1)S(1)}, bf16[1024,256]{1,0:T(8,128)(2,1)S(1)}, u32[]{:S(2)}, u32[]{:S(2)}) %collective-permute-start.23) | collective-permute-done | bytes 524320 | tf_op jit(solution)/shard_map/ppermute | solution.py:354
  124.4 3.5 %collective-permute-done.25 = bf16[1024,256]{1,0:T(8,128)(2,1)S(1)} collective-permute-done((bf16[1024,256]{1,0:T(8,128)(2,1)S(1)}, bf16[1024,256]{1,0:T(8,128)(2,1)S(1)}, u32[]{:S(2)}, u32[]{:S(2)}) %collective-permute-start.25) | collective-permute-done | bytes 524320 | tf_op jit(solution)/shard_map/ppermute | solution.py:354
  127.9 1.3 fusion.2
  (58 shorter events, 0.9 us)
Async XLA Ops:
  0.0 113.6 %copy-start = (bf16[256,256]{1,0:T(8,128)(2,1)S(1)}, bf16[256,256]{1,0:T(8,128)(2,1)}, u32[]{:S(2)}) copy-start(bf16[256,256]{1,0:T(8,128)(2,1)} %param.17) | copy-start | bytes 393220
  0.0 1.1 copy-start.1
  1.1 0.7 copy-start.4
  1.8 40.5 %copy-start.2 = (s32[1,1,704]{2,1,0:T(1,128)S(1)}, s32[1,1,704]{2,1,0:T(1,128)}, u32[]{:S(2)}) copy-start(s32[1,1,704]{2,1,0:T(1,128)} %param.13) | copy-start | bytes 8452
  1.8 40.5 %copy-start.3 = (s32[1,1,704]{2,1,0:T(1,128)S(1)}, s32[1,1,704]{2,1,0:T(1,128)}, u32[]{:S(2)}) copy-start(s32[1,1,704]{2,1,0:T(1,128)} %param.14) | copy-start | bytes 8452
  35.0 9.3 %collective-permute-start = (bf16[512,256]{1,0:T(8,128)(2,1)S(1)}, bf16[512,256]{1,0:T(8,128)(2,1)S(1)}, u32[]{:S(2)}, u32[]{:S(2)}) collective-permute-start(bf16[512,256]{1,0:T(8,128)(2,1)S(1)} %get-tuple-element.44), channel_id=1, source_target_pairs={{0,4},{1,5},{2,6},{3,7},{4,8},{5,9},{6,10},{7,11},{8,12},{9,13},{1... | collective-permute-start | bytes 786440 | tf_op jit(solution)/shard_map/ppermute | solution.py:320
  35.9 8.4 %collective-permute-start.1 = (bf16[512,256]{1,0:T(8,128)(2,1)S(1)}, bf16[512,256]{1,0:T(8,128)(2,1)S(1)}, u32[]{:S(2)}, u32[]{:S(2)}) collective-permute-start(bf16[512,256]{1,0:T(8,128)(2,1)S(1)} %get-tuple-element.44), channel_id=1, source_target_pairs={{0,12},{1,13},{2,14},{3,15},{4,0},{5,1},{6,2},{7,3},{8,4},{9,5},{1... | collective-permute-start | bytes 786440 | tf_op jit(solution)/shard_map/ppermute | solution.py:320
  38.3 9.4 %collective-permute-start.2 = (bf16[512,256]{1,0:T(8,128)(2,1)S(1)}, bf16[512,256]{1,0:T(8,128)(2,1)S(1)}, u32[]{:S(2)}, u32[]{:S(2)}) collective-permute-start(bf16[512,256]{1,0:T(8,128)(2,1)S(1)} %get-tuple-element.43), channel_id=1, source_target_pairs={{0,1},{1,2},{2,3},{3,0},{4,5},{5,6},{6,7},{7,4},{8,9},{9,10},{10,1... | collective-permute-start | bytes 786440 | tf_op jit(solution)/shard_map/ppermute | solution.py:320
  38.9 9.4 %collective-permute-start.6 = (bf16[512,256]{1,0:T(8,128)(2,1)S(1)}, bf16[512,256]{1,0:T(8,128)(2,1)S(1)}, u32[]{:S(2)}, u32[]{:S(2)}) collective-permute-start(bf16[512,256]{1,0:T(8,128)(2,1)S(1)} %get-tuple-element.43), channel_id=1, source_target_pairs={{0,3},{1,0},{2,1},{3,2},{4,7},{5,4},{6,5},{7,6},{8,11},{9,8},{10,9... | collective-permute-start | bytes 786440 | tf_op jit(solution)/shard_map/ppermute | solution.py:320
  44.3 6.8 %collective-permute-start.3 = (bf16[256,256]{1,0:T(8,128)(2,1)S(1)}, bf16[256,256]{1,0:T(8,128)(2,1)S(1)}, u32[]{:S(2)}, u32[]{:S(2)}) collective-permute-start(bf16[256,256]{1,0:T(8,128)(2,1)S(1)} %slice.53), channel_id=1, source_target_pairs={{0,4},{1,5},{2,6},{3,7},{4,8},{5,9},{6,10},{7,11},{8,12},{9,13},{1... | collective-permute-start | bytes 393224 | tf_op jit(solution)/shard_map/ppermute | solution.py:320
  44.4 6.8 %collective-permute-start.4 = (bf16[256,256]{1,0:T(8,128)(2,1)S(1)}, bf16[256,256]{1,0:T(8,128)(2,1)S(1)}, u32[]{:S(2)}, u32[]{:S(2)}) collective-permute-start(bf16[256,256]{1,0:T(8,128)(2,1)S(1)} %slice.54), channel_id=1, source_target_pairs={{0,12},{1,13},{2,14},{3,15},{4,0},{5,1},{6,2},{7,3},{8,4},{9,5},{1... | collective-permute-start | bytes 393224 | tf_op jit(solution)/shard_map/ppermute | solution.py:320
  47.7 6.2 %collective-permute-start.7 = (bf16[256,256]{1,0:T(8,128)(2,1)S(1)}, bf16[256,256]{1,0:T(8,128)(2,1)S(1)}, u32[]{:S(2)}, u32[]{:S(2)}) collective-permute-start(bf16[256,256]{1,0:T(8,128)(2,1)S(1)} %slice.69), channel_id=1, source_target_pairs={{0,1},{1,2},{2,3},{3,0},{4,5},{5,6},{6,7},{7,4},{8,9},{9,10},{10,1... | collective-permute-start | bytes 393224 | tf_op jit(solution)/shard_map/ppermute | solution.py:320
  48.4 5.5 %collective-permute-start.8 = (bf16[256,256]{1,0:T(8,128)(2,1)S(1)}, bf16[256,256]{1,0:T(8,128)(2,1)S(1)}, u32[]{:S(2)}, u32[]{:S(2)}) collective-permute-start(bf16[256,256]{1,0:T(8,128)(2,1)S(1)} %slice.70), channel_id=1, source_target_pairs={{0,3},{1,0},{2,1},{3,2},{4,7},{5,4},{6,5},{7,6},{8,11},{9,8},{10,9... | collective-permute-start | bytes 393224 | tf_op jit(solution)/shard_map/ppermute | solution.py:320
  53.9 14.4 %collective-permute-start.11 = (bf16[1024,256]{1,0:T(8,128)(2,1)S(1)}, bf16[1024,256]{1,0:T(8,128)(2,1)S(1)}, u32[]{:S(2)}, u32[]{:S(2)}) collective-permute-start(bf16[1024,256]{1,0:T(8,128)(2,1)S(1)} %constant_dynamic-update-slice_fusion.7), channel_id=1, source_target_pairs={{0,3},{1,0},{2,1},{3,2},{4,7},{5,4},{6,5},{7,6},{8,11},{9,8},{10,9... | collective-permute-start | bytes 1572872 | tf_op jit(solution)/shard_map/ppermute | solution.py:320
  57.4 11.7 %collective-permute-start.10 = (bf16[1024,256]{1,0:T(8,128)(2,1)S(1)}, bf16[1024,256]{1,0:T(8,128)(2,1)S(1)}, u32[]{:S(2)}, u32[]{:S(2)}) collective-permute-start(bf16[1024,256]{1,0:T(8,128)(2,1)S(1)} %constant_dynamic-update-slice_fusion.5), channel_id=1, source_target_pairs={{0,1},{1,2},{2,3},{3,0},{4,5},{5,6},{6,7},{7,4},{8,9},{9,10},{10,1... | collective-permute-start | bytes 1572872 | tf_op jit(solution)/shard_map/ppermute | solution.py:320
  57.5 14.6 %collective-permute-start.9 = (bf16[1024,256]{1,0:T(8,128)(2,1)S(1)}, bf16[1024,256]{1,0:T(8,128)(2,1)S(1)}, u32[]{:S(2)}, u32[]{:S(2)}) collective-permute-start(bf16[1024,256]{1,0:T(8,128)(2,1)S(1)} %constant_dynamic-update-slice_fusion.2), channel_id=1, source_target_pairs={{0,12},{1,13},{2,14},{3,15},{4,0},{5,1},{6,2},{7,3},{8,4},{9,5},{1... | collective-permute-start | bytes 1572872 | tf_op jit(solution)/shard_map/ppermute | solution.py:320
  59.3 13.7 %collective-permute-start.5 = (bf16[1024,256]{1,0:T(8,128)(2,1)S(1)}, bf16[1024,256]{1,0:T(8,128)(2,1)S(1)}, u32[]{:S(2)}, u32[]{:S(2)}) collective-permute-start(bf16[1024,256]{1,0:T(8,128)(2,1)S(1)} %constant_dynamic-update-slice_fusion), channel_id=1, source_target_pairs={{0,4},{1,5},{2,6},{3,7},{4,8},{5,9},{6,10},{7,11},{8,12},{9,13},{1... | collective-permute-start | bytes 1572872 | tf_op jit(solution)/shard_map/ppermute | solution.py:320
  65.4 14.5 %collective-permute-start.16 = (bf16[1024,256]{1,0:T(8,128)(2,1)S(1)}, bf16[1024,256]{1,0:T(8,128)(2,1)S(1)}, u32[]{:S(2)}, u32[]{:S(2)}) collective-permute-start(bf16[1024,256]{1,0:T(8,128)(2,1)S(1)} %constant_dynamic-update-slice_fusion), channel_id=1, source_target_pairs={{0,12},{1,13},{2,14},{3,15},{4,0},{5,1},{6,2},{7,3},{8,4},{9,5},{1... | collective-permute-start | bytes 1572872 | tf_op jit(solution)/shard_map/ppermute | solution.py:320
  68.4 16.1 %collective-permute-start.17 = (bf16[1024,256]{1,0:T(8,128)(2,1)S(1)}, bf16[1024,256]{1,0:T(8,128)(2,1)S(1)}, u32[]{:S(2)}, u32[]{:S(2)}) collective-permute-start(bf16[1024,256]{1,0:T(8,128)(2,1)S(1)} %constant_dynamic-update-slice_fusion.2), channel_id=1, source_target_pairs={{0,4},{1,5},{2,6},{3,7},{4,8},{5,9},{6,10},{7,11},{8,12},{9,13},{1... | collective-permute-start | bytes 1572872 | tf_op jit(solution)/shard_map/ppermute | solution.py:320
  69.1 15.4 %collective-permute-start.18 = (bf16[1024,256]{1,0:T(8,128)(2,1)S(1)}, bf16[1024,256]{1,0:T(8,128)(2,1)S(1)}, u32[]{:S(2)}, u32[]{:S(2)}) collective-permute-start(bf16[1024,256]{1,0:T(8,128)(2,1)S(1)} %constant_dynamic-update-slice_fusion.5), channel_id=1, source_target_pairs={{0,3},{1,0},{2,1},{3,2},{4,7},{5,4},{6,5},{7,6},{8,11},{9,8},{10,9... | collective-permute-start | bytes 1572872 | tf_op jit(solution)/shard_map/ppermute | solution.py:320
  72.1 16.0 %collective-permute-start.19 = (bf16[1024,256]{1,0:T(8,128)(2,1)S(1)}, bf16[1024,256]{1,0:T(8,128)(2,1)S(1)}, u32[]{:S(2)}, u32[]{:S(2)}) collective-permute-start(bf16[1024,256]{1,0:T(8,128)(2,1)S(1)} %constant_dynamic-update-slice_fusion.7), channel_id=1, source_target_pairs={{0,1},{1,2},{2,3},{3,0},{4,5},{5,6},{6,7},{7,4},{8,9},{9,10},{10,1... | collective-permute-start | bytes 1572872 | tf_op jit(solution)/shard_map/ppermute | solution.py:320
  77.3 15.6 %collective-permute-start.12 = (bf16[1024,256]{1,0:T(8,128)(2,1)S(1)}, bf16[1024,256]{1,0:T(8,128)(2,1)S(1)}, u32[]{:S(2)}, u32[]{:S(2)}) collective-permute-start(bf16[1024,256]{1,0:T(8,128)(2,1)S(1)} %collective-permute-done.5), channel_id=1, source_target_pairs={{0,4},{1,5},{2,6},{3,7},{4,8},{5,9},{6,10},{7,11},{8,12},{9,13},{1... | collective-permute-start | bytes 1572872 | tf_op jit(solution)/shard_map/ppermute | solution.py:320
  79.9 13.0 %collective-permute-start.13 = (bf16[1024,256]{1,0:T(8,128)(2,1)S(1)}, bf16[1024,256]{1,0:T(8,128)(2,1)S(1)}, u32[]{:S(2)}, u32[]{:S(2)}) collective-permute-start(bf16[1024,256]{1,0:T(8,128)(2,1)S(1)} %collective-permute-done.9), channel_id=1, source_target_pairs={{0,12},{1,13},{2,14},{3,15},{4,0},{5,1},{6,2},{7,3},{8,4},{9,5},{1... | collective-permute-start | bytes 1572872 | tf_op jit(solution)/shard_map/ppermute | solution.py:320
  84.4 10.8 %collective-permute-start.14 = (bf16[1024,256]{1,0:T(8,128)(2,1)S(1)}, bf16[1024,256]{1,0:T(8,128)(2,1)S(1)}, u32[]{:S(2)}, u32[]{:S(2)}) collective-permute-start(bf16[1024,256]{1,0:T(8,128)(2,1)S(1)} %collective-permute-done.10), channel_id=1, source_target_pairs={{0,1},{1,2},{2,3},{3,0},{4,5},{5,6},{6,7},{7,4},{8,9},{9,10},{10,1... | collective-permute-start | bytes 1572872 | tf_op jit(solution)/shard_map/ppermute | solution.py:320
  84.5 10.7 %collective-permute-start.15 = (bf16[1024,256]{1,0:T(8,128)(2,1)S(1)}, bf16[1024,256]{1,0:T(8,128)(2,1)S(1)}, u32[]{:S(2)}, u32[]{:S(2)}) collective-permute-start(bf16[1024,256]{1,0:T(8,128)(2,1)S(1)} %collective-permute-done.11), channel_id=1, source_target_pairs={{0,3},{1,0},{2,1},{3,2},{4,7},{5,4},{6,5},{7,6},{8,11},{9,8},{10,9... | collective-permute-start | bytes 1572872 | tf_op jit(solution)/shard_map/ppermute | solution.py:320
  99.5 2.0 %collective-permute-start.20 = (bf16[1024,256]{1,0:T(8,128)(2,1)S(1)}, bf16[1024,256]{1,0:T(8,128)(2,1)S(1)}, u32[]{:S(2)}, u32[]{:S(2)}) collective-permute-start(bf16[1024,256]{1,0:T(8,128)(2,1)S(1)} %bitcast.86), channel_id=1, source_target_pairs={{0,16},{16,0},{32,48},{48,32},{64,80},{80,64},{96,112},{112,96},{1... | collective-permute-start | bytes 1572872 | tf_op jit(solution)/shard_map/ppermute | solution.py:354
  101.7 3.5 %collective-permute-start.21 = (bf16[3,1024,256]{2,1,0:T(8,128)(2,1)S(1)}, bf16[3,1024,256]{2,1,0:T(8,128)(2,1)S(1)}, u32[]{:S(2)}, u32[]{:S(2)}) collective-permute-start(bf16[3,1024,256]{2,1,0:T(8,128)(2,1)S(1)} %bitcast.85), channel_id=1, source_target_pairs={{0,16},{16,0},{32,48},{48,32},{64,80},{80,64},{96,112},{112,96},{1... | collective-permute-start | bytes 4718600 | tf_op jit(solution)/shard_map/ppermute | solution.py:354
  102.1 8.7 %collective-permute-start.22 = (bf16[512,256]{1,0:T(8,128)(2,1)S(1)}, bf16[512,256]{1,0:T(8,128)(2,1)S(1)}, u32[]{:S(2)}, u32[]{:S(2)}) collective-permute-start(bf16[512,256]{1,0:T(8,128)(2,1)S(1)} %get-tuple-element.86), channel_id=1, source_target_pairs={{0,32},{16,48},{32,64},{48,80},{64,96},{80,112},{96,0},{112,16},{1... | collective-permute-start | bytes 786440 | tf_op jit(solution)/shard_map/ppermute | solution.py:354
  103.3 10.0 %collective-permute-start.24 = (bf16[512,256]{1,0:T(8,128)(2,1)S(1)}, bf16[512,256]{1,0:T(8,128)(2,1)S(1)}, u32[]{:S(2)}, u32[]{:S(2)}) collective-permute-start(bf16[512,256]{1,0:T(8,128)(2,1)S(1)} %get-tuple-element.87), channel_id=1, source_target_pairs={{0,96},{16,112},{32,0},{48,16},{64,32},{80,48},{96,64},{112,80},{1... | collective-permute-start | bytes 786440 | tf_op jit(solution)/shard_map/ppermute | solution.py:354
  105.2 8.4 %copy-start.5 = (s32[1024]{0:T(1024)S(1)}, s32[1024]{0:T(1024)}, u32[]{:S(2)}) copy-start(s32[1024]{0:T(1024)} %param.12) | copy-start | bytes 12292
  105.2 8.4 %copy-start.7 = (bf16[256]{0:T(256)(128)(2,1)S(1)}, bf16[256]{0:T(256)(128)(2,1)}, u32[]{:S(2)}) copy-start(bf16[256]{0:T(256)(128)(2,1)} %param.19) | copy-start | bytes 1540
  105.6 22.3 %copy-start.6 = (bf16[256,256]{1,0:T(8,128)(2,1)S(1)}, bf16[256,256]{1,0:T(8,128)(2,1)}, u32[]{:S(2)}) copy-start(bf16[256,256]{1,0:T(8,128)(2,1)} %param.18) | copy-start | bytes 393220
  110.9 13.5 %collective-permute-start.23 = (bf16[1024,256]{1,0:T(8,128)(2,1)S(1)}, bf16[1024,256]{1,0:T(8,128)(2,1)S(1)}, u32[]{:S(2)}, u32[]{:S(2)}) collective-permute-start(bf16[1024,256]{1,0:T(8,128)(2,1)S(1)} %pad_maximum_fusion), channel_id=1, source_target_pairs={{0,32},{16,48},{32,64},{48,80},{64,96},{80,112},{96,0},{112,16},{1... | collective-permute-start | bytes 1572872 | tf_op jit(solution)/shard_map/ppermute | solution.py:354
  113.5 14.4 %collective-permute-start.25 = (bf16[1024,256]{1,0:T(8,128)(2,1)S(1)}, bf16[1024,256]{1,0:T(8,128)(2,1)S(1)}, u32[]{:S(2)}, u32[]{:S(2)}) collective-permute-start(bf16[1024,256]{1,0:T(8,128)(2,1)S(1)} %pad_maximum_fusion.1), channel_id=1, source_target_pairs={{0,96},{16,112},{32,0},{48,16},{64,32},{80,48},{96,64},{112,80},{1... | collective-permute-start | bytes 1572872 | tf_op jit(solution)/shard_map/ppermute | solution.py:354

commit v3 on v2

--- a/solution.py
+++ b/solution.py
@@ -60,9 +60,9 @@
     out_ref[...] = data.astype(jnp.bfloat16)
 
 
-def unpack_kernel(in_ref, a_ref, b_ref):
+def unpack_kernel(in_ref, out_ref):
     ins = in_ref.shape[0]
-    rows = a_ref.shape[0] + b_ref.shape[0]
+    rows = out_ref.shape[0]
     data = in_ref[...]
     drop = onehot(iota((128, ins), 1) == iota((128, ins), 0) * SLOT_ROWS + POS_ROW)
     pos_rows = jnp.dot(drop, data, preferred_element_type=jnp.float32).astype(jnp.bfloat16)
@@ -77,9 +77,7 @@
     low = lanes(pos_rows[:, 128:])
     target = 4 * (high - 1) + 2 * low + (iota((1, ins), 1) & 1)
     pick = onehot(iota((rows, ins), 0) == target)
-    owned = jnp.dot(pick, data, preferred_element_type=jnp.float32).astype(jnp.bfloat16)
-    a_ref[...] = owned[: rows // 2]
-    b_ref[...] = owned[rows // 2 :]
+    out_ref[...] = jnp.dot(pick, data, preferred_element_type=jnp.float32).astype(jnp.bfloat16)
 
 
 def ring_order(step):
@@ -95,12 +93,11 @@
     source = col >> 3
     order_z = ring_order(((source >> 2) - z) & 3)
     order_y = ring_order(((source & 3) - y) & 3)
-    half = (col >> 2) & 1
-    outer = jnp.where(half == 0, order_z, order_y)
-    inner = jnp.where(half == 0, order_y, order_z)
+    outer = jnp.where(core == 0, order_z, order_y)
+    inner = jnp.where(core == 0, order_y, order_z)
     stage = jnp.where((outer == 1) == (inner < 2), 1, 2)
     stage = jnp.where(outer == 3, 3, jnp.where(outer == 0, 0, stage))
-    tile = half * 16 + inner * 4 + (col & 3)
+    tile = inner * 8 + (col & 7)
     owner = row >> 3
     dx = ((owner >> 1) - x) & 3
     order_x = jnp.where(dx == 2, 0, jnp.where(dx == 1, 1, jnp.where(dx == 3, 2, 3)))
@@ -252,8 +249,15 @@
     )(*args, *state)
 
 
-def col_perm(dz, dy):
-    return [(z * 4 + y, (z + dz) % 4 * 4 + (y + dy) % 4) for z in range(4) for y in range(4)]
+def panel_perm(turn, step):
+    pairs = []
+    for row in range(8):
+        along_y = row % 2 == turn
+        for z in range(4):
+            for y in range(4):
+                to = z * 4 + (y + step) % 4 if along_y else (z + step) % 4 * 4 + y
+                pairs.append((row * 16 + z * 4 + y, row * 16 + to))
+    return pairs
 
 
 def row_perm(dx, flip=0):
@@ -291,12 +295,11 @@
         tiled=True,
     )
     half = rows // 2
-    quarter = half // 2
-    a0, b0 = pl.pallas_call(
+    owned = pl.pallas_call(
         unpack_kernel,
-        out_shape=(jax.ShapeDtypeStruct((half, width), jnp.bfloat16),) * 2,
+        out_shape=jax.ShapeDtypeStruct((rows, width), jnp.bfloat16),
         in_specs=[vmem],
-        out_specs=(vmem, vmem),
+        out_specs=vmem,
         compiler_params=big,
         name="unpack",
     )(incoming.reshape(devices * SLOT_ROWS, width))
@@ -316,34 +319,25 @@
     start = start.reshape(LANES)
     weights = tile_values.reshape(slots, tile, tile)
 
-    def send(v, dz, dy):
-        return lax.ppermute(v, "col", col_perm(dz, dy))
+    def send(v, turn, step):
+        return lax.ppermute(v, ("row", "col"), panel_perm(turn, step))
 
     def cat(*parts):
         return jnp.concatenate(parts, axis=0)
 
-    ap, am = send(a0, 0, 1), send(a0, 0, -1)
-    bp, bm = send(b0, 1, 0), send(b0, -1, 0)
-    bp, bm, code, start = lax.optimization_barrier((bp, bm, code, start))
-    a_far = (send(ap[:quarter], 0, 1), send(am[quarter:], 0, -1))
-    b_far = (send(bp[:quarter], 1, 0), send(bm[quarter:], -1, 0))
-    ap, b_far = lax.optimization_barrier((ap, b_far))
-    bp, a_far = lax.optimization_barrier((bp, a_far))
-    a_lo, b_lo = cat(a0, ap), cat(b0, bp)
-    a_hi, b_hi = cat(am, *a_far), cat(bm, *b_far)
+    plus, minus = send(owned, 0, 1), send(owned, 0, -1)
+    plus, minus, code, start = lax.optimization_barrier((plus, minus, code, start))
+    hi = cat(minus, send(plus[:half], 0, 1), send(minus[half:], 0, -1))
+    hi, plus = lax.optimization_barrier((hi, plus))
+    lo = cat(owned, plus)
     lists = (code, start, weights)
-    a_lo_p, a_hi_m = send(a_lo, 1, 0), send(a_hi, -1, 0)
-    b_lo_p, b_hi_m = send(b_lo, 0, 1), send(b_hi, 0, -1)
-    state = run_tiles(0, *lists, [a_lo, a_hi, b_lo, b_hi])
-    a_lo, a_hi, b_lo, b_hi, *state = lax.optimization_barrier((a_lo, a_hi, b_lo, b_hi, *state))
-    a_hi_p, a_lo_m = send(a_hi, 1, 0), send(a_lo, -1, 0)
-    b_hi_p, b_lo_m = send(b_hi, 0, 1), send(b_lo, 0, -1)
-    state = run_tiles(1, *lists, [a_lo_p, a_hi_m, b_lo_p, b_hi_m], state)
-    a_lo_p, a_hi_m, b_lo_p, b_hi_m, *state = lax.optimization_barrier(
-        (a_lo_p, a_hi_m, b_lo_p, b_hi_m, *state)
-    )
-    far = [send(a_lo_p, 1, 0), send(a_hi_m, -1, 0), send(b_lo_p, 0, 1), send(b_hi_m, 0, -1)]
-    state = run_tiles(2, *lists, [a_lo_m, a_hi_p, b_lo_m, b_hi_p], state)
+    lo_p, hi_m = send(lo, 1, 1), send(hi, 1, -1)
+    hi_p, lo_m = send(hi, 1, 1), send(lo, 1, -1)
+    state = run_tiles(0, *lists, [lo, hi])
+    lo_p, hi_m, *state = lax.optimization_barrier((lo_p, hi_m, *state))
+    far = [send(lo_p, 1, 1), send(hi_m, 1, -1)]
+    state = run_tiles(1, *lists, [lo_p, hi_m], state)
+    state = run_tiles(2, *lists, [lo_m, hi_p], state)
     *_, other_far, mine_far, other_rest, mine_rest = run_tiles(
         3, *lists, far, state, ((0, 8), (8, 8), (16, 24), (40, 24))
     )
@@ -365,7 +359,7 @@
     summed = both[2] + over(to_plus, 1).astype(f32) + over(to_minus, -1).astype(f32)
 
     neighbor_mean = (summed / degree.astype(f32)[:, None]).astype(jnp.bfloat16)
-    total = jnp.dot(cat(a0, b0), w_self, preferred_element_type=f32)
+    total = jnp.dot(owned, w_self, preferred_element_type=f32)
     total = total + jnp.dot(neighbor_mean, w_neigh, preferred_element_type=f32)
     total = total + bias.astype(f32)[None, :]
     return jnp.maximum(total, f32(0.0)).astype(jnp.bfloat16)

time: 130 us -> 129 us (level)
  the two profiles are of different devices: /device:TPU:6 before, /device:TPU:126 now
where the time goes in v3:
time: 129 us
  waiting for transfers between devices  55.5 us (43%)
  blocking collectives  23 us (18%)
  starting transfers between devices  22.7 us (18%)
  Pallas kernels  22.1 us (17%)
  local copies, waits for them, and re-layouts  2.06 us (2%)
  matrix products  1.58 us (1%)
    ppermute x10, waiting for transfers between devices, send(): return lax.ppermute(v, ('row', 'col'), panel_perm(turn, step))  33.9 us
    all_to_all x1, blocking collectives, per_device(): lax.all_to_all(outgoing.reshape(devices, SLOT_ROWS, width), ('row', 'col'...  23 us
    ppermute x6, waiting for transfers between devices, over(): return lax.ppermute(v, 'row', row_perm(dx, flip))  21.6 us
    pallas_call x4, Pallas kernels, run_tiles(): pl.pallas_call(functools.partial(tiles_kernel, stage, n, outs), out_shape...  15.4 us
    ppermute x10, starting transfers between devices, send(): return lax.ppermute(v, ('row', 'col'), panel_perm(turn, step))  12.7 us
    ppermute x6, starting transfers between devices, over(): return lax.ppermute(v, 'row', row_perm(dx, flip))  9.95 us
    pallas_call x1, Pallas kernels, per_device(): pl.pallas_call(pack_kernel, out_shape=jax.ShapeDtypeStruct((devices * SLO...  2.74 us
  transfers between devices with their start and end apart: 16, of which 13 were waited for; matrix products, arithmetic and copies ran while one was open for 1% of the time, Pallas kernels for 11%

profile of v3, /device:TPU:126, one launch (start us, length us, event | category | flops | bytes accessed | tf_op | source)
XLA Modules:
  0.0 128.9 jit_solution(18390900968313790182)
XLA Ops:
  0.0 1.1 copy-done.1
  1.1 0.7 copy-done.4
  1.8 2.7 %pack.1 = bf16[2048,256]{1,0:T(8,128)(2,1)S(1)} custom-call(s32[1,512]{1,0:T(1,128)S(1)} %bitcast.69, bf16[1024,256]{1,0:T(8,128)(2,1)S(1)} %copy-done.1), custom_call_target="tpu_custom_call" | custom-call | tf_op jit(solution)/shard_map/pack/pallas_call | solution.py:282
  4.5 0.0 copy-start.2
  4.5 0.0 copy-start.3
  4.5 23.0 %all_to_all.5 = bf16[128,16,256]{2,1,0:T(8,128)(2,1)S(1)} all-to-all(bf16[128,16,256]{2,1,0:T(8,128)(2,1)S(1)} %bitcast.56), channel_id=1, replica_groups=mesh['row'=8,'col'=16] {'row','col'}, dimensions={0} | all-to-all | bytes 2097152 | tf_op jit(solution)/shard_map/all_to_all | solution.py:290
  27.6 2.1 %unpack.1 = bf16[1024,256]{1,0:T(8,128)(2,1)S(1)} custom-call(bf16[2048,256]{1,0:T(8,128)(2,1)S(1)} %bitcast.55), custom_call_target="tpu_custom_call" | custom-call | tf_op jit(solution)/shard_map/unpack/pallas_call | solution.py:298
  29.6 1.7 %collective-permute-start = (bf16[1024,256]{1,0:T(8,128)(2,1)S(1)}, bf16[1024,256]{1,0:T(8,128)(2,1)S(1)}, u32[]{:S(2)}, u32[]{:S(2)}) collective-permute-start(bf16[1024,256]{1,0:T(8,128)(2,1)S(1)} %unpack.1), channel_id=1, source_target_pairs={{0,1},{1,2},{2,3},{3,0},{4,5},{5,6},{6,7},{7,4},{8,9},{9,10},{10,1... | collective-permute-start | bytes 1572872 | tf_op jit(solution)/shard_map/ppermute | solution.py:323
  31.4 0.4 collective-permute-start.1
  32.4 0.1 pad_add_fusion.where_ref
  32.5 1.9 %plan.1 = (s32[1,1024]{1,0:T(1,128)S(1)}, s32[1,384]{1,0:T(1,128)S(1)}) custom-call(s32[4]{0:T(128)S(1)} %pad_add_fusion.where_ref, s32[1]{0:T(128)} %bitcast.52.count_ref, s32[1,704]{1,0:T(1,128)S(1)} %bitcast.67, s32[1,704]{1,0:T(1,128)S(1)} %bitcast.68), custom_call_target="tpu_custom_call" | custom-call | tf_op jit(solution)/shard_map/plan/pallas_call | solution.py:307
  34.4 4.5 %collective-permute-done = bf16[1024,256]{1,0:T(8,128)(2,1)S(1)} collective-permute-done((bf16[1024,256]{1,0:T(8,128)(2,1)S(1)}, bf16[1024,256]{1,0:T(8,128)(2,1)S(1)}, u32[]{:S(2)}, u32[]{:S(2)}) %collective-permute-start) | collective-permute-done | bytes 524320 | tf_op jit(solution)/shard_map/ppermute | solution.py:323
  38.9 2.9 %collective-permute-done.1 = bf16[1024,256]{1,0:T(8,128)(2,1)S(1)} collective-permute-done((bf16[1024,256]{1,0:T(8,128)(2,1)S(1)}, bf16[1024,256]{1,0:T(8,128)(2,1)S(1)}, u32[]{:S(2)}, u32[]{:S(2)}) %collective-permute-start.1) | collective-permute-done | bytes 524320 | tf_op jit(solution)/shard_map/ppermute | solution.py:323
  41.8 0.1 collective-permute-start.2
  41.9 2.1 %collective-permute-start.3 = (bf16[512,256]{1,0:T(8,128)(2,1)S(1)}, bf16[512,256]{1,0:T(8,128)(2,1)S(1)}, u32[]{:S(2)}, u32[]{:S(2)}) collective-permute-start(bf16[512,256]{1,0:T(8,128)(2,1)S(1)} %slice.48), channel_id=1, source_target_pairs={{0,3},{1,0},{2,1},{3,2},{4,7},{5,4},{6,5},{7,6},{8,11},{9,8},{10,9... | collective-permute-start | bytes 786440 | tf_op jit(solution)/shard_map/ppermute | solution.py:323
  44.0 4.3 %collective-permute-done.2 = bf16[512,256]{1,0:T(8,128)(2,1)S(1)} collective-permute-done((bf16[512,256]{1,0:T(8,128)(2,1)S(1)}, bf16[512,256]{1,0:T(8,128)(2,1)S(1)}, u32[]{:S(2)}, u32[]{:S(2)}) %collective-permute-start.2) | collective-permute-done | bytes 262176 | tf_op jit(solution)/shard_map/ppermute | solution.py:323
  48.2 1.3 %collective-permute-done.3 = bf16[512,256]{1,0:T(8,128)(2,1)S(1)} collective-permute-done((bf16[512,256]{1,0:T(8,128)(2,1)S(1)}, bf16[512,256]{1,0:T(8,128)(2,1)S(1)}, u32[]{:S(2)}, u32[]{:S(2)}) %collective-permute-start.3) | collective-permute-done | bytes 262176 | tf_op jit(solution)/shard_map/ppermute | solution.py:323
  49.5 0.1 pad_maximum_fusion
  49.6 0.1 pad_maximum_fusion.1
  49.7 3.2 %collective-permute-start.4 = (bf16[2048,256]{1,0:T(8,128)(2,1)S(1)}, bf16[2048,256]{1,0:T(8,128)(2,1)S(1)}, u32[]{:S(2)}, u32[]{:S(2)}) collective-permute-start(bf16[2048,256]{1,0:T(8,128)(2,1)S(1)} %pad_maximum_fusion.1), channel_id=1, source_target_pairs={{0,4},{1,5},{2,6},{3,7},{4,8},{5,9},{6,10},{7,11},{8,12},{9,13},{1... | collective-permute-start | bytes 3145736 | tf_op jit(solution)/shard_map/ppermute | solution.py:323
  52.9 0.6 collective-permute-start.8
  53.5 2.7 %collective-permute-start.9 = (bf16[2048,256]{1,0:T(8,128)(2,1)S(1)}, bf16[2048,256]{1,0:T(8,128)(2,1)S(1)}, u32[]{:S(2)}, u32[]{:S(2)}) collective-permute-start(bf16[2048,256]{1,0:T(8,128)(2,1)S(1)} %pad_maximum_fusion), channel_id=1, source_target_pairs={{0,4},{1,5},{2,6},{3,7},{4,8},{5,9},{6,10},{7,11},{8,12},{9,13},{1... | collective-permute-start | bytes 3145736 | tf_op jit(solution)/shard_map/ppermute | solution.py:323
  56.2 5.4 %tiles_0.1 = (f32[64,128,256]{2,1,0:T(8,128)S(1)}, bf16[8,16,128,128]{3,2,1,0:T(8,128)(2,1)S(1)}) custom-call(s32[1024]{0:T(1024)S(1)} %bitcast.63, s32[384]{0:T(512)S(1)} %reduce.refs_1_, bf16[704,128,128]{2,1,0:T(8,128)(2,1)} %bitcast.72, bf16[16,128,256]{2,1,0:T(8,128)(2,1)S(1)} %bitcast.54, bf16[16,128,256]{2,1,0:T(8,128)(2,1)S(1)} %bitcast.53), custom_call_target="tpu_custom_call" | custom-call | flops 1476395008 | bytes 5767168 | tf_op jit(solution)/shard_map/tiles_0/pallas_call | solution.py:233
  61.6 3.6 %collective-permute-done.4 = bf16[2048,256]{1,0:T(8,128)(2,1)S(1)} collective-permute-done((bf16[2048,256]{1,0:T(8,128)(2,1)S(1)}, bf16[2048,256]{1,0:T(8,128)(2,1)S(1)}, u32[]{:S(2)}, u32[]{:S(2)}) %collective-permute-start.4) | collective-permute-done | bytes 1048608 | tf_op jit(solution)/shard_map/ppermute | solution.py:323
  65.2 3.7 %collective-permute-done.5 = bf16[2048,256]{1,0:T(8,128)(2,1)S(1)} collective-permute-done((bf16[2048,256]{1,0:T(8,128)(2,1)S(1)}, bf16[2048,256]{1,0:T(8,128)(2,1)S(1)}, u32[]{:S(2)}, u32[]{:S(2)}) %collective-permute-start.5) | collective-permute-done | bytes 1048608 | tf_op jit(solution)/shard_map/ppermute | solution.py:323
  68.9 2.0 %collective-permute-start.7 = (bf16[2048,256]{1,0:T(8,128)(2,1)S(1)}, bf16[2048,256]{1,0:T(8,128)(2,1)S(1)}, u32[]{:S(2)}, u32[]{:S(2)}) collective-permute-start(bf16[2048,256]{1,0:T(8,128)(2,1)S(1)} %collective-permute-done.5), channel_id=1, source_target_pairs={{0,12},{1,13},{2,14},{3,15},{4,0},{5,1},{6,2},{7,3},{8,4},{9,5},{1... | collective-permute-start | bytes 3145736 | tf_op jit(solution)/shard_map/ppermute | solution.py:323
  70.9 3.8 %tiles_1.1 = (f32[64,128,256]{2,1,0:T(8,128)S(1)}, bf16[8,16,128,128]{3,2,1,0:T(8,128)(2,1)S(1)}) custom-call(s32[1024]{0:T(1024)S(1)} %bitcast.64, s32[384]{0:T(512)S(1)} %reduce.refs_1_, bf16[704,128,128]{2,1,0:T(8,128)(2,1)} %bitcast.73, bf16[16,128,256]{2,1,0:T(8,128)(2,1)S(1)} %bitcast.57, ...), custom_call_target="tpu_custom_call", output_to_operand_aliasing={{0}: (5, {}), {1}: (6, {})} | custom-call | flops 1476395008 | bytes 5767168 | tf_op jit(solution)/shard_map/tiles_1/pallas_call | solution.py:233
  74.8 5.4 %collective-permute-done.8 = bf16[2048,256]{1,0:T(8,128)(2,1)S(1)} collective-permute-done((bf16[2048,256]{1,0:T(8,128)(2,1)S(1)}, bf16[2048,256]{1,0:T(8,128)(2,1)S(1)}, u32[]{:S(2)}, u32[]{:S(2)}) %collective-permute-start.8) | collective-permute-done | bytes 1048608 | tf_op jit(solution)/shard_map/ppermute | solution.py:323
  80.1 2.9 %tiles_2.1 = (f32[64,128,256]{2,1,0:T(8,128)S(1)}, bf16[8,16,128,128]{3,2,1,0:T(8,128)(2,1)S(1)}) custom-call(s32[1024]{0:T(1024)S(1)} %bitcast.65, s32[384]{0:T(512)S(1)} %reduce.refs_1_, bf16[704,128,128]{2,1,0:T(8,128)(2,1)} %bitcast.74, bf16[16,128,256]{2,1,0:T(8,128)(2,1)S(1)} %bitcast.61, ...), custom_call_target="tpu_custom_call", output_to_operand_aliasing={{0}: (5, {}), {1}: (6, {})} | custom-call | flops 1476395008 | bytes 5767168 | tf_op jit(solution)/shard_map/tiles_2/pallas_call | solution.py:233
  83.0 4.6 %collective-permute-done.6 = bf16[2048,256]{1,0:T(8,128)(2,1)S(1)} collective-permute-done((bf16[2048,256]{1,0:T(8,128)(2,1)S(1)}, bf16[2048,256]{1,0:T(8,128)(2,1)S(1)}, u32[]{:S(2)}, u32[]{:S(2)}) %collective-permute-start.6) | collective-permute-done | bytes 1048608 | tf_op jit(solution)/shard_map/ppermute | solution.py:323
  87.7 3.7 %collective-permute-done.7 = bf16[2048,256]{1,0:T(8,128)(2,1)S(1)} collective-permute-done((bf16[2048,256]{1,0:T(8,128)(2,1)S(1)}, bf16[2048,256]{1,0:T(8,128)(2,1)S(1)}, u32[]{:S(2)}, u32[]{:S(2)}) %collective-permute-start.7) | collective-permute-done | bytes 1048608 | tf_op jit(solution)/shard_map/ppermute | solution.py:323
  91.4 3.2 %tiles_3.1 = (f32[64,128,256]{2,1,0:T(8,128)S(1)}, bf16[8,16,128,128]{3,2,1,0:T(8,128)(2,1)S(1)}, bf16[8,128,256]{2,1,0:T(8,128)(2,1)S(1)}, bf16[8,128,256]{2,1,...) custom-call(s32[1024]{0:T(1024)S(1)} %bitcast.66, ...), custom_call_target="tpu_custom_call", output_to_operand_aliasing={{0}: (5, {}), {1}: (6, {})} | custom-call | flops 1476395008 | bytes 5767168 | tf_op jit(solution)/shard_map/tiles_3/pallas_call | solution.py:233
  94.6 0.1 collective-permute-start.10
  94.7 1.9 %collective-permute-done.10 = bf16[1024,256]{1,0:T(8,128)(2,1)S(1)} collective-permute-done((bf16[1024,256]{1,0:T(8,128)(2,1)S(1)}, bf16[1024,256]{1,0:T(8,128)(2,1)S(1)}, u32[]{:S(2)}, u32[]{:S(2)}) %collective-permute-start.10) | collective-permute-done | bytes 524320 | tf_op jit(solution)/shard_map/ppermute | solution.py:348
  96.6 0.2 fusion.6
  96.8 0.2 collective-permute-start.11
  97.0 0.1 fusion.12
  97.2 5.8 %collective-permute-start.12 = (bf16[512,256]{1,0:T(8,128)(2,1)S(1)}, bf16[512,256]{1,0:T(8,128)(2,1)S(1)}, u32[]{:S(2)}, u32[]{:S(2)}) collective-permute-start(bf16[512,256]{1,0:T(8,128)(2,1)S(1)} %get-tuple-element.58), channel_id=1, source_target_pairs={{0,32},{16,48},{32,64},{48,80},{64,96},{80,112},{96,0},{112,16},{1... | collective-permute-start | bytes 786440 | tf_op jit(solution)/shard_map/ppermute | solution.py:348
  103.0 0.3 convert_add_fusion.1
  103.4 5.7 %collective-permute-done.12 = bf16[512,256]{1,0:T(8,128)(2,1)S(1)} collective-permute-done((bf16[512,256]{1,0:T(8,128)(2,1)S(1)}, bf16[512,256]{1,0:T(8,128)(2,1)S(1)}, u32[]{:S(2)}, u32[]{:S(2)}) %collective-permute-start.12) | collective-permute-done | bytes 262176 | tf_op jit(solution)/shard_map/ppermute | solution.py:348
  109.1 0.1 fusion.10
  109.3 3.8 %collective-permute-start.13 = (bf16[1024,256]{1,0:T(8,128)(2,1)S(1)}, bf16[1024,256]{1,0:T(8,128)(2,1)S(1)}, u32[]{:S(2)}, u32[]{:S(2)}) collective-permute-start(bf16[1024,256]{1,0:T(8,128)(2,1)S(1)} %pad_maximum_fusion.2), channel_id=1, source_target_pairs={{0,32},{16,48},{32,64},{48,80},{64,96},{80,112},{96,0},{112,16},{1... | collective-permute-start | bytes 1572872 | tf_op jit(solution)/shard_map/ppermute | solution.py:348
  113.1 0.1 fusion.9
  113.2 0.1 collective-permute-start.15
  113.3 0.3 fusion.14
  113.6 10.3 %collective-permute-done.13 = bf16[1024,256]{1,0:T(8,128)(2,1)S(1)} collective-permute-done((bf16[1024,256]{1,0:T(8,128)(2,1)S(1)}, bf16[1024,256]{1,0:T(8,128)(2,1)S(1)}, u32[]{:S(2)}, u32[]{:S(2)}) %collective-permute-start.13) | collective-permute-done | bytes 524320 | tf_op jit(solution)/shard_map/ppermute | solution.py:348
  123.9 3.6 %collective-permute-done.15 = bf16[1024,256]{1,0:T(8,128)(2,1)S(1)} collective-permute-done((bf16[1024,256]{1,0:T(8,128)(2,1)S(1)}, bf16[1024,256]{1,0:T(8,128)(2,1)S(1)}, u32[]{:S(2)}, u32[]{:S(2)}) %collective-permute-start.15) | collective-permute-done | bytes 524320 | tf_op jit(solution)/shard_map/ppermute | solution.py:348
  127.6 1.3 fusion.2
  (28 shorter events, 0.3 us)
Async XLA Ops:
  0.0 113.3 %copy-start = (bf16[256,256]{1,0:T(8,128)(2,1)S(1)}, bf16[256,256]{1,0:T(8,128)(2,1)}, u32[]{:S(2)}) copy-start(bf16[256,256]{1,0:T(8,128)(2,1)} %param.17) | copy-start | bytes 393220
  0.0 1.1 copy-start.1
  1.1 0.7 copy-start.4
  4.5 28.0 %copy-start.2 = (s32[1,1,704]{2,1,0:T(1,128)S(1)}, s32[1,1,704]{2,1,0:T(1,128)}, u32[]{:S(2)}) copy-start(s32[1,1,704]{2,1,0:T(1,128)} %param.13) | copy-start | bytes 8452
  4.5 28.0 %copy-start.3 = (s32[1,1,704]{2,1,0:T(1,128)S(1)}, s32[1,1,704]{2,1,0:T(1,128)}, u32[]{:S(2)}) copy-start(s32[1,1,704]{2,1,0:T(1,128)} %param.14) | copy-start | bytes 8452
  29.6 9.2 %collective-permute-start = (bf16[1024,256]{1,0:T(8,128)(2,1)S(1)}, bf16[1024,256]{1,0:T(8,128)(2,1)S(1)}, u32[]{:S(2)}, u32[]{:S(2)}) collective-permute-start(bf16[1024,256]{1,0:T(8,128)(2,1)S(1)} %unpack.1), channel_id=1, source_target_pairs={{0,1},{1,2},{2,3},{3,0},{4,5},{5,6},{6,7},{7,4},{8,9},{9,10},{10,1... | collective-permute-start | bytes 1572872 | tf_op jit(solution)/shard_map/ppermute | solution.py:323
  31.4 10.4 %collective-permute-start.1 = (bf16[1024,256]{1,0:T(8,128)(2,1)S(1)}, bf16[1024,256]{1,0:T(8,128)(2,1)S(1)}, u32[]{:S(2)}, u32[]{:S(2)}) collective-permute-start(bf16[1024,256]{1,0:T(8,128)(2,1)S(1)} %unpack.1), channel_id=1, source_target_pairs={{0,3},{1,0},{2,1},{3,2},{4,7},{5,4},{6,5},{7,6},{8,11},{9,8},{10,9... | collective-permute-start | bytes 1572872 | tf_op jit(solution)/shard_map/ppermute | solution.py:323
  41.8 6.4 %collective-permute-start.2 = (bf16[512,256]{1,0:T(8,128)(2,1)S(1)}, bf16[512,256]{1,0:T(8,128)(2,1)S(1)}, u32[]{:S(2)}, u32[]{:S(2)}) collective-permute-start(bf16[512,256]{1,0:T(8,128)(2,1)S(1)} %slice.47), channel_id=1, source_target_pairs={{0,1},{1,2},{2,3},{3,0},{4,5},{5,6},{6,7},{7,4},{8,9},{9,10},{10,1... | collective-permute-start | bytes 786440 | tf_op jit(solution)/shard_map/ppermute | solution.py:323
  41.9 7.7 %collective-permute-start.3 = (bf16[512,256]{1,0:T(8,128)(2,1)S(1)}, bf16[512,256]{1,0:T(8,128)(2,1)S(1)}, u32[]{:S(2)}, u32[]{:S(2)}) collective-permute-start(bf16[512,256]{1,0:T(8,128)(2,1)S(1)} %slice.48), channel_id=1, source_target_pairs={{0,3},{1,0},{2,1},{3,2},{4,7},{5,4},{6,5},{7,6},{8,11},{9,8},{10,9... | collective-permute-start | bytes 786440 | tf_op jit(solution)/shard_map/ppermute | solution.py:323
  49.7 15.5 %collective-permute-start.4 = (bf16[2048,256]{1,0:T(8,128)(2,1)S(1)}, bf16[2048,256]{1,0:T(8,128)(2,1)S(1)}, u32[]{:S(2)}, u32[]{:S(2)}) collective-permute-start(bf16[2048,256]{1,0:T(8,128)(2,1)S(1)} %pad_maximum_fusion.1), channel_id=1, source_target_pairs={{0,4},{1,5},{2,6},{3,7},{4,8},{5,9},{6,10},{7,11},{8,12},{9,13},{1... | collective-permute-start | bytes 3145736 | tf_op jit(solution)/shard_map/ppermute | solution.py:323
  52.9 16.0 %collective-permute-start.5 = (bf16[2048,256]{1,0:T(8,128)(2,1)S(1)}, bf16[2048,256]{1,0:T(8,128)(2,1)S(1)}, u32[]{:S(2)}, u32[]{:S(2)}) collective-permute-start(bf16[2048,256]{1,0:T(8,128)(2,1)S(1)} %pad_maximum_fusion), channel_id=1, source_target_pairs={{0,12},{1,13},{2,14},{3,15},{4,0},{5,1},{6,2},{7,3},{8,4},{9,5},{1... | collective-permute-start | bytes 3145736 | tf_op jit(solution)/shard_map/ppermute | solution.py:323
  52.9 27.2 %collective-permute-start.8 = (bf16[2048,256]{1,0:T(8,128)(2,1)S(1)}, bf16[2048,256]{1,0:T(8,128)(2,1)S(1)}, u32[]{:S(2)}, u32[]{:S(2)}) collective-permute-start(bf16[2048,256]{1,0:T(8,128)(2,1)S(1)} %pad_maximum_fusion.1), channel_id=1, source_target_pairs={{0,12},{1,13},{2,14},{3,15},{4,0},{5,1},{6,2},{7,3},{8,4},{9,5},{1... | collective-permute-start | bytes 3145736 | tf_op jit(solution)/shard_map/ppermute | solution.py:323
  53.5 26.6 %collective-permute-start.9 = (bf16[2048,256]{1,0:T(8,128)(2,1)S(1)}, bf16[2048,256]{1,0:T(8,128)(2,1)S(1)}, u32[]{:S(2)}, u32[]{:S(2)}) collective-permute-start(bf16[2048,256]{1,0:T(8,128)(2,1)S(1)} %pad_maximum_fusion), channel_id=1, source_target_pairs={{0,4},{1,5},{2,6},{3,7},{4,8},{5,9},{6,10},{7,11},{8,12},{9,13},{1... | collective-permute-start | bytes 3145736 | tf_op jit(solution)/shard_map/ppermute | solution.py:323
  68.9 18.8 %collective-permute-start.6 = (bf16[2048,256]{1,0:T(8,128)(2,1)S(1)}, bf16[2048,256]{1,0:T(8,128)(2,1)S(1)}, u32[]{:S(2)}, u32[]{:S(2)}) collective-permute-start(bf16[2048,256]{1,0:T(8,128)(2,1)S(1)} %collective-permute-done.4), channel_id=1, source_target_pairs={{0,4},{1,5},{2,6},{3,7},{4,8},{5,9},{6,10},{7,11},{8,12},{9,13},{1... | collective-permute-start | bytes 3145736 | tf_op jit(solution)/shard_map/ppermute | solution.py:323
  68.9 22.5 %collective-permute-start.7 = (bf16[2048,256]{1,0:T(8,128)(2,1)S(1)}, bf16[2048,256]{1,0:T(8,128)(2,1)S(1)}, u32[]{:S(2)}, u32[]{:S(2)}) collective-permute-start(bf16[2048,256]{1,0:T(8,128)(2,1)S(1)} %collective-permute-done.5), channel_id=1, source_target_pairs={{0,12},{1,13},{2,14},{3,15},{4,0},{5,1},{6,2},{7,3},{8,4},{9,5},{1... | collective-permute-start | bytes 3145736 | tf_op jit(solution)/shard_map/ppermute | solution.py:323
  94.6 2.0 %collective-permute-start.10 = (bf16[1024,256]{1,0:T(8,128)(2,1)S(1)}, bf16[1024,256]{1,0:T(8,128)(2,1)S(1)}, u32[]{:S(2)}, u32[]{:S(2)}) collective-permute-start(bf16[1024,256]{1,0:T(8,128)(2,1)S(1)} %bitcast.71), channel_id=1, source_target_pairs={{0,16},{16,0},{32,48},{48,32},{64,80},{80,64},{96,112},{112,96},{1... | collective-permute-start | bytes 1572872 | tf_op jit(solution)/shard_map/ppermute | solution.py:348
  96.8 6.2 %collective-permute-start.11 = (bf16[3,1024,256]{2,1,0:T(8,128)(2,1)S(1)}, bf16[3,1024,256]{2,1,0:T(8,128)(2,1)S(1)}, u32[]{:S(2)}, u32[]{:S(2)}) collective-permute-start(bf16[3,1024,256]{2,1,0:T(8,128)(2,1)S(1)} %bitcast.70), channel_id=1, source_target_pairs={{0,16},{16,0},{32,48},{48,32},{64,80},{80,64},{96,112},{112,96},{1... | collective-permute-start | bytes 4718600 | tf_op jit(solution)/shard_map/ppermute | solution.py:348
  97.2 11.9 %collective-permute-start.12 = (bf16[512,256]{1,0:T(8,128)(2,1)S(1)}, bf16[512,256]{1,0:T(8,128)(2,1)S(1)}, u32[]{:S(2)}, u32[]{:S(2)}) collective-permute-start(bf16[512,256]{1,0:T(8,128)(2,1)S(1)} %get-tuple-element.58), channel_id=1, source_target_pairs={{0,32},{16,48},{32,64},{48,80},{64,96},{80,112},{96,0},{112,16},{1... | collective-permute-start | bytes 786440 | tf_op jit(solution)/shard_map/ppermute | solution.py:348
  103.0 10.0 %collective-permute-start.14 = (bf16[512,256]{1,0:T(8,128)(2,1)S(1)}, bf16[512,256]{1,0:T(8,128)(2,1)S(1)}, u32[]{:S(2)}, u32[]{:S(2)}) collective-permute-start(bf16[512,256]{1,0:T(8,128)(2,1)S(1)} %get-tuple-element.59), channel_id=1, source_target_pairs={{0,96},{16,112},{32,0},{48,16},{64,32},{80,48},{96,64},{112,80},{1... | collective-permute-start | bytes 786440 | tf_op jit(solution)/shard_map/ppermute | solution.py:348
  109.2 4.1 %copy-start.5 = (s32[1024]{0:T(1024)S(1)}, s32[1024]{0:T(1024)}, u32[]{:S(2)}) copy-start(s32[1024]{0:T(1024)} %param.12) | copy-start | bytes 12292
  109.2 4.1 %copy-start.7 = (bf16[256]{0:T(256)(128)(2,1)S(1)}, bf16[256]{0:T(256)(128)(2,1)}, u32[]{:S(2)}) copy-start(bf16[256]{0:T(256)(128)(2,1)} %param.19) | copy-start | bytes 1540
  109.3 14.7 %collective-permute-start.13 = (bf16[1024,256]{1,0:T(8,128)(2,1)S(1)}, bf16[1024,256]{1,0:T(8,128)(2,1)S(1)}, u32[]{:S(2)}, u32[]{:S(2)}) collective-permute-start(bf16[1024,256]{1,0:T(8,128)(2,1)S(1)} %pad_maximum_fusion.2), channel_id=1, source_target_pairs={{0,32},{16,48},{32,64},{48,80},{64,96},{80,112},{96,0},{112,16},{1... | collective-permute-start | bytes 1572872 | tf_op jit(solution)/shard_map/ppermute | solution.py:348
  113.0 14.6 %copy-start.6 = (bf16[256,256]{1,0:T(8,128)(2,1)S(1)}, bf16[256,256]{1,0:T(8,128)(2,1)}, u32[]{:S(2)}) copy-start(bf16[256,256]{1,0:T(8,128)(2,1)} %param.18) | copy-start | bytes 393220
  113.2 14.4 %collective-permute-start.15 = (bf16[1024,256]{1,0:T(8,128)(2,1)S(1)}, bf16[1024,256]{1,0:T(8,128)(2,1)S(1)}, u32[]{:S(2)}, u32[]{:S(2)}) collective-permute-start(bf16[1024,256]{1,0:T(8,128)(2,1)S(1)} %pad_maximum_fusion.3), channel_id=1, source_target_pairs={{0,96},{16,112},{32,0},{48,16},{64,32},{80,48},{96,64},{112,80},{1... | collective-permute-start | bytes 1572872 | tf_op jit(solution)/shard_map/ppermute | solution.py:348

commit v4 on v3

--- a/solution.py
+++ b/solution.py
@@ -12,7 +12,8 @@
 PAIRS = 8
 BLOCK = 2 * PAIRS
 BUFS = 8
-LIST = 1024
+LIST = 1152
+STAGES = 5
 LANES = 384
 MB = 1 << 20
 VMEM_TILES = 30 * MB
@@ -29,25 +30,28 @@
 def pack_kernel(home_ref, table_ref, out_ref):
     rows = table_ref.shape[0]
     blocks = home_ref.shape[1]
-    parts = jnp.where(iota((16, blocks), 0) == 0, home_ref[...] >> 8, home_ref[...] & 255)
+    home = home_ref[...]
+    dest = home >> 9
+    dest_f = dest.astype(jnp.float32)
+    dest_col = jnp.broadcast_to(dest_f, (128, blocks)).T[:, :1]
+    before = (dest_col == dest_f) & (iota((blocks, blocks), 0) < iota((blocks, blocks), 1))
+    rank = jnp.sum(jnp.where(before, 1.0, 0.0), axis=0, keepdims=True).astype(jnp.int32)
+    line = iota((16, blocks), 0)
+    parts = jnp.where(line == 2, (home & 511) >> 1, home & 1)
+    parts = jnp.where(line == 0, dest, jnp.where(line == 1, rank, parts))
     twice = onehot(iota((blocks, rows), 0) == (iota((blocks, rows), 1) >> 1))
     parts = jnp.dot(
         parts.astype(jnp.float32).astype(jnp.bfloat16), twice, preferred_element_type=jnp.float32
     ).astype(jnp.int32)
-    home = (parts[:1] << 8) + parts[1:2]
-    dest = home >> 9
-    pos = home & 511
-    dest_f = dest.astype(jnp.float32)
-    dest_col = jnp.broadcast_to(dest_f, (128, rows)).T[:, :1]
-    before = (dest_col == dest_f) & (iota((rows, rows), 0) < iota((rows, rows), 1))
-    rank = jnp.sum(jnp.where(before, 1.0, 0.0), axis=0, keepdims=True).astype(jnp.int32)
+    dest = parts[:1]
+    rank = parts[1:2] * 2 + (iota((1, rows), 1) & 1)
     place = dest * SLOT_ROWS + rank
     outs = out_ref.shape[0]
     spread = onehot(iota((outs, rows), 0) == place)
     data = jnp.dot(spread, table_ref[...], preferred_element_type=jnp.float32)
     lane = iota((256, rows), 0)
-    high = jnp.broadcast_to(((pos >> 1) + 1).astype(jnp.float32), (256, rows))
-    low = jnp.broadcast_to((pos & 1).astype(jnp.float32), (256, rows))
+    high = jnp.broadcast_to((parts[2:3] + 1).astype(jnp.float32), (256, rows))
+    low = jnp.broadcast_to(parts[3:4].astype(jnp.float32), (256, rows))
     marks = jnp.where(lane == rank, high, jnp.where(lane == rank + 128, low, 0.0)).astype(
         jnp.bfloat16
     )
@@ -95,9 +99,9 @@
     order_y = ring_order(((source & 3) - y) & 3)
     outer = jnp.where(core == 0, order_z, order_y)
     inner = jnp.where(core == 0, order_y, order_z)
-    stage = jnp.where((outer == 1) == (inner < 2), 1, 2)
-    stage = jnp.where(outer == 3, 3, jnp.where(outer == 0, 0, stage))
-    tile = inner * 8 + (col & 7)
+    stage = jnp.where(outer == 0, 0, jnp.where(inner < 2, 1, 2) + jnp.where(outer == 3, 2, 0))
+    side = (inner & 1) * 8 + jnp.where(outer == 2, 16, 0)
+    tile = jnp.where(outer == 0, inner * 8, side) + (col & 7)
     owner = row >> 3
     dx = ((owner >> 1) - x) & 3
     order_x = jnp.where(dx == 2, 0, jnp.where(dx == 1, 1, jnp.where(dx == 3, 2, 3)))
@@ -153,7 +157,7 @@
     panel, wsem, psem = refs[k + 2 + len(outs) :]
     first = start_ref[64 * stage]
     last = start_ref[64 * stage + 64]
-    total = start_ref[256]
+    total = start_ref[64 * STAGES]
     ahead = BUFS - 1
 
     copies = []
@@ -328,18 +332,20 @@
     plus, minus = send(owned, 0, 1), send(owned, 0, -1)
     plus, minus, code, start = lax.optimization_barrier((plus, minus, code, start))
     hi = cat(minus, send(plus[:half], 0, 1), send(minus[half:], 0, -1))
-    hi, plus = lax.optimization_barrier((hi, plus))
     lo = cat(owned, plus)
     lists = (code, start, weights)
-    lo_p, hi_m = send(lo, 1, 1), send(hi, 1, -1)
-    hi_p, lo_m = send(hi, 1, 1), send(lo, 1, -1)
+    lo_p, lo_m = send(lo, 1, 1), send(lo, 1, -1)
+    hi_p, hi_m = send(hi, 1, 1), send(hi, 1, -1)
     state = run_tiles(0, *lists, [lo, hi])
-    lo_p, hi_m, *state = lax.optimization_barrier((lo_p, hi_m, *state))
-    far = [send(lo_p, 1, 1), send(hi_m, 1, -1)]
-    state = run_tiles(1, *lists, [lo_p, hi_m], state)
-    state = run_tiles(2, *lists, [lo_m, hi_p], state)
+    lo_p, lo_m, *state = lax.optimization_barrier((lo_p, lo_m, *state))
+    far_lo = [send(lo_p[:rows], 1, 1), send(lo_m[rows:], 1, -1)]
+    state = run_tiles(1, *lists, [lo_p, lo_m], state)
+    hi_p, hi_m, *state = lax.optimization_barrier((hi_p, hi_m, *state))
+    far_hi = [send(hi_p[:rows], 1, 1), send(hi_m[rows:], 1, -1)]
+    state = run_tiles(2, *lists, [hi_p, hi_m], state)
+    state = run_tiles(3, *lists, far_lo, state)
     *_, other_far, mine_far, other_rest, mine_rest = run_tiles(
-        3, *lists, far, state, ((0, 8), (8, 8), (16, 24), (40, 24))
+        4, *lists, far_hi, state, ((0, 8), (8, 8), (16, 24), (40, 24))
     )
 
     f32 = jnp.float32

time: 129 us -> 122 us (0.946)
  the two profiles are of different devices: /device:TPU:126 before, /device:TPU:6 now
where the time goes in v4:
time: 122 us; the launch traced here: 120 us
  waiting for transfers between devices  34.6 us (28%)
  blocking collectives  28.4 us (23%)
  starting transfers between devices  26 us (21%)
  Pallas kernels  25.5 us (21%)
  local copies, waits for them, and re-layouts  2.27 us (2%)
  matrix products  1.59 us (1%)
    all_to_all x1, blocking collectives, per_device(): lax.all_to_all(outgoing.reshape(devices, SLOT_ROWS, width), ('row', 'col'...  28.4 us
    ppermute x6, waiting for transfers between devices, over(): return lax.ppermute(v, 'row', row_perm(dx, flip))  22 us
    ppermute x12, starting transfers between devices, send(): return lax.ppermute(v, ('row', 'col'), panel_perm(turn, step))  20.2 us
    pallas_call x5, Pallas kernels, run_tiles(): pl.pallas_call(functools.partial(tiles_kernel, stage, n, outs), out_shape...  19 us
    ppermute x12, waiting for transfers between devices, send(): return lax.ppermute(v, ('row', 'col'), panel_perm(turn, step))  12.6 us
    ppermute x6, starting transfers between devices, over(): return lax.ppermute(v, 'row', row_perm(dx, flip))  5.76 us
    pallas_call x1, Pallas kernels, per_device(): pl.pallas_call(pack_kernel, out_shape=jax.ShapeDtypeStruct((devices * SLO...  2.54 us
  transfers between devices with their start and end apart: 18, of which 11 were waited for; matrix products, arithmetic and copies ran while one was open for 1% of the time, Pallas kernels for 15%

profile of v4, /device:TPU:6, one launch (start us, length us, event | category | flops | bytes accessed | tf_op | source)
XLA Modules:
  0.0 120.3 jit_solution(12353924368622824111)
XLA Ops:
  0.0 1.1 copy-done.1
  1.1 0.7 copy-done.4
  1.8 2.5 %pack.1 = bf16[2048,256]{1,0:T(8,128)(2,1)S(1)} custom-call(s32[1,512]{1,0:T(1,128)S(1)} %bitcast.68, bf16[1024,256]{1,0:T(8,128)(2,1)S(1)} %copy-done.1), custom_call_target="tpu_custom_call" | custom-call | tf_op jit(solution)/shard_map/pack/pallas_call | solution.py:286
  4.3 28.4 %all_to_all.5 = bf16[128,16,256]{2,1,0:T(8,128)(2,1)S(1)} all-to-all(bf16[128,16,256]{2,1,0:T(8,128)(2,1)S(1)} %bitcast.56), channel_id=1, replica_groups=mesh['row'=8,'col'=16] {'row','col'}, dimensions={0} | all-to-all | bytes 2097152 | tf_op jit(solution)/shard_map/all_to_all | solution.py:294
  32.7 2.1 %unpack.1 = bf16[1024,256]{1,0:T(8,128)(2,1)S(1)} custom-call(bf16[2048,256]{1,0:T(8,128)(2,1)S(1)} %bitcast.55), custom_call_target="tpu_custom_call" | custom-call | tf_op jit(solution)/shard_map/unpack/pallas_call | solution.py:302
  34.8 0.7 collective-permute-start
  35.5 2.6 %collective-permute-start.1 = (bf16[1024,256]{1,0:T(8,128)(2,1)S(1)}, bf16[1024,256]{1,0:T(8,128)(2,1)S(1)}, u32[]{:S(2)}, u32[]{:S(2)}) collective-permute-start(bf16[1024,256]{1,0:T(8,128)(2,1)S(1)} %unpack.1), channel_id=1, source_target_pairs={{0,3},{1,0},{2,1},{3,2},{4,7},{5,4},{6,5},{7,6},{8,11},{9,8},{10,9... | collective-permute-start | bytes 1572872 | tf_op jit(solution)/shard_map/ppermute | solution.py:327
  38.7 0.1 pad_add_fusion.where_ref
  38.8 1.9 %plan.1 = (s32[1,1152]{1,0:T(1,128)S(1)}, s32[1,384]{1,0:T(1,128)S(1)}) custom-call(s32[4]{0:T(128)S(1)} %pad_add_fusion.where_ref, s32[1]{0:T(128)} %bitcast.53.count_ref, s32[1,704]{1,0:T(1,128)S(1)} %bitcast.66, s32[1,704]{1,0:T(1,128)S(1)} %bitcast.67), custom_call_target="tpu_custom_call" | custom-call | tf_op jit(solution)/shard_map/plan/pallas_call | solution.py:311
  40.8 4.4 %collective-permute-done = bf16[1024,256]{1,0:T(8,128)(2,1)S(1)} collective-permute-done((bf16[1024,256]{1,0:T(8,128)(2,1)S(1)}, bf16[1024,256]{1,0:T(8,128)(2,1)S(1)}, u32[]{:S(2)}, u32[]{:S(2)}) %collective-permute-start) | collective-permute-done | bytes 524320 | tf_op jit(solution)/shard_map/ppermute | solution.py:327
  45.3 0.1 collective-permute-start.2
  45.4 3.3 %collective-permute-start.3 = (bf16[512,256]{1,0:T(8,128)(2,1)S(1)}, bf16[512,256]{1,0:T(8,128)(2,1)S(1)}, u32[]{:S(2)}, u32[]{:S(2)}) collective-permute-start(bf16[512,256]{1,0:T(8,128)(2,1)S(1)} %slice.60), channel_id=1, source_target_pairs={{0,3},{1,0},{2,1},{3,2},{4,7},{5,4},{6,5},{7,6},{8,11},{9,8},{10,9... | collective-permute-start | bytes 786440 | tf_op jit(solution)/shard_map/ppermute | solution.py:327
  48.7 0.1 pad_maximum_fusion
  48.7 0.9 collective-permute-start.6
  49.6 2.4 %collective-permute-start.7 = (bf16[2048,256]{1,0:T(8,128)(2,1)S(1)}, bf16[2048,256]{1,0:T(8,128)(2,1)S(1)}, u32[]{:S(2)}, u32[]{:S(2)}) collective-permute-start(bf16[2048,256]{1,0:T(8,128)(2,1)S(1)} %pad_maximum_fusion), channel_id=1, source_target_pairs={{0,12},{1,13},{2,14},{3,15},{4,0},{5,1},{6,2},{7,3},{8,4},{9,5},{1... | collective-permute-start | bytes 3145736 | tf_op jit(solution)/shard_map/ppermute | solution.py:327
  52.1 2.8 %collective-permute-done.2 = bf16[512,256]{1,0:T(8,128)(2,1)S(1)} collective-permute-done((bf16[512,256]{1,0:T(8,128)(2,1)S(1)}, bf16[512,256]{1,0:T(8,128)(2,1)S(1)}, u32[]{:S(2)}, u32[]{:S(2)}) %collective-permute-start.2) | collective-permute-done | bytes 262176 | tf_op jit(solution)/shard_map/ppermute | solution.py:327
  54.9 0.1 collective-permute-done.3
  55.0 1.7 %collective-permute-start.4 = (bf16[2048,256]{1,0:T(8,128)(2,1)S(1)}, bf16[2048,256]{1,0:T(8,128)(2,1)S(1)}, u32[]{:S(2)}, u32[]{:S(2)}) collective-permute-start(bf16[2048,256]{1,0:T(8,128)(2,1)S(1)} %constant_dynamic-update-slice_fusion), channel_id=1, source_target_pairs={{0,4},{1,5},{2,6},{3,7},{4,8},{5,9},{6,10},{7,11},{8,12},{9,13},{1... | collective-permute-start | bytes 3145736 | tf_op jit(solution)/shard_map/ppermute | solution.py:327
  56.7 1.6 %collective-permute-start.5 = (bf16[2048,256]{1,0:T(8,128)(2,1)S(1)}, bf16[2048,256]{1,0:T(8,128)(2,1)S(1)}, u32[]{:S(2)}, u32[]{:S(2)}) collective-permute-start(bf16[2048,256]{1,0:T(8,128)(2,1)S(1)} %constant_dynamic-update-slice_fusion), channel_id=1, source_target_pairs={{0,12},{1,13},{2,14},{3,15},{4,0},{5,1},{6,2},{7,3},{8,4},{9,5},{1... | collective-permute-start | bytes 3145736 | tf_op jit(solution)/shard_map/ppermute | solution.py:327
  58.3 5.9 %tiles_0.1 = (f32[64,128,256]{2,1,0:T(8,128)S(1)}, bf16[8,16,128,128]{3,2,1,0:T(8,128)(2,1)S(1)}) custom-call(s32[1152]{0:T(1024)S(1)} %reduce.refs_0_, s32[384]{0:T(512)S(1)} %reduce.1.refs_1_, bf16[704,128,128]{2,1,0:T(8,128)(2,1)} %bitcast.71, bf16[16,128,256]{2,1,0:T(8,128)(2,1)S(1)} %bitcast.54, bf16[16,128,256]{2,1,0:T(8,128)(2,1)S(1)} %bitcast.61), custom_call_target="tpu_custom_call" | custom-call | flops 1476395008 | bytes 5767168 | tf_op jit(solution)/shard_map/tiles_0/pallas_call | solution.py:237
  64.2 0.6 collective-permute-done.6
  64.9 0.1 collective-permute-start.10
  65.0 3.3 %collective-permute-start.11 = (bf16[1024,256]{1,0:T(8,128)(2,1)S(1)}, bf16[1024,256]{1,0:T(8,128)(2,1)S(1)}, u32[]{:S(2)}, u32[]{:S(2)}) collective-permute-start(bf16[1024,256]{1,0:T(8,128)(2,1)S(1)} %slice.64), channel_id=1, source_target_pairs={{0,12},{1,13},{2,14},{3,15},{4,0},{5,1},{6,2},{7,3},{8,4},{9,5},{1... | collective-permute-start | bytes 1572872 | tf_op jit(solution)/shard_map/ppermute | solution.py:327
  68.3 4.3 %tiles_1.1 = (f32[64,128,256]{2,1,0:T(8,128)S(1)}, bf16[8,16,128,128]{3,2,1,0:T(8,128)(2,1)S(1)}) custom-call(s32[1152]{0:T(1024)S(1)} %reduce.refs_0_, s32[384]{0:T(512)S(1)} %reduce.1.refs_1_, bf16[704,128,128]{2,1,0:T(8,128)(2,1)} %bitcast.72, bf16[16,128,256]{2,1,0:T(8,128)(2,1)S(1)} %bitcast.58, ...), custom_call_target="tpu_custom_call", output_to_operand_aliasing={{0}: (5, {}), {1}: (6, {})} | custom-call | flops 1476395008 | bytes 5767168 | tf_op jit(solution)/shard_map/tiles_1/pallas_call | solution.py:237
  72.6 3.4 %collective-permute-done.4 = bf16[2048,256]{1,0:T(8,128)(2,1)S(1)} collective-permute-done((bf16[2048,256]{1,0:T(8,128)(2,1)S(1)}, bf16[2048,256]{1,0:T(8,128)(2,1)S(1)}, u32[]{:S(2)}, u32[]{:S(2)}) %collective-permute-start.4) | collective-permute-done | bytes 1048608 | tf_op jit(solution)/shard_map/ppermute | solution.py:327
  76.1 0.1 collective-permute-start.8
  76.2 3.5 %collective-permute-start.9 = (bf16[1024,256]{1,0:T(8,128)(2,1)S(1)}, bf16[1024,256]{1,0:T(8,128)(2,1)S(1)}, u32[]{:S(2)}, u32[]{:S(2)}) collective-permute-start(bf16[1024,256]{1,0:T(8,128)(2,1)S(1)} %slice.62), channel_id=1, source_target_pairs={{0,12},{1,13},{2,14},{3,15},{4,0},{5,1},{6,2},{7,3},{8,4},{9,5},{1... | collective-permute-start | bytes 1572872 | tf_op jit(solution)/shard_map/ppermute | solution.py:327
  79.7 4.1 %tiles_2.1 = (f32[64,128,256]{2,1,0:T(8,128)S(1)}, bf16[8,16,128,128]{3,2,1,0:T(8,128)(2,1)S(1)}) custom-call(s32[1152]{0:T(1024)S(1)} %reduce.refs_0_, s32[384]{0:T(512)S(1)} %reduce.1.refs_1_, bf16[704,128,128]{2,1,0:T(8,128)(2,1)} %bitcast.73, bf16[16,128,256]{2,1,0:T(8,128)(2,1)S(1)} %bitcast.57, ...), custom_call_target="tpu_custom_call", output_to_operand_aliasing={{0}: (5, {}), {1}: (6, {})} | custom-call | flops 1476395008 | bytes 5767168 | tf_op jit(solution)/shard_map/tiles_2/pallas_call | solution.py:237
  83.8 2.2 %tiles_3.1 = (f32[64,128,256]{2,1,0:T(8,128)S(1)}, bf16[8,16,128,128]{3,2,1,0:T(8,128)(2,1)S(1)}) custom-call(s32[1152]{0:T(1024)S(1)} %reduce.refs_0_, s32[384]{0:T(512)S(1)} %reduce.1.refs_1_, bf16[704,128,128]{2,1,0:T(8,128)(2,1)} %bitcast.74, bf16[8,128,256]{2,1,0:T(8,128)(2,1)S(1)} %bitcast.62, ...), custom_call_target="tpu_custom_call", output_to_operand_aliasing={{0}: (5, {}), {1}: (6, {})} | custom-call | flops 738197504 | bytes 2883584 | tf_op jit(solution)/shard_map/tiles_3/pallas_call | solution.py:237
  86.0 1.3 %collective-permute-done.8 = bf16[1024,256]{1,0:T(8,128)(2,1)S(1)} collective-permute-done((bf16[1024,256]{1,0:T(8,128)(2,1)S(1)}, bf16[1024,256]{1,0:T(8,128)(2,1)S(1)}, u32[]{:S(2)}, u32[]{:S(2)}) %collective-permute-start.8) | collective-permute-done | bytes 524320 | tf_op jit(solution)/shard_map/ppermute | solution.py:327
  87.3 2.5 %tiles_4.1 = (f32[64,128,256]{2,1,0:T(8,128)S(1)}, bf16[8,16,128,128]{3,2,1,0:T(8,128)(2,1)S(1)}, bf16[8,128,256]{2,1,0:T(8,128)(2,1)S(1)}, bf16[8,128,256]{2,1,...) custom-call(s32[1152]{0:T(1024)S(1)} %reduce.refs_0_, ...), custom_call_target="tpu_custom_call", output_to_operand_aliasing={{0}: (5, {}), {1}: (6, {})} | custom-call | flops 738197504 | bytes 2883584 | tf_op jit(solution)/shard_map/tiles_4/pallas_call | solution.py:237
  89.8 0.1 collective-permute-start.12
  89.9 1.9 %collective-permute-done.12 = bf16[1024,256]{1,0:T(8,128)(2,1)S(1)} collective-permute-done((bf16[1024,256]{1,0:T(8,128)(2,1)S(1)}, bf16[1024,256]{1,0:T(8,128)(2,1)S(1)}, u32[]{:S(2)}, u32[]{:S(2)}) %collective-permute-start.12) | collective-permute-done | bytes 524320 | tf_op jit(solution)/shard_map/ppermute | solution.py:354
  91.8 0.2 fusion.6
  92.0 0.2 collective-permute-start.13
  92.2 0.1 fusion.12
  92.4 2.1 %collective-permute-start.14 = (bf16[512,256]{1,0:T(8,128)(2,1)S(1)}, bf16[512,256]{1,0:T(8,128)(2,1)S(1)}, u32[]{:S(2)}, u32[]{:S(2)}) collective-permute-start(bf16[512,256]{1,0:T(8,128)(2,1)S(1)} %get-tuple-element.66), channel_id=1, source_target_pairs={{0,32},{16,48},{32,64},{48,80},{64,96},{80,112},{96,0},{112,16},{1... | collective-permute-start | bytes 786440 | tf_op jit(solution)/shard_map/ppermute | solution.py:354
  94.5 1.0 collective-permute-done.13
  95.5 0.3 convert_add_fusion.1
  95.9 5.2 %collective-permute-done.14 = bf16[512,256]{1,0:T(8,128)(2,1)S(1)} collective-permute-done((bf16[512,256]{1,0:T(8,128)(2,1)S(1)}, bf16[512,256]{1,0:T(8,128)(2,1)S(1)}, u32[]{:S(2)}, u32[]{:S(2)}) %collective-permute-start.14) | collective-permute-done | bytes 262176 | tf_op jit(solution)/shard_map/ppermute | solution.py:354
  101.1 0.1 fusion.10
  101.2 3.3 %collective-permute-start.15 = (bf16[1024,256]{1,0:T(8,128)(2,1)S(1)}, bf16[1024,256]{1,0:T(8,128)(2,1)S(1)}, u32[]{:S(2)}, u32[]{:S(2)}) collective-permute-start(bf16[1024,256]{1,0:T(8,128)(2,1)S(1)} %pad_maximum_fusion.1), channel_id=1, source_target_pairs={{0,32},{16,48},{32,64},{48,80},{64,96},{80,112},{96,0},{112,16},{1... | collective-permute-start | bytes 1572872 | tf_op jit(solution)/shard_map/ppermute | solution.py:354
  104.5 0.1 fusion.9
  104.6 0.1 collective-permute-start.17
  104.7 0.3 fusion.14
  105.0 10.3 %collective-permute-done.15 = bf16[1024,256]{1,0:T(8,128)(2,1)S(1)} collective-permute-done((bf16[1024,256]{1,0:T(8,128)(2,1)S(1)}, bf16[1024,256]{1,0:T(8,128)(2,1)S(1)}, u32[]{:S(2)}, u32[]{:S(2)}) %collective-permute-start.15) | collective-permute-done | bytes 524320 | tf_op jit(solution)/shard_map/ppermute | solution.py:354
  115.3 3.6 %collective-permute-done.17 = bf16[1024,256]{1,0:T(8,128)(2,1)S(1)} collective-permute-done((bf16[1024,256]{1,0:T(8,128)(2,1)S(1)}, bf16[1024,256]{1,0:T(8,128)(2,1)S(1)}, u32[]{:S(2)}, u32[]{:S(2)}) %collective-permute-start.17) | collective-permute-done | bytes 524320 | tf_op jit(solution)/shard_map/ppermute | solution.py:354
  119.0 1.3 %fusion.2 = bf16[1024,256]{1,0:T(8,128)(2,1)} fusion(f32[1024,256]{1,0:T(8,128)S(1)} %fusion.14, bf16[256,256]{1,0:T(8,128)(2,1)S(1)} %copy-done.6, bf16[1024,256]{1,0:T(8,128)(2,1)S(1)} %collective-permute-done.17, bf16[1024,256]{1,0:T(8,128)(2,1)S(1)} %collective-permute-done.15, bf16[1024,256]{1,0:T(8,128)(2,1)S(1)} %bitcast.76, ...), kind=kOutput, calls=%fused_computation.3 | convolution fusion | flops 137625600 | bytes 3806208 | tf_op jit(solution)/shard_map/dot_general | solution.py:369
  (40 shorter events, 0.5 us)
Async XLA Ops:
  0.0 104.7 %copy-start = (bf16[256,256]{1,0:T(8,128)(2,1)S(1)}, bf16[256,256]{1,0:T(8,128)(2,1)}, u32[]{:S(2)}) copy-start(bf16[256,256]{1,0:T(8,128)(2,1)} %param.17) | copy-start | bytes 393220
  0.0 1.1 copy-start.1
  1.1 0.7 copy-start.4
  1.8 37.1 %copy-start.2 = (s32[1,1,704]{2,1,0:T(1,128)S(1)}, s32[1,1,704]{2,1,0:T(1,128)}, u32[]{:S(2)}) copy-start(s32[1,1,704]{2,1,0:T(1,128)} %param.13) | copy-start | bytes 8452
  1.8 37.1 %copy-start.3 = (s32[1,1,704]{2,1,0:T(1,128)S(1)}, s32[1,1,704]{2,1,0:T(1,128)}, u32[]{:S(2)}) copy-start(s32[1,1,704]{2,1,0:T(1,128)} %param.14) | copy-start | bytes 8452
  34.8 10.5 %collective-permute-start = (bf16[1024,256]{1,0:T(8,128)(2,1)S(1)}, bf16[1024,256]{1,0:T(8,128)(2,1)S(1)}, u32[]{:S(2)}, u32[]{:S(2)}) collective-permute-start(bf16[1024,256]{1,0:T(8,128)(2,1)S(1)} %unpack.1), channel_id=1, source_target_pairs={{0,1},{1,2},{2,3},{3,0},{4,5},{5,6},{6,7},{7,4},{8,9},{9,10},{10,1... | collective-permute-start | bytes 1572872 | tf_op jit(solution)/shard_map/ppermute | solution.py:327
  35.5 9.8 %collective-permute-start.1 = (bf16[1024,256]{1,0:T(8,128)(2,1)S(1)}, bf16[1024,256]{1,0:T(8,128)(2,1)S(1)}, u32[]{:S(2)}, u32[]{:S(2)}) collective-permute-start(bf16[1024,256]{1,0:T(8,128)(2,1)S(1)} %unpack.1), channel_id=1, source_target_pairs={{0,3},{1,0},{2,1},{3,2},{4,7},{5,4},{6,5},{7,6},{8,11},{9,8},{10,9... | collective-permute-start | bytes 1572872 | tf_op jit(solution)/shard_map/ppermute | solution.py:327
  45.3 9.6 %collective-permute-start.2 = (bf16[512,256]{1,0:T(8,128)(2,1)S(1)}, bf16[512,256]{1,0:T(8,128)(2,1)S(1)}, u32[]{:S(2)}, u32[]{:S(2)}) collective-permute-start(bf16[512,256]{1,0:T(8,128)(2,1)S(1)} %slice.59), channel_id=1, source_target_pairs={{0,1},{1,2},{2,3},{3,0},{4,5},{5,6},{6,7},{7,4},{8,9},{9,10},{10,1... | collective-permute-start | bytes 786440 | tf_op jit(solution)/shard_map/ppermute | solution.py:327
  45.4 9.6 %collective-permute-start.3 = (bf16[512,256]{1,0:T(8,128)(2,1)S(1)}, bf16[512,256]{1,0:T(8,128)(2,1)S(1)}, u32[]{:S(2)}, u32[]{:S(2)}) collective-permute-start(bf16[512,256]{1,0:T(8,128)(2,1)S(1)} %slice.60), channel_id=1, source_target_pairs={{0,3},{1,0},{2,1},{3,2},{4,7},{5,4},{6,5},{7,6},{8,11},{9,8},{10,9... | collective-permute-start | bytes 786440 | tf_op jit(solution)/shard_map/ppermute | solution.py:327
  48.7 16.1 %collective-permute-start.6 = (bf16[2048,256]{1,0:T(8,128)(2,1)S(1)}, bf16[2048,256]{1,0:T(8,128)(2,1)S(1)}, u32[]{:S(2)}, u32[]{:S(2)}) collective-permute-start(bf16[2048,256]{1,0:T(8,128)(2,1)S(1)} %pad_maximum_fusion), channel_id=1, source_target_pairs={{0,4},{1,5},{2,6},{3,7},{4,8},{5,9},{6,10},{7,11},{8,12},{9,13},{1... | collective-permute-start | bytes 3145736 | tf_op jit(solution)/shard_map/ppermute | solution.py:327
  49.6 15.2 %collective-permute-start.7 = (bf16[2048,256]{1,0:T(8,128)(2,1)S(1)}, bf16[2048,256]{1,0:T(8,128)(2,1)S(1)}, u32[]{:S(2)}, u32[]{:S(2)}) collective-permute-start(bf16[2048,256]{1,0:T(8,128)(2,1)S(1)} %pad_maximum_fusion), channel_id=1, source_target_pairs={{0,12},{1,13},{2,14},{3,15},{4,0},{5,1},{6,2},{7,3},{8,4},{9,5},{1... | collective-permute-start | bytes 3145736 | tf_op jit(solution)/shard_map/ppermute | solution.py:327
  55.0 21.1 %collective-permute-start.4 = (bf16[2048,256]{1,0:T(8,128)(2,1)S(1)}, bf16[2048,256]{1,0:T(8,128)(2,1)S(1)}, u32[]{:S(2)}, u32[]{:S(2)}) collective-permute-start(bf16[2048,256]{1,0:T(8,128)(2,1)S(1)} %constant_dynamic-update-slice_fusion), channel_id=1, source_target_pairs={{0,4},{1,5},{2,6},{3,7},{4,8},{5,9},{6,10},{7,11},{8,12},{9,13},{1... | collective-permute-start | bytes 3145736 | tf_op jit(solution)/shard_map/ppermute | solution.py:327
  56.7 19.4 %collective-permute-start.5 = (bf16[2048,256]{1,0:T(8,128)(2,1)S(1)}, bf16[2048,256]{1,0:T(8,128)(2,1)S(1)}, u32[]{:S(2)}, u32[]{:S(2)}) collective-permute-start(bf16[2048,256]{1,0:T(8,128)(2,1)S(1)} %constant_dynamic-update-slice_fusion), channel_id=1, source_target_pairs={{0,12},{1,13},{2,14},{3,15},{4,0},{5,1},{6,2},{7,3},{8,4},{9,5},{1... | collective-permute-start | bytes 3145736 | tf_op jit(solution)/shard_map/ppermute | solution.py:327
  64.9 19.0 %collective-permute-start.10 = (bf16[1024,256]{1,0:T(8,128)(2,1)S(1)}, bf16[1024,256]{1,0:T(8,128)(2,1)S(1)}, u32[]{:S(2)}, u32[]{:S(2)}) collective-permute-start(bf16[1024,256]{1,0:T(8,128)(2,1)S(1)} %slice.63), channel_id=1, source_target_pairs={{0,4},{1,5},{2,6},{3,7},{4,8},{5,9},{6,10},{7,11},{8,12},{9,13},{1... | collective-permute-start | bytes 1572872 | tf_op jit(solution)/shard_map/ppermute | solution.py:327
  65.0 18.8 %collective-permute-start.11 = (bf16[1024,256]{1,0:T(8,128)(2,1)S(1)}, bf16[1024,256]{1,0:T(8,128)(2,1)S(1)}, u32[]{:S(2)}, u32[]{:S(2)}) collective-permute-start(bf16[1024,256]{1,0:T(8,128)(2,1)S(1)} %slice.64), channel_id=1, source_target_pairs={{0,12},{1,13},{2,14},{3,15},{4,0},{5,1},{6,2},{7,3},{8,4},{9,5},{1... | collective-permute-start | bytes 1572872 | tf_op jit(solution)/shard_map/ppermute | solution.py:327
  76.1 11.2 %collective-permute-start.8 = (bf16[1024,256]{1,0:T(8,128)(2,1)S(1)}, bf16[1024,256]{1,0:T(8,128)(2,1)S(1)}, u32[]{:S(2)}, u32[]{:S(2)}) collective-permute-start(bf16[1024,256]{1,0:T(8,128)(2,1)S(1)} %slice.61), channel_id=1, source_target_pairs={{0,4},{1,5},{2,6},{3,7},{4,8},{5,9},{6,10},{7,11},{8,12},{9,13},{1... | collective-permute-start | bytes 1572872 | tf_op jit(solution)/shard_map/ppermute | solution.py:327
  76.2 11.1 %collective-permute-start.9 = (bf16[1024,256]{1,0:T(8,128)(2,1)S(1)}, bf16[1024,256]{1,0:T(8,128)(2,1)S(1)}, u32[]{:S(2)}, u32[]{:S(2)}) collective-permute-start(bf16[1024,256]{1,0:T(8,128)(2,1)S(1)} %slice.62), channel_id=1, source_target_pairs={{0,12},{1,13},{2,14},{3,15},{4,0},{5,1},{6,2},{7,3},{8,4},{9,5},{1... | collective-permute-start | bytes 1572872 | tf_op jit(solution)/shard_map/ppermute | solution.py:327
  89.8 2.0 %collective-permute-start.12 = (bf16[1024,256]{1,0:T(8,128)(2,1)S(1)}, bf16[1024,256]{1,0:T(8,128)(2,1)S(1)}, u32[]{:S(2)}, u32[]{:S(2)}) collective-permute-start(bf16[1024,256]{1,0:T(8,128)(2,1)S(1)} %bitcast.70), channel_id=1, source_target_pairs={{0,16},{16,0},{32,48},{48,32},{64,80},{80,64},{96,112},{112,96},{1... | collective-permute-start | bytes 1572872 | tf_op jit(solution)/shard_map/ppermute | solution.py:354
  92.0 3.5 %collective-permute-start.13 = (bf16[3,1024,256]{2,1,0:T(8,128)(2,1)S(1)}, bf16[3,1024,256]{2,1,0:T(8,128)(2,1)S(1)}, u32[]{:S(2)}, u32[]{:S(2)}) collective-permute-start(bf16[3,1024,256]{2,1,0:T(8,128)(2,1)S(1)} %bitcast.69), channel_id=1, source_target_pairs={{0,16},{16,0},{32,48},{48,32},{64,80},{80,64},{96,112},{112,96},{1... | collective-permute-start | bytes 4718600 | tf_op jit(solution)/shard_map/ppermute | solution.py:354
  92.4 8.7 %collective-permute-start.14 = (bf16[512,256]{1,0:T(8,128)(2,1)S(1)}, bf16[512,256]{1,0:T(8,128)(2,1)S(1)}, u32[]{:S(2)}, u32[]{:S(2)}) collective-permute-start(bf16[512,256]{1,0:T(8,128)(2,1)S(1)} %get-tuple-element.66), channel_id=1, source_target_pairs={{0,32},{16,48},{32,64},{48,80},{64,96},{80,112},{96,0},{112,16},{1... | collective-permute-start | bytes 786440 | tf_op jit(solution)/shard_map/ppermute | solution.py:354
  94.5 10.0 %collective-permute-start.16 = (bf16[512,256]{1,0:T(8,128)(2,1)S(1)}, bf16[512,256]{1,0:T(8,128)(2,1)S(1)}, u32[]{:S(2)}, u32[]{:S(2)}) collective-permute-start(bf16[512,256]{1,0:T(8,128)(2,1)S(1)} %get-tuple-element.67), channel_id=1, source_target_pairs={{0,96},{16,112},{32,0},{48,16},{64,32},{80,48},{96,64},{112,80},{1... | collective-permute-start | bytes 786440 | tf_op jit(solution)/shard_map/ppermute | solution.py:354
  95.5 9.2 %copy-start.5 = (s32[1024]{0:T(1024)S(1)}, s32[1024]{0:T(1024)}, u32[]{:S(2)}) copy-start(s32[1024]{0:T(1024)} %param.12) | copy-start | bytes 12292
  95.5 9.2 %copy-start.7 = (bf16[256]{0:T(256)(128)(2,1)S(1)}, bf16[256]{0:T(256)(128)(2,1)}, u32[]{:S(2)}) copy-start(bf16[256]{0:T(256)(128)(2,1)} %param.19) | copy-start | bytes 1540
  95.8 23.1 %copy-start.6 = (bf16[256,256]{1,0:T(8,128)(2,1)S(1)}, bf16[256,256]{1,0:T(8,128)(2,1)}, u32[]{:S(2)}) copy-start(bf16[256,256]{1,0:T(8,128)(2,1)} %param.18) | copy-start | bytes 393220
  101.2 14.2 %collective-permute-start.15 = (bf16[1024,256]{1,0:T(8,128)(2,1)S(1)}, bf16[1024,256]{1,0:T(8,128)(2,1)S(1)}, u32[]{:S(2)}, u32[]{:S(2)}) collective-permute-start(bf16[1024,256]{1,0:T(8,128)(2,1)S(1)} %pad_maximum_fusion.1), channel_id=1, source_target_pairs={{0,32},{16,48},{32,64},{48,80},{64,96},{80,112},{96,0},{112,16},{1... | collective-permute-start | bytes 1572872 | tf_op jit(solution)/shard_map/ppermute | solution.py:354
  104.6 14.4 %collective-permute-start.17 = (bf16[1024,256]{1,0:T(8,128)(2,1)S(1)}, bf16[1024,256]{1,0:T(8,128)(2,1)S(1)}, u32[]{:S(2)}, u32[]{:S(2)}) collective-permute-start(bf16[1024,256]{1,0:T(8,128)(2,1)S(1)} %pad_maximum_fusion.2), channel_id=1, source_target_pairs={{0,96},{16,112},{32,0},{48,16},{64,32},{80,48},{96,64},{112,80},{1... | collective-permute-start | bytes 1572872 | tf_op jit(solution)/shard_map/ppermute | solution.py:354

commit v5 on v4

--- a/solution.py
+++ b/solution.py
@@ -12,8 +12,8 @@
 PAIRS = 8
 BLOCK = 2 * PAIRS
 BUFS = 8
-LIST = 1152
-STAGES = 5
+LIST = 1024
+STAGES = 4
 LANES = 384
 MB = 1 << 20
 VMEM_TILES = 30 * MB
@@ -99,8 +99,8 @@
     order_y = ring_order(((source & 3) - y) & 3)
     outer = jnp.where(core == 0, order_z, order_y)
     inner = jnp.where(core == 0, order_y, order_z)
-    stage = jnp.where(outer == 0, 0, jnp.where(inner < 2, 1, 2) + jnp.where(outer == 3, 2, 0))
-    side = (inner & 1) * 8 + jnp.where(outer == 2, 16, 0)
+    stage = jnp.where(outer == 0, 0, jnp.where(inner < 2, 1, 2) + jnp.where(outer == 3, 1, 0))
+    side = (inner & 1) * 8 + jnp.where(outer == 2, 16, jnp.where((outer == 3) & (inner < 2), 32, 0))
     tile = jnp.where(outer == 0, inner * 8, side) + (col & 7)
     owner = row >> 3
     dx = ((owner >> 1) - x) & 3
@@ -145,13 +145,36 @@
     start_ref[...] = ahead[:1].astype(jnp.int32)
 
 
+def fetch(block, code_ref, weights, wbuf, wsem):
+    slot = lax.rem(block, BUFS)
+    for i in range(BLOCK):
+        s = (code_ref[block * BLOCK + i] >> 8) & 1023
+        pltpu.make_async_copy(weights.at[s], wbuf.at[slot, i], wsem.at[slot]).start()
+
+
+def arrive(block, weights, wbuf, wsem):
+    slot = lax.rem(block, BUFS)
+    pltpu.make_async_copy(weights.at[pl.ds(0, BLOCK)], wbuf.at[slot], wsem.at[slot]).wait()
+
+
+def open_kernel(code_ref, start_ref, weights, acc, wbuf, wsem):
+    total = start_ref[64 * STAGES]
+    for i in range(BUFS - 1):
+        pl.when(i < total)(functools.partial(fetch, i, code_ref, weights, wbuf, wsem))
+
+    def clear(i, _):
+        acc[i] = jnp.zeros(acc.shape[1:], acc.dtype)
+        return 0
+
+    lax.fori_loop(0, acc.shape[0], clear, 0)
+    for i in range(BUFS - 1):
+        pl.when(i < total)(functools.partial(arrive, i, weights, wbuf, wsem))
+
+
 def tiles_kernel(stage, n_pieces, outs, *refs):
-    opening = stage == 0
     code_ref, start_ref, weights = refs[:3]
     pieces = refs[3 : 3 + n_pieces]
-    k = 3 + n_pieces
-    if not opening:
-        k += 2
+    k = 5 + n_pieces
     acc, wbuf = refs[k : k + 2]
     out_refs = refs[k + 2 : k + 2 + len(outs)]
     panel, wsem, psem = refs[k + 2 + len(outs) :]
@@ -169,33 +192,13 @@
     for c in copies:
         c.start()
     panel[0] = jnp.zeros(panel.shape[1:], panel.dtype)
-
-    def fetch(block):
-        slot = lax.rem(block, BUFS)
-        for i in range(BLOCK):
-            s = (code_ref[block * BLOCK + i] >> 8) & 1023
-            pltpu.make_async_copy(weights.at[s], wbuf.at[slot, i], wsem.at[slot]).start()
-
-    def arrive(block):
-        slot = lax.rem(block, BUFS)
-        pltpu.make_async_copy(weights.at[pl.ds(0, BLOCK)], wbuf.at[slot], wsem.at[slot]).wait()
-
-    if opening:
-        for i in range(ahead):
-            pl.when(first + i < total)(functools.partial(fetch, first + i))
-
-        def clear(i, _):
-            acc[i] = jnp.zeros(acc.shape[1:], acc.dtype)
-            return 0
-
-        lax.fori_loop(0, acc.shape[0], clear, 0)
-    fetched = first if opening else first + ahead
+    fetched = first + ahead
     for c in copies:
         c.wait()
 
     def run_block(block, _):
-        pl.when(block + ahead < total)(functools.partial(fetch, block + ahead))
-        pl.when(block >= fetched)(functools.partial(arrive, block))
+        pl.when(block + ahead < total)(functools.partial(fetch, block + ahead, code_ref, weights, wbuf, wsem))
+        pl.when(block >= fetched)(functools.partial(arrive, block, weights, wbuf, wsem))
         slot = lax.rem(block, BUFS)
         for u in range(PAIRS):
             c0 = code_ref[block * BLOCK + 2 * u]
@@ -214,10 +217,30 @@
 
         lax.fori_loop(0, n, give, 0)
     for i in range(ahead):
-        pl.when((last + i < total) & (last + i >= fetched))(functools.partial(arrive, last + i))
-
-
-def run_tiles(stage, code, start, weights, pieces, state=(), outs=()):
+        pl.when((last + i < total) & (last + i >= fetched))(
+            functools.partial(arrive, last + i, weights, wbuf, wsem)
+        )
+
+
+def open_tiles(code, start, weights, width):
+    vmem = pl.BlockSpec(memory_space=pltpu.VMEM)
+    smem = pl.BlockSpec(memory_space=pltpu.SMEM)
+    t = weights.shape[1]
+    return pl.pallas_call(
+        open_kernel,
+        out_shape=[
+            pltpu.VMEM((64, t, width), jnp.float32),
+            pltpu.VMEM((BUFS, BLOCK, t, t), jnp.bfloat16),
+        ],
+        in_specs=[smem, smem, pl.BlockSpec(memory_space=pl.ANY)],
+        out_specs=[vmem, vmem],
+        scratch_shapes=[pltpu.SemaphoreType.DMA((BUFS,))],
+        compiler_params=pltpu.CompilerParams(vmem_limit_bytes=VMEM_TILES),
+        name="tiles_open",
+    )(code, start, weights)
+
+
+def run_tiles(stage, code, start, weights, pieces, state, outs=()):
     any_spec = pl.BlockSpec(memory_space=pl.ANY)
     vmem = pl.BlockSpec(memory_space=pltpu.VMEM)
     smem = pl.BlockSpec(memory_space=pltpu.SMEM)
@@ -330,22 +353,22 @@
         return jnp.concatenate(parts, axis=0)
 
     plus, minus = send(owned, 0, 1), send(owned, 0, -1)
-    plus, minus, code, start = lax.optimization_barrier((plus, minus, code, start))
+    state = open_tiles(code, start, weights, width)
+    plus, minus, code, start, *state = lax.optimization_barrier((plus, minus, code, start, *state))
     hi = cat(minus, send(plus[:half], 0, 1), send(minus[half:], 0, -1))
     lo = cat(owned, plus)
     lists = (code, start, weights)
     lo_p, lo_m = send(lo, 1, 1), send(lo, 1, -1)
     hi_p, hi_m = send(hi, 1, 1), send(hi, 1, -1)
-    state = run_tiles(0, *lists, [lo, hi])
+    state = run_tiles(0, *lists, [lo, hi], state)
     lo_p, lo_m, *state = lax.optimization_barrier((lo_p, lo_m, *state))
     far_lo = [send(lo_p[:rows], 1, 1), send(lo_m[rows:], 1, -1)]
     state = run_tiles(1, *lists, [lo_p, lo_m], state)
     hi_p, hi_m, *state = lax.optimization_barrier((hi_p, hi_m, *state))
     far_hi = [send(hi_p[:rows], 1, 1), send(hi_m[rows:], 1, -1)]
-    state = run_tiles(2, *lists, [hi_p, hi_m], state)
-    state = run_tiles(3, *lists, far_lo, state)
+    state = run_tiles(2, *lists, [hi_p, hi_m, *far_lo], state)
     *_, other_far, mine_far, other_rest, mine_rest = run_tiles(
-        4, *lists, far_hi, state, ((0, 8), (8, 8), (16, 24), (40, 24))
+        3, *lists, far_hi, state, ((0, 8), (8, 8), (16, 24), (40, 24))
     )
 
     f32 = jnp.float32

time: 122 us -> 121 us (level); the launches traced: 120 us -> 121 us
  Pallas kernels: 25.5 us -> 21.9 us
  waiting for transfers between devices: 34.6 us -> 37.5 us
    pallas_call x5 -> x4, Pallas kernels: 19 us -> 11.9 us  [run_tiles(): pl.pallas_call(functools.partial(tiles_kernel, stage, n, outs), out_shape...]
    pallas_call x0 -> x1, Pallas kernels: none -> 3.5 us  [open_tiles(): pl.pallas_call(open_kernel, out_shape=[pltpu.VMEM((64, t, width), jnp.flo...]
    ppermute x12, waiting for transfers between devices: 12.6 us -> 16 us  [send(): return lax.ppermute(v, ('row', 'col'), panel_perm(turn, step))]
  transfers between devices with their start and end apart: 18 -> 18, of which waited for: 11 -> 12; matrix products, arithmetic and copies ran while one was open for 1% -> 1% of each run, Pallas kernels for 15% -> 13%
where the time goes in v5:
time: 121 us
  waiting for transfers between devices  37.5 us (31%)
  blocking collectives  28.4 us (23%)
  starting transfers between devices  27.1 us (22%)
  Pallas kernels  21.9 us (18%)
  local copies, waits for them, and re-layouts  2.27 us (2%)
  matrix products  1.58 us (1%)
    all_to_all x1, blocking collectives, per_device(): lax.all_to_all(outgoing.reshape(devices, SLOT_ROWS, width), ('row', 'col'...  28.4 us
    ppermute x6, waiting for transfers between devices, over(): return lax.ppermute(v, 'row', row_perm(dx, flip))  21.5 us
    ppermute x12, starting transfers between devices, send(): return lax.ppermute(v, ('row', 'col'), panel_perm(turn, step))  20.2 us
    ppermute x12, waiting for transfers between devices, send(): return lax.ppermute(v, ('row', 'col'), panel_perm(turn, step))  16 us
    pallas_call x4, Pallas kernels, run_tiles(): pl.pallas_call(functools.partial(tiles_kernel, stage, n, outs), out_shape...  11.9 us
    ppermute x6, starting transfers between devices, over(): return lax.ppermute(v, 'row', row_perm(dx, flip))  6.89 us
    pallas_call x1, Pallas kernels, open_tiles(): pl.pallas_call(open_kernel, out_shape=[pltpu.VMEM((64, t, width), jnp.flo...  3.5 us
    pallas_call x1, Pallas kernels, per_device(): pl.pallas_call(pack_kernel, out_shape=jax.ShapeDtypeStruct((devices * SLO...  2.54 us
  transfers between devices with their start and end apart: 18, of which 12 were waited for; matrix products, arithmetic and copies ran while one was open for 1% of the time, Pallas kernels for 13%

profile of v5, /device:TPU:6, one launch (start us, length us, event | category | flops | bytes accessed | tf_op | source)
XLA Modules:
  0.0 120.6 jit_solution(3682451297018054396)
XLA Ops:
  0.0 1.1 copy-done.1
  1.1 0.7 copy-done.4
  1.8 2.5 %pack.1 = bf16[2048,256]{1,0:T(8,128)(2,1)S(1)} custom-call(s32[1,512]{1,0:T(1,128)S(1)} %bitcast.74, bf16[1024,256]{1,0:T(8,128)(2,1)S(1)} %copy-done.1), custom_call_target="tpu_custom_call" | custom-call | tf_op jit(solution)/shard_map/pack/pallas_call | solution.py:309
  4.3 28.4 %all_to_all.5 = bf16[128,16,256]{2,1,0:T(8,128)(2,1)S(1)} all-to-all(bf16[128,16,256]{2,1,0:T(8,128)(2,1)S(1)} %bitcast.57), channel_id=1, replica_groups=mesh['row'=8,'col'=16] {'row','col'}, dimensions={0} | all-to-all | bytes 2097152 | tf_op jit(solution)/shard_map/all_to_all | solution.py:317
  32.7 2.1 %unpack.1 = bf16[1024,256]{1,0:T(8,128)(2,1)S(1)} custom-call(bf16[2048,256]{1,0:T(8,128)(2,1)S(1)} %bitcast.56), custom_call_target="tpu_custom_call" | custom-call | tf_op jit(solution)/shard_map/unpack/pallas_call | solution.py:325
  34.8 0.7 collective-permute-start
  35.5 2.6 %collective-permute-start.1 = (bf16[1024,256]{1,0:T(8,128)(2,1)S(1)}, bf16[1024,256]{1,0:T(8,128)(2,1)S(1)}, u32[]{:S(2)}, u32[]{:S(2)}) collective-permute-start(bf16[1024,256]{1,0:T(8,128)(2,1)S(1)} %unpack.1), channel_id=1, source_target_pairs={{0,3},{1,0},{2,1},{3,2},{4,7},{5,4},{6,5},{7,6},{8,11},{9,8},{10,9... | collective-permute-start | bytes 1572872 | tf_op jit(solution)/shard_map/ppermute | solution.py:350
  38.7 0.1 pad_add_fusion.where_ref
  38.8 1.9 %plan.1 = (s32[1,1024]{1,0:T(1,128)S(1)}, s32[1,384]{1,0:T(1,128)S(1)}) custom-call(s32[4]{0:T(128)S(1)} %pad_add_fusion.where_ref, s32[1]{0:T(128)} %bitcast.54.count_ref, s32[1,704]{1,0:T(1,128)S(1)} %bitcast.72, s32[1,704]{1,0:T(1,128)S(1)} %bitcast.73), custom_call_target="tpu_custom_call" | custom-call | tf_op jit(solution)/shard_map/plan/pallas_call | solution.py:334
  40.7 3.5 %tiles_open.1 = (f32[64,128,256]{2,1,0:T(8,128)S(1)}, bf16[8,16,128,128]{3,2,1,0:T(8,128)(2,1)S(1)}) custom-call(s32[1024]{0:T(1024)S(1)} %bitcast.67, s32[384]{0:T(512)S(1)} %reduce.start_ref.refs_1_, bf16[704,128,128]{2,1,0:T(8,128)(2,1)} %bitcast.77), custom_call_target="tpu_custom_call" | custom-call | tf_op jit(solution)/shard_map/tiles_open/pallas_call | solution.py:229
  44.2 1.0 collective-permute-done
  45.3 0.1 collective-permute-start.2
  45.4 3.3 %collective-permute-start.3 = (bf16[512,256]{1,0:T(8,128)(2,1)S(1)}, bf16[512,256]{1,0:T(8,128)(2,1)S(1)}, u32[]{:S(2)}, u32[]{:S(2)}) collective-permute-start(bf16[512,256]{1,0:T(8,128)(2,1)S(1)} %slice.60), channel_id=1, source_target_pairs={{0,3},{1,0},{2,1},{3,2},{4,7},{5,4},{6,5},{7,6},{8,11},{9,8},{10,9... | collective-permute-start | bytes 786440 | tf_op jit(solution)/shard_map/ppermute | solution.py:350
  48.7 0.1 pad_maximum_fusion
  48.7 0.9 collective-permute-start.6
  49.6 2.4 %collective-permute-start.7 = (bf16[2048,256]{1,0:T(8,128)(2,1)S(1)}, bf16[2048,256]{1,0:T(8,128)(2,1)S(1)}, u32[]{:S(2)}, u32[]{:S(2)}) collective-permute-start(bf16[2048,256]{1,0:T(8,128)(2,1)S(1)} %pad_maximum_fusion), channel_id=1, source_target_pairs={{0,12},{1,13},{2,14},{3,15},{4,0},{5,1},{6,2},{7,3},{8,4},{9,5},{1... | collective-permute-start | bytes 3145736 | tf_op jit(solution)/shard_map/ppermute | solution.py:350
  52.1 2.8 %collective-permute-done.2 = bf16[512,256]{1,0:T(8,128)(2,1)S(1)} collective-permute-done((bf16[512,256]{1,0:T(8,128)(2,1)S(1)}, bf16[512,256]{1,0:T(8,128)(2,1)S(1)}, u32[]{:S(2)}, u32[]{:S(2)}) %collective-permute-start.2) | collective-permute-done | bytes 262176 | tf_op jit(solution)/shard_map/ppermute | solution.py:350
  55.0 1.7 %collective-permute-start.4 = (bf16[2048,256]{1,0:T(8,128)(2,1)S(1)}, bf16[2048,256]{1,0:T(8,128)(2,1)S(1)}, u32[]{:S(2)}, u32[]{:S(2)}) collective-permute-start(bf16[2048,256]{1,0:T(8,128)(2,1)S(1)} %constant_dynamic-update-slice_fusion), channel_id=1, source_target_pairs={{0,4},{1,5},{2,6},{3,7},{4,8},{5,9},{6,10},{7,11},{8,12},{9,13},{1... | collective-permute-start | bytes 3145736 | tf_op jit(solution)/shard_map/ppermute | solution.py:350
  56.7 1.6 %collective-permute-start.5 = (bf16[2048,256]{1,0:T(8,128)(2,1)S(1)}, bf16[2048,256]{1,0:T(8,128)(2,1)S(1)}, u32[]{:S(2)}, u32[]{:S(2)}) collective-permute-start(bf16[2048,256]{1,0:T(8,128)(2,1)S(1)} %constant_dynamic-update-slice_fusion), channel_id=1, source_target_pairs={{0,12},{1,13},{2,14},{3,15},{4,0},{5,1},{6,2},{7,3},{8,4},{9,5},{1... | collective-permute-start | bytes 3145736 | tf_op jit(solution)/shard_map/ppermute | solution.py:350
  58.3 3.1 %tiles_0.1 = (f32[64,128,256]{2,1,0:T(8,128)S(1)}, bf16[8,16,128,128]{3,2,1,0:T(8,128)(2,1)S(1)}) custom-call(s32[1024]{0:T(1024)S(1)} %bitcast.68, s32[384]{0:T(512)S(1)} %reduce.start_ref.refs_1_, bf16[704,128,128]{2,1,0:T(8,128)(2,1)} %bitcast.78, bf16[16,128,256]{2,1,0:T(8,128)(2,1)S(1)} %bitcast.55, ...), custom_call_target="tpu_custom_call", output_to_operand_aliasing={{0}: (5, {}), {1}: (6, {})} | custom-call | flops 1476395008 | bytes 5767168 | tf_op jit(solution)/shard_map/tiles_0/pallas_call | solution.py:260
  61.4 3.5 %collective-permute-done.6 = bf16[2048,256]{1,0:T(8,128)(2,1)S(1)} collective-permute-done((bf16[2048,256]{1,0:T(8,128)(2,1)S(1)}, bf16[2048,256]{1,0:T(8,128)(2,1)S(1)}, u32[]{:S(2)}, u32[]{:S(2)}) %collective-permute-start.6) | collective-permute-done | bytes 1048608 | tf_op jit(solution)/shard_map/ppermute | solution.py:350
  64.9 0.1 collective-permute-start.10
  65.0 3.3 %collective-permute-start.11 = (bf16[1024,256]{1,0:T(8,128)(2,1)S(1)}, bf16[1024,256]{1,0:T(8,128)(2,1)S(1)}, u32[]{:S(2)}, u32[]{:S(2)}) collective-permute-start(bf16[1024,256]{1,0:T(8,128)(2,1)S(1)} %slice.64), channel_id=1, source_target_pairs={{0,12},{1,13},{2,14},{3,15},{4,0},{5,1},{6,2},{7,3},{8,4},{9,5},{1... | collective-permute-start | bytes 1572872 | tf_op jit(solution)/shard_map/ppermute | solution.py:350
  68.3 3.3 %tiles_1.1 = (f32[64,128,256]{2,1,0:T(8,128)S(1)}, bf16[8,16,128,128]{3,2,1,0:T(8,128)(2,1)S(1)}) custom-call(s32[1024]{0:T(1024)S(1)} %bitcast.69, s32[384]{0:T(512)S(1)} %reduce.start_ref.refs_1_, bf16[704,128,128]{2,1,0:T(8,128)(2,1)} %bitcast.79, bf16[16,128,256]{2,1,0:T(8,128)(2,1)S(1)} %bitcast.60, ...), custom_call_target="tpu_custom_call", output_to_operand_aliasing={{0}: (5, {}), {1}: (6, {})} | custom-call | flops 1476395008 | bytes 5767168 | tf_op jit(solution)/shard_map/tiles_1/pallas_call | solution.py:260
  71.6 4.5 %collective-permute-done.4 = bf16[2048,256]{1,0:T(8,128)(2,1)S(1)} collective-permute-done((bf16[2048,256]{1,0:T(8,128)(2,1)S(1)}, bf16[2048,256]{1,0:T(8,128)(2,1)S(1)}, u32[]{:S(2)}, u32[]{:S(2)}) %collective-permute-start.4) | collective-permute-done | bytes 1048608 | tf_op jit(solution)/shard_map/ppermute | solution.py:350
  76.1 0.1 collective-permute-start.8
  76.2 3.5 %collective-permute-start.9 = (bf16[1024,256]{1,0:T(8,128)(2,1)S(1)}, bf16[1024,256]{1,0:T(8,128)(2,1)S(1)}, u32[]{:S(2)}, u32[]{:S(2)}) collective-permute-start(bf16[1024,256]{1,0:T(8,128)(2,1)S(1)} %slice.62), channel_id=1, source_target_pairs={{0,12},{1,13},{2,14},{3,15},{4,0},{5,1},{6,2},{7,3},{8,4},{9,5},{1... | collective-permute-start | bytes 1572872 | tf_op jit(solution)/shard_map/ppermute | solution.py:350
  79.7 2.0 %collective-permute-done.10 = bf16[1024,256]{1,0:T(8,128)(2,1)S(1)} collective-permute-done((bf16[1024,256]{1,0:T(8,128)(2,1)S(1)}, bf16[1024,256]{1,0:T(8,128)(2,1)S(1)}, u32[]{:S(2)}, u32[]{:S(2)}) %collective-permute-start.10) | collective-permute-done | bytes 524320 | tf_op jit(solution)/shard_map/ppermute | solution.py:350
  81.7 3.4 %tiles_2.1 = (f32[64,128,256]{2,1,0:T(8,128)S(1)}, bf16[8,16,128,128]{3,2,1,0:T(8,128)(2,1)S(1)}) custom-call(s32[1024]{0:T(1024)S(1)} %bitcast.70, s32[384]{0:T(512)S(1)} %reduce.start_ref.refs_1_, bf16[704,128,128]{2,1,0:T(8,128)(2,1)} %bitcast.80, bf16[16,128,256]{2,1,0:T(8,128)(2,1)S(1)} %bitcast.58, ...), custom_call_target="tpu_custom_call", output_to_operand_aliasing={{0}: (7, {}), {1}: (8, {})} | custom-call | flops 2214592512 | bytes 8650752 | tf_op jit(solution)/shard_map/tiles_2/pallas_call | solution.py:260
  85.1 2.2 %collective-permute-done.8 = bf16[1024,256]{1,0:T(8,128)(2,1)S(1)} collective-permute-done((bf16[1024,256]{1,0:T(8,128)(2,1)S(1)}, bf16[1024,256]{1,0:T(8,128)(2,1)S(1)}, u32[]{:S(2)}, u32[]{:S(2)}) %collective-permute-start.8) | collective-permute-done | bytes 524320 | tf_op jit(solution)/shard_map/ppermute | solution.py:350
  87.3 2.1 %tiles_3.1 = (f32[64,128,256]{2,1,0:T(8,128)S(1)}, bf16[8,16,128,128]{3,2,1,0:T(8,128)(2,1)S(1)}, bf16[8,128,256]{2,1,0:T(8,128)(2,1)S(1)}, bf16[8,128,256]{2,1,...) custom-call(s32[1024]{0:T(1024)S(1)} %bitcast.71, ...), custom_call_target="tpu_custom_call", output_to_operand_aliasing={{0}: (5, {}), {1}: (6, {})} | custom-call | flops 738197504 | bytes 2883584 | tf_op jit(solution)/shard_map/tiles_3/pallas_call | solution.py:260
  89.4 0.1 collective-permute-start.12
  89.5 1.9 %collective-permute-done.12 = bf16[1024,256]{1,0:T(8,128)(2,1)S(1)} collective-permute-done((bf16[1024,256]{1,0:T(8,128)(2,1)S(1)}, bf16[1024,256]{1,0:T(8,128)(2,1)S(1)}, u32[]{:S(2)}, u32[]{:S(2)}) %collective-permute-start.12) | collective-permute-done | bytes 524320 | tf_op jit(solution)/shard_map/ppermute | solution.py:377
  91.4 0.2 fusion.6
  91.6 0.2 collective-permute-start.13
  91.9 0.1 fusion.12
  92.1 2.7 %collective-permute-start.14 = (bf16[512,256]{1,0:T(8,128)(2,1)S(1)}, bf16[512,256]{1,0:T(8,128)(2,1)S(1)}, u32[]{:S(2)}, u32[]{:S(2)}) collective-permute-start(bf16[512,256]{1,0:T(8,128)(2,1)S(1)} %get-tuple-element.70), channel_id=1, source_target_pairs={{0,32},{16,48},{32,64},{48,80},{64,96},{80,112},{96,0},{112,16},{1... | collective-permute-start | bytes 786440 | tf_op jit(solution)/shard_map/ppermute | solution.py:377
  94.8 0.3 collective-permute-done.13
  95.1 0.3 convert_add_fusion.1
  95.5 5.4 %collective-permute-done.14 = bf16[512,256]{1,0:T(8,128)(2,1)S(1)} collective-permute-done((bf16[512,256]{1,0:T(8,128)(2,1)S(1)}, bf16[512,256]{1,0:T(8,128)(2,1)S(1)}, u32[]{:S(2)}, u32[]{:S(2)}) %collective-permute-start.14) | collective-permute-done | bytes 262176 | tf_op jit(solution)/shard_map/ppermute | solution.py:377
  100.9 0.1 fusion.10
  101.0 3.8 %collective-permute-start.15 = (bf16[1024,256]{1,0:T(8,128)(2,1)S(1)}, bf16[1024,256]{1,0:T(8,128)(2,1)S(1)}, u32[]{:S(2)}, u32[]{:S(2)}) collective-permute-start(bf16[1024,256]{1,0:T(8,128)(2,1)S(1)} %pad_maximum_fusion.1), channel_id=1, source_target_pairs={{0,32},{16,48},{32,64},{48,80},{64,96},{80,112},{96,0},{112,16},{1... | collective-permute-start | bytes 1572872 | tf_op jit(solution)/shard_map/ppermute | solution.py:377
  104.8 0.1 fusion.9
  104.9 0.1 collective-permute-start.17
  105.1 0.3 fusion.14
  105.4 10.3 %collective-permute-done.15 = bf16[1024,256]{1,0:T(8,128)(2,1)S(1)} collective-permute-done((bf16[1024,256]{1,0:T(8,128)(2,1)S(1)}, bf16[1024,256]{1,0:T(8,128)(2,1)S(1)}, u32[]{:S(2)}, u32[]{:S(2)}) %collective-permute-start.15) | collective-permute-done | bytes 524320 | tf_op jit(solution)/shard_map/ppermute | solution.py:377
  115.7 3.6 %collective-permute-done.17 = bf16[1024,256]{1,0:T(8,128)(2,1)S(1)} collective-permute-done((bf16[1024,256]{1,0:T(8,128)(2,1)S(1)}, bf16[1024,256]{1,0:T(8,128)(2,1)S(1)}, u32[]{:S(2)}, u32[]{:S(2)}) %collective-permute-start.17) | collective-permute-done | bytes 524320 | tf_op jit(solution)/shard_map/ppermute | solution.py:377
  119.3 1.3 %fusion.2 = bf16[1024,256]{1,0:T(8,128)(2,1)} fusion(f32[1024,256]{1,0:T(8,128)S(1)} %fusion.14, bf16[256,256]{1,0:T(8,128)(2,1)S(1)} %copy-done.6, bf16[1024,256]{1,0:T(8,128)(2,1)S(1)} %collective-permute-done.17, bf16[1024,256]{1,0:T(8,128)(2,1)S(1)} %collective-permute-done.15, bf16[1024,256]{1,0:T(8,128)(2,1)S(1)} %bitcast.82, ...), kind=kOutput, calls=%fused_computation.3 | convolution fusion | flops 137625600 | bytes 3806208 | tf_op jit(solution)/shard_map/dot_general | solution.py:392
  (39 shorter events, 0.6 us)
Async XLA Ops:
  0.0 105.1 %copy-start = (bf16[256,256]{1,0:T(8,128)(2,1)S(1)}, bf16[256,256]{1,0:T(8,128)(2,1)}, u32[]{:S(2)}) copy-start(bf16[256,256]{1,0:T(8,128)(2,1)} %param.17) | copy-start | bytes 393220
  0.0 1.1 copy-start.1
  1.1 0.7 copy-start.4
  1.8 37.1 %copy-start.2 = (s32[1,1,704]{2,1,0:T(1,128)S(1)}, s32[1,1,704]{2,1,0:T(1,128)}, u32[]{:S(2)}) copy-start(s32[1,1,704]{2,1,0:T(1,128)} %param.13) | copy-start | bytes 8452
  1.8 37.1 %copy-start.3 = (s32[1,1,704]{2,1,0:T(1,128)S(1)}, s32[1,1,704]{2,1,0:T(1,128)}, u32[]{:S(2)}) copy-start(s32[1,1,704]{2,1,0:T(1,128)} %param.14) | copy-start | bytes 8452
  34.8 10.5 %collective-permute-start = (bf16[1024,256]{1,0:T(8,128)(2,1)S(1)}, bf16[1024,256]{1,0:T(8,128)(2,1)S(1)}, u32[]{:S(2)}, u32[]{:S(2)}) collective-permute-start(bf16[1024,256]{1,0:T(8,128)(2,1)S(1)} %unpack.1), channel_id=1, source_target_pairs={{0,1},{1,2},{2,3},{3,0},{4,5},{5,6},{6,7},{7,4},{8,9},{9,10},{10,1... | collective-permute-start | bytes 1572872 | tf_op jit(solution)/shard_map/ppermute | solution.py:350
  35.5 9.8 %collective-permute-start.1 = (bf16[1024,256]{1,0:T(8,128)(2,1)S(1)}, bf16[1024,256]{1,0:T(8,128)(2,1)S(1)}, u32[]{:S(2)}, u32[]{:S(2)}) collective-permute-start(bf16[1024,256]{1,0:T(8,128)(2,1)S(1)} %unpack.1), channel_id=1, source_target_pairs={{0,3},{1,0},{2,1},{3,2},{4,7},{5,4},{6,5},{7,6},{8,11},{9,8},{10,9... | collective-permute-start | bytes 1572872 | tf_op jit(solution)/shard_map/ppermute | solution.py:350
  45.3 9.6 %collective-permute-start.2 = (bf16[512,256]{1,0:T(8,128)(2,1)S(1)}, bf16[512,256]{1,0:T(8,128)(2,1)S(1)}, u32[]{:S(2)}, u32[]{:S(2)}) collective-permute-start(bf16[512,256]{1,0:T(8,128)(2,1)S(1)} %slice.59), channel_id=1, source_target_pairs={{0,1},{1,2},{2,3},{3,0},{4,5},{5,6},{6,7},{7,4},{8,9},{9,10},{10,1... | collective-permute-start | bytes 786440 | tf_op jit(solution)/shard_map/ppermute | solution.py:350
  45.4 9.6 %collective-permute-start.3 = (bf16[512,256]{1,0:T(8,128)(2,1)S(1)}, bf16[512,256]{1,0:T(8,128)(2,1)S(1)}, u32[]{:S(2)}, u32[]{:S(2)}) collective-permute-start(bf16[512,256]{1,0:T(8,128)(2,1)S(1)} %slice.60), channel_id=1, source_target_pairs={{0,3},{1,0},{2,1},{3,2},{4,7},{5,4},{6,5},{7,6},{8,11},{9,8},{10,9... | collective-permute-start | bytes 786440 | tf_op jit(solution)/shard_map/ppermute | solution.py:350
  48.7 16.1 %collective-permute-start.6 = (bf16[2048,256]{1,0:T(8,128)(2,1)S(1)}, bf16[2048,256]{1,0:T(8,128)(2,1)S(1)}, u32[]{:S(2)}, u32[]{:S(2)}) collective-permute-start(bf16[2048,256]{1,0:T(8,128)(2,1)S(1)} %pad_maximum_fusion), channel_id=1, source_target_pairs={{0,4},{1,5},{2,6},{3,7},{4,8},{5,9},{6,10},{7,11},{8,12},{9,13},{1... | collective-permute-start | bytes 3145736 | tf_op jit(solution)/shard_map/ppermute | solution.py:350
  49.6 15.2 %collective-permute-start.7 = (bf16[2048,256]{1,0:T(8,128)(2,1)S(1)}, bf16[2048,256]{1,0:T(8,128)(2,1)S(1)}, u32[]{:S(2)}, u32[]{:S(2)}) collective-permute-start(bf16[2048,256]{1,0:T(8,128)(2,1)S(1)} %pad_maximum_fusion), channel_id=1, source_target_pairs={{0,12},{1,13},{2,14},{3,15},{4,0},{5,1},{6,2},{7,3},{8,4},{9,5},{1... | collective-permute-start | bytes 3145736 | tf_op jit(solution)/shard_map/ppermute | solution.py:350
  55.0 21.1 %collective-permute-start.4 = (bf16[2048,256]{1,0:T(8,128)(2,1)S(1)}, bf16[2048,256]{1,0:T(8,128)(2,1)S(1)}, u32[]{:S(2)}, u32[]{:S(2)}) collective-permute-start(bf16[2048,256]{1,0:T(8,128)(2,1)S(1)} %constant_dynamic-update-slice_fusion), channel_id=1, source_target_pairs={{0,4},{1,5},{2,6},{3,7},{4,8},{5,9},{6,10},{7,11},{8,12},{9,13},{1... | collective-permute-start | bytes 3145736 | tf_op jit(solution)/shard_map/ppermute | solution.py:350
  56.7 19.4 %collective-permute-start.5 = (bf16[2048,256]{1,0:T(8,128)(2,1)S(1)}, bf16[2048,256]{1,0:T(8,128)(2,1)S(1)}, u32[]{:S(2)}, u32[]{:S(2)}) collective-permute-start(bf16[2048,256]{1,0:T(8,128)(2,1)S(1)} %constant_dynamic-update-slice_fusion), channel_id=1, source_target_pairs={{0,12},{1,13},{2,14},{3,15},{4,0},{5,1},{6,2},{7,3},{8,4},{9,5},{1... | collective-permute-start | bytes 3145736 | tf_op jit(solution)/shard_map/ppermute | solution.py:350
  64.9 16.8 %collective-permute-start.10 = (bf16[1024,256]{1,0:T(8,128)(2,1)S(1)}, bf16[1024,256]{1,0:T(8,128)(2,1)S(1)}, u32[]{:S(2)}, u32[]{:S(2)}) collective-permute-start(bf16[1024,256]{1,0:T(8,128)(2,1)S(1)} %slice.63), channel_id=1, source_target_pairs={{0,4},{1,5},{2,6},{3,7},{4,8},{5,9},{6,10},{7,11},{8,12},{9,13},{1... | collective-permute-start | bytes 1572872 | tf_op jit(solution)/shard_map/ppermute | solution.py:350
  65.0 16.7 %collective-permute-start.11 = (bf16[1024,256]{1,0:T(8,128)(2,1)S(1)}, bf16[1024,256]{1,0:T(8,128)(2,1)S(1)}, u32[]{:S(2)}, u32[]{:S(2)}) collective-permute-start(bf16[1024,256]{1,0:T(8,128)(2,1)S(1)} %slice.64), channel_id=1, source_target_pairs={{0,12},{1,13},{2,14},{3,15},{4,0},{5,1},{6,2},{7,3},{8,4},{9,5},{1... | collective-permute-start | bytes 1572872 | tf_op jit(solution)/shard_map/ppermute | solution.py:350
  76.1 11.2 %collective-permute-start.8 = (bf16[1024,256]{1,0:T(8,128)(2,1)S(1)}, bf16[1024,256]{1,0:T(8,128)(2,1)S(1)}, u32[]{:S(2)}, u32[]{:S(2)}) collective-permute-start(bf16[1024,256]{1,0:T(8,128)(2,1)S(1)} %slice.61), channel_id=1, source_target_pairs={{0,4},{1,5},{2,6},{3,7},{4,8},{5,9},{6,10},{7,11},{8,12},{9,13},{1... | collective-permute-start | bytes 1572872 | tf_op jit(solution)/shard_map/ppermute | solution.py:350
  76.2 11.1 %collective-permute-start.9 = (bf16[1024,256]{1,0:T(8,128)(2,1)S(1)}, bf16[1024,256]{1,0:T(8,128)(2,1)S(1)}, u32[]{:S(2)}, u32[]{:S(2)}) collective-permute-start(bf16[1024,256]{1,0:T(8,128)(2,1)S(1)} %slice.62), channel_id=1, source_target_pairs={{0,12},{1,13},{2,14},{3,15},{4,0},{5,1},{6,2},{7,3},{8,4},{9,5},{1... | collective-permute-start | bytes 1572872 | tf_op jit(solution)/shard_map/ppermute | solution.py:350
  89.4 2.0 %collective-permute-start.12 = (bf16[1024,256]{1,0:T(8,128)(2,1)S(1)}, bf16[1024,256]{1,0:T(8,128)(2,1)S(1)}, u32[]{:S(2)}, u32[]{:S(2)}) collective-permute-start(bf16[1024,256]{1,0:T(8,128)(2,1)S(1)} %bitcast.76), channel_id=1, source_target_pairs={{0,16},{16,0},{32,48},{48,32},{64,80},{80,64},{96,112},{112,96},{1... | collective-permute-start | bytes 1572872 | tf_op jit(solution)/shard_map/ppermute | solution.py:377
  91.6 3.5 %collective-permute-start.13 = (bf16[3,1024,256]{2,1,0:T(8,128)(2,1)S(1)}, bf16[3,1024,256]{2,1,0:T(8,128)(2,1)S(1)}, u32[]{:S(2)}, u32[]{:S(2)}) collective-permute-start(bf16[3,1024,256]{2,1,0:T(8,128)(2,1)S(1)} %bitcast.75), channel_id=1, source_target_pairs={{0,16},{16,0},{32,48},{48,32},{64,80},{80,64},{96,112},{112,96},{1... | collective-permute-start | bytes 4718600 | tf_op jit(solution)/shard_map/ppermute | solution.py:377
  92.1 8.8 %collective-permute-start.14 = (bf16[512,256]{1,0:T(8,128)(2,1)S(1)}, bf16[512,256]{1,0:T(8,128)(2,1)S(1)}, u32[]{:S(2)}, u32[]{:S(2)}) collective-permute-start(bf16[512,256]{1,0:T(8,128)(2,1)S(1)} %get-tuple-element.70), channel_id=1, source_target_pairs={{0,32},{16,48},{32,64},{48,80},{64,96},{80,112},{96,0},{112,16},{1... | collective-permute-start | bytes 786440 | tf_op jit(solution)/shard_map/ppermute | solution.py:377
  94.8 10.0 %collective-permute-start.16 = (bf16[512,256]{1,0:T(8,128)(2,1)S(1)}, bf16[512,256]{1,0:T(8,128)(2,1)S(1)}, u32[]{:S(2)}, u32[]{:S(2)}) collective-permute-start(bf16[512,256]{1,0:T(8,128)(2,1)S(1)} %get-tuple-element.71), channel_id=1, source_target_pairs={{0,96},{16,112},{32,0},{48,16},{64,32},{80,48},{96,64},{112,80},{1... | collective-permute-start | bytes 786440 | tf_op jit(solution)/shard_map/ppermute | solution.py:377
  95.1 9.9 %copy-start.5 = (s32[1024]{0:T(1024)S(1)}, s32[1024]{0:T(1024)}, u32[]{:S(2)}) copy-start(s32[1024]{0:T(1024)} %param.12) | copy-start | bytes 12292
  95.1 9.9 %copy-start.7 = (bf16[256]{0:T(256)(128)(2,1)S(1)}, bf16[256]{0:T(256)(128)(2,1)}, u32[]{:S(2)}) copy-start(bf16[256]{0:T(256)(128)(2,1)} %param.19) | copy-start | bytes 1540
  95.5 23.8 %copy-start.6 = (bf16[256,256]{1,0:T(8,128)(2,1)S(1)}, bf16[256,256]{1,0:T(8,128)(2,1)}, u32[]{:S(2)}) copy-start(bf16[256,256]{1,0:T(8,128)(2,1)} %param.18) | copy-start | bytes 393220
  101.0 14.7 %collective-permute-start.15 = (bf16[1024,256]{1,0:T(8,128)(2,1)S(1)}, bf16[1024,256]{1,0:T(8,128)(2,1)S(1)}, u32[]{:S(2)}, u32[]{:S(2)}) collective-permute-start(bf16[1024,256]{1,0:T(8,128)(2,1)S(1)} %pad_maximum_fusion.1), channel_id=1, source_target_pairs={{0,32},{16,48},{32,64},{48,80},{64,96},{80,112},{96,0},{112,16},{1... | collective-permute-start | bytes 1572872 | tf_op jit(solution)/shard_map/ppermute | solution.py:377
  104.9 14.4 %collective-permute-start.17 = (bf16[1024,256]{1,0:T(8,128)(2,1)S(1)}, bf16[1024,256]{1,0:T(8,128)(2,1)S(1)}, u32[]{:S(2)}, u32[]{:S(2)}) collective-permute-start(bf16[1024,256]{1,0:T(8,128)(2,1)S(1)} %pad_maximum_fusion.2), channel_id=1, source_target_pairs={{0,96},{16,112},{32,0},{48,16},{64,32},{80,48},{96,64},{112,80},{1... | collective-permute-start | bytes 1572872 | tf_op jit(solution)/shard_map/ppermute | solution.py:377

commit v6 on v5

--- a/solution.py
+++ b/solution.py
@@ -99,9 +99,9 @@
     order_y = ring_order(((source & 3) - y) & 3)
     outer = jnp.where(core == 0, order_z, order_y)
     inner = jnp.where(core == 0, order_y, order_z)
-    stage = jnp.where(outer == 0, 0, jnp.where(inner < 2, 1, 2) + jnp.where(outer == 3, 1, 0))
-    side = (inner & 1) * 8 + jnp.where(outer == 2, 16, jnp.where((outer == 3) & (inner < 2), 32, 0))
-    tile = jnp.where(outer == 0, inner * 8, side) + (col & 7)
+    stage = jnp.where(outer == 0, 0, jnp.where(outer == 3, 3, jnp.where(inner < 2, 1, 2)))
+    side = (inner & 1) * 8 + jnp.where(outer == 2, 16, 0)
+    tile = jnp.where((outer == 0) | (outer == 3), inner * 8, side) + (col & 7)
     owner = row >> 3
     dx = ((owner >> 1) - x) & 3
     order_x = jnp.where(dx == 2, 0, jnp.where(dx == 1, 1, jnp.where(dx == 3, 2, 3)))
@@ -366,9 +366,9 @@
     state = run_tiles(1, *lists, [lo_p, lo_m], state)
     hi_p, hi_m, *state = lax.optimization_barrier((hi_p, hi_m, *state))
     far_hi = [send(hi_p[:rows], 1, 1), send(hi_m[rows:], 1, -1)]
-    state = run_tiles(2, *lists, [hi_p, hi_m, *far_lo], state)
+    state = run_tiles(2, *lists, [hi_p, hi_m], state)
     *_, other_far, mine_far, other_rest, mine_rest = run_tiles(
-        3, *lists, far_hi, state, ((0, 8), (8, 8), (16, 24), (40, 24))
+        3, *lists, far_lo + far_hi, state, ((0, 8), (8, 8), (16, 24), (40, 24))
     )
 
     f32 = jnp.float32
@@ -383,9 +383,15 @@
     got_rest = over(other_rest.reshape(3, rows, width), 0, 1)
     mine_rest = mine_rest.reshape(3, rows, width)
     both = [mine_rest[i].astype(f32) + got_rest[i].astype(f32) for i in range(3)]
-    to_plus = cat(both[0][:half] + from_minus.astype(f32), both[0][half:]).astype(jnp.bfloat16)
-    to_minus = cat(both[1][:half], both[1][half:] + from_plus.astype(f32)).astype(jnp.bfloat16)
-    summed = both[2] + over(to_plus, 1).astype(f32) + over(to_minus, -1).astype(f32)
+    low = over(both[0][half:].astype(jnp.bfloat16), 1)
+    high = over(both[1][:half].astype(jnp.bfloat16), -1)
+    to_plus = (both[0][:half] + from_minus.astype(f32)).astype(jnp.bfloat16)
+    to_minus = (both[1][half:] + from_plus.astype(f32)).astype(jnp.bfloat16)
+    top = both[2][:half] + high.astype(f32)
+    bottom = both[2][half:] + low.astype(f32)
+    top, bottom = lax.optimization_barrier((top, bottom))
+    last_top, last_bottom = over(to_plus, 1), over(to_minus, -1)
+    summed = cat(top + last_top.astype(f32), bottom + last_bottom.astype(f32))
 
     neighbor_mean = (summed / degree.astype(f32)[:, None]).astype(jnp.bfloat16)
     total = jnp.dot(owned, w_self, preferred_element_type=f32)

time: 121 us -> 119 us (0.983)
  waiting for transfers between devices: 37.5 us -> 30.2 us
  starting transfers between devices: 27.1 us -> 29.3 us
  Pallas kernels: 21.9 us -> 24 us
    ppermute x6 -> x8, waiting for transfers between devices: 21.5 us -> 15 us  [over(): return lax.ppermute(v, 'row', row_perm(dx, flip))]
    ppermute x6 -> x8, starting transfers between devices: 6.89 us -> 9.12 us  [over(): return lax.ppermute(v, 'row', row_perm(dx, flip))]
    pallas_call x4, Pallas kernels: 11.9 us -> 13.8 us  [run_tiles(): pl.pallas_call(functools.partial(tiles_kernel, stage, n, outs), out_shape...]
  transfers between devices with their start and end apart: 18 -> 20, of which waited for: 12 -> 12; matrix products, arithmetic and copies ran while one was open for 1% -> 1% of each run, Pallas kernels for 13% -> 13%
where the time goes in v6:
time: 119 us; the launch traced here: 118 us
  waiting for transfers between devices  30.2 us (25%)
  starting transfers between devices  29.3 us (25%)
  blocking collectives  28.4 us (24%)
  Pallas kernels  24 us (20%)
  local copies, waits for them, and re-layouts  2.27 us (2%)
  matrix products  1.47 us (1%)
  other arithmetic  1.25 us (1%)
    all_to_all x1, blocking collectives, per_device(): lax.all_to_all(outgoing.reshape(devices, SLOT_ROWS, width), ('row', 'col'...  28.4 us
    ppermute x12, starting transfers between devices, send(): return lax.ppermute(v, ('row', 'col'), panel_perm(turn, step))  20.2 us
    ppermute x12, waiting for transfers between devices, send(): return lax.ppermute(v, ('row', 'col'), panel_perm(turn, step))  15.2 us
    ppermute x8, waiting for transfers between devices, over(): return lax.ppermute(v, 'row', row_perm(dx, flip))  15 us
    pallas_call x4, Pallas kernels, run_tiles(): pl.pallas_call(functools.partial(tiles_kernel, stage, n, outs), out_shape...  13.8 us
    ppermute x8, starting transfers between devices, over(): return lax.ppermute(v, 'row', row_perm(dx, flip))  9.12 us
    pallas_call x1, Pallas kernels, open_tiles(): pl.pallas_call(open_kernel, out_shape=[pltpu.VMEM((64, t, width), jnp.flo...  3.78 us
    pallas_call x1, Pallas kernels, per_device(): pl.pallas_call(pack_kernel, out_shape=jax.ShapeDtypeStruct((devices * SLO...  2.54 us
  transfers between devices with their start and end apart: 20, of which 12 were waited for; matrix products, arithmetic and copies ran while one was open for 1% of the time, Pallas kernels for 13%

profile of v6, /device:TPU:6, one launch (start us, length us, event | category | flops | bytes accessed | tf_op | source)
XLA Modules:
  0.0 117.9 jit_solution(17963269747415167821)
XLA Ops:
  0.0 1.1 copy-done.1
  1.1 0.7 copy-done.4
  1.8 2.5 %pack.1 = bf16[2048,256]{1,0:T(8,128)(2,1)S(1)} custom-call(s32[1,512]{1,0:T(1,128)S(1)} %bitcast.74, bf16[1024,256]{1,0:T(8,128)(2,1)S(1)} %copy-done.1), custom_call_target="tpu_custom_call" | custom-call | tf_op jit(solution)/shard_map/pack/pallas_call | solution.py:309
  4.3 28.4 %all_to_all.5 = bf16[128,16,256]{2,1,0:T(8,128)(2,1)S(1)} all-to-all(bf16[128,16,256]{2,1,0:T(8,128)(2,1)S(1)} %bitcast.57), channel_id=1, replica_groups=mesh['row'=8,'col'=16] {'row','col'}, dimensions={0} | all-to-all | bytes 2097152 | tf_op jit(solution)/shard_map/all_to_all | solution.py:317
  32.7 2.1 %unpack.1 = bf16[1024,256]{1,0:T(8,128)(2,1)S(1)} custom-call(bf16[2048,256]{1,0:T(8,128)(2,1)S(1)} %bitcast.56), custom_call_target="tpu_custom_call" | custom-call | tf_op jit(solution)/shard_map/unpack/pallas_call | solution.py:325
  34.8 0.7 collective-permute-start
  35.5 2.6 %collective-permute-start.1 = (bf16[1024,256]{1,0:T(8,128)(2,1)S(1)}, bf16[1024,256]{1,0:T(8,128)(2,1)S(1)}, u32[]{:S(2)}, u32[]{:S(2)}) collective-permute-start(bf16[1024,256]{1,0:T(8,128)(2,1)S(1)} %unpack.1), channel_id=1, source_target_pairs={{0,3},{1,0},{2,1},{3,2},{4,7},{5,4},{6,5},{7,6},{8,11},{9,8},{10,9... | collective-permute-start | bytes 1572872 | tf_op jit(solution)/shard_map/ppermute | solution.py:350
  38.7 0.1 pad_add_fusion.where_ref
  38.8 1.9 %plan.1 = (s32[1,1024]{1,0:T(1,128)S(1)}, s32[1,384]{1,0:T(1,128)S(1)}) custom-call(s32[4]{0:T(128)S(1)} %pad_add_fusion.where_ref, s32[1]{0:T(128)} %bitcast.54.count_ref, s32[1,704]{1,0:T(1,128)S(1)} %bitcast.72, s32[1,704]{1,0:T(1,128)S(1)} %bitcast.73), custom_call_target="tpu_custom_call" | custom-call | tf_op jit(solution)/shard_map/plan/pallas_call | solution.py:334
  40.7 3.8 %tiles_open.1 = (f32[64,128,256]{2,1,0:T(8,128)S(1)}, bf16[8,16,128,128]{3,2,1,0:T(8,128)(2,1)S(1)}) custom-call(s32[1024]{0:T(1024)S(1)} %bitcast.67, s32[384]{0:T(512)S(1)} %reduce.start_ref.refs_1_, bf16[704,128,128]{2,1,0:T(8,128)(2,1)} %bitcast.77), custom_call_target="tpu_custom_call" | custom-call | tf_op jit(solution)/shard_map/tiles_open/pallas_call | solution.py:229
  44.5 0.7 collective-permute-done
  45.3 0.1 collective-permute-start.4
  45.4 3.3 %collective-permute-start.5 = (bf16[512,256]{1,0:T(8,128)(2,1)S(1)}, bf16[512,256]{1,0:T(8,128)(2,1)S(1)}, u32[]{:S(2)}, u32[]{:S(2)}) collective-permute-start(bf16[512,256]{1,0:T(8,128)(2,1)S(1)} %slice.66), channel_id=1, source_target_pairs={{0,3},{1,0},{2,1},{3,2},{4,7},{5,4},{6,5},{7,6},{8,11},{9,8},{10,9... | collective-permute-start | bytes 786440 | tf_op jit(solution)/shard_map/ppermute | solution.py:350
  48.7 0.9 collective-permute-start.2
  49.6 2.4 %collective-permute-start.3 = (bf16[2048,256]{1,0:T(8,128)(2,1)S(1)}, bf16[2048,256]{1,0:T(8,128)(2,1)S(1)}, u32[]{:S(2)}, u32[]{:S(2)}) collective-permute-start(bf16[2048,256]{1,0:T(8,128)(2,1)S(1)} %pad_maximum_fusion), channel_id=1, source_target_pairs={{0,12},{1,13},{2,14},{3,15},{4,0},{5,1},{6,2},{7,3},{8,4},{9,5},{1... | collective-permute-start | bytes 3145736 | tf_op jit(solution)/shard_map/ppermute | solution.py:350
  52.1 2.8 %collective-permute-done.4 = bf16[512,256]{1,0:T(8,128)(2,1)S(1)} collective-permute-done((bf16[512,256]{1,0:T(8,128)(2,1)S(1)}, bf16[512,256]{1,0:T(8,128)(2,1)S(1)}, u32[]{:S(2)}, u32[]{:S(2)}) %collective-permute-start.4) | collective-permute-done | bytes 262176 | tf_op jit(solution)/shard_map/ppermute | solution.py:350
  55.0 1.7 %collective-permute-start.8 = (bf16[2048,256]{1,0:T(8,128)(2,1)S(1)}, bf16[2048,256]{1,0:T(8,128)(2,1)S(1)}, u32[]{:S(2)}, u32[]{:S(2)}) collective-permute-start(bf16[2048,256]{1,0:T(8,128)(2,1)S(1)} %constant_dynamic-update-slice_fusion), channel_id=1, source_target_pairs={{0,4},{1,5},{2,6},{3,7},{4,8},{5,9},{6,10},{7,11},{8,12},{9,13},{1... | collective-permute-start | bytes 3145736 | tf_op jit(solution)/shard_map/ppermute | solution.py:350
  56.7 1.6 %collective-permute-start.9 = (bf16[2048,256]{1,0:T(8,128)(2,1)S(1)}, bf16[2048,256]{1,0:T(8,128)(2,1)S(1)}, u32[]{:S(2)}, u32[]{:S(2)}) collective-permute-start(bf16[2048,256]{1,0:T(8,128)(2,1)S(1)} %constant_dynamic-update-slice_fusion), channel_id=1, source_target_pairs={{0,12},{1,13},{2,14},{3,15},{4,0},{5,1},{6,2},{7,3},{8,4},{9,5},{1... | collective-permute-start | bytes 3145736 | tf_op jit(solution)/shard_map/ppermute | solution.py:350
  58.3 3.5 %tiles_0.1 = (f32[64,128,256]{2,1,0:T(8,128)S(1)}, bf16[8,16,128,128]{3,2,1,0:T(8,128)(2,1)S(1)}) custom-call(s32[1024]{0:T(1024)S(1)} %bitcast.68, s32[384]{0:T(512)S(1)} %reduce.start_ref.refs_1_, bf16[704,128,128]{2,1,0:T(8,128)(2,1)} %bitcast.78, bf16[16,128,256]{2,1,0:T(8,128)(2,1)S(1)} %bitcast.55, ...), custom_call_target="tpu_custom_call", output_to_operand_aliasing={{0}: (5, {}), {1}: (6, {})} | custom-call | flops 1476395008 | bytes 5767168 | tf_op jit(solution)/shard_map/tiles_0/pallas_call | solution.py:260
  61.8 3.0 %collective-permute-done.2 = bf16[2048,256]{1,0:T(8,128)(2,1)S(1)} collective-permute-done((bf16[2048,256]{1,0:T(8,128)(2,1)S(1)}, bf16[2048,256]{1,0:T(8,128)(2,1)S(1)}, u32[]{:S(2)}, u32[]{:S(2)}) %collective-permute-start.2) | collective-permute-done | bytes 1048608 | tf_op jit(solution)/shard_map/ppermute | solution.py:350
  64.9 0.1 collective-permute-start.6
  65.0 3.3 %collective-permute-start.7 = (bf16[1024,256]{1,0:T(8,128)(2,1)S(1)}, bf16[1024,256]{1,0:T(8,128)(2,1)S(1)}, u32[]{:S(2)}, u32[]{:S(2)}) collective-permute-start(bf16[1024,256]{1,0:T(8,128)(2,1)S(1)} %slice.68), channel_id=1, source_target_pairs={{0,12},{1,13},{2,14},{3,15},{4,0},{5,1},{6,2},{7,3},{8,4},{9,5},{1... | collective-permute-start | bytes 1572872 | tf_op jit(solution)/shard_map/ppermute | solution.py:350
  68.3 3.5 %tiles_1.1 = (f32[64,128,256]{2,1,0:T(8,128)S(1)}, bf16[8,16,128,128]{3,2,1,0:T(8,128)(2,1)S(1)}) custom-call(s32[1024]{0:T(1024)S(1)} %bitcast.69, s32[384]{0:T(512)S(1)} %reduce.start_ref.refs_1_, bf16[704,128,128]{2,1,0:T(8,128)(2,1)} %bitcast.79, bf16[16,128,256]{2,1,0:T(8,128)(2,1)S(1)} %bitcast.59, ...), custom_call_target="tpu_custom_call", output_to_operand_aliasing={{0}: (5, {}), {1}: (6, {})} | custom-call | flops 1476395008 | bytes 5767168 | tf_op jit(solution)/shard_map/tiles_1/pallas_call | solution.py:260
  71.8 4.3 %collective-permute-done.8 = bf16[2048,256]{1,0:T(8,128)(2,1)S(1)} collective-permute-done((bf16[2048,256]{1,0:T(8,128)(2,1)S(1)}, bf16[2048,256]{1,0:T(8,128)(2,1)S(1)}, u32[]{:S(2)}, u32[]{:S(2)}) %collective-permute-start.8) | collective-permute-done | bytes 1048608 | tf_op jit(solution)/shard_map/ppermute | solution.py:350
  76.1 0.1 collective-permute-start.10
  76.2 3.5 %collective-permute-start.11 = (bf16[1024,256]{1,0:T(8,128)(2,1)S(1)}, bf16[1024,256]{1,0:T(8,128)(2,1)S(1)}, u32[]{:S(2)}, u32[]{:S(2)}) collective-permute-start(bf16[1024,256]{1,0:T(8,128)(2,1)S(1)} %slice.70), channel_id=1, source_target_pairs={{0,12},{1,13},{2,14},{3,15},{4,0},{5,1},{6,2},{7,3},{8,4},{9,5},{1... | collective-permute-start | bytes 1572872 | tf_op jit(solution)/shard_map/ppermute | solution.py:350
  79.7 3.2 %tiles_2.1 = (f32[64,128,256]{2,1,0:T(8,128)S(1)}, bf16[8,16,128,128]{3,2,1,0:T(8,128)(2,1)S(1)}) custom-call(s32[1024]{0:T(1024)S(1)} %bitcast.70, s32[384]{0:T(512)S(1)} %reduce.start_ref.refs_1_, bf16[704,128,128]{2,1,0:T(8,128)(2,1)} %bitcast.80, bf16[16,128,256]{2,1,0:T(8,128)(2,1)S(1)} %bitcast.58, ...), custom_call_target="tpu_custom_call", output_to_operand_aliasing={{0}: (5, {}), {1}: (6, {})} | custom-call | flops 1476395008 | bytes 5767168 | tf_op jit(solution)/shard_map/tiles_2/pallas_call | solution.py:260
  83.0 4.3 %collective-permute-done.10 = bf16[1024,256]{1,0:T(8,128)(2,1)S(1)} collective-permute-done((bf16[1024,256]{1,0:T(8,128)(2,1)S(1)}, bf16[1024,256]{1,0:T(8,128)(2,1)S(1)}, u32[]{:S(2)}, u32[]{:S(2)}) %collective-permute-start.10) | collective-permute-done | bytes 524320 | tf_op jit(solution)/shard_map/ppermute | solution.py:350
  87.3 3.6 %tiles_3.1 = (f32[64,128,256]{2,1,0:T(8,128)S(1)}, bf16[8,16,128,128]{3,2,1,0:T(8,128)(2,1)S(1)}, bf16[8,128,256]{2,1,0:T(8,128)(2,1)S(1)}, bf16[8,128,256]{2,1,...) custom-call(s32[1024]{0:T(1024)S(1)} %bitcast.71, ...), custom_call_target="tpu_custom_call", output_to_operand_aliasing={{0}: (7, {}), {1}: (8, {})} | custom-call | flops 1476395008 | bytes 5767168 | tf_op jit(solution)/shard_map/tiles_3/pallas_call | solution.py:260
  90.9 0.1 collective-permute-start.12
  91.0 1.9 %collective-permute-done.12 = bf16[1024,256]{1,0:T(8,128)(2,1)S(1)} collective-permute-done((bf16[1024,256]{1,0:T(8,128)(2,1)S(1)}, bf16[1024,256]{1,0:T(8,128)(2,1)S(1)}, u32[]{:S(2)}, u32[]{:S(2)}) %collective-permute-start.12) | collective-permute-done | bytes 524320 | tf_op jit(solution)/shard_map/ppermute | solution.py:377
  92.9 0.2 fusion.4
  93.1 0.2 collective-permute-start.13
  93.3 0.3 fusion.12
  93.6 0.1 fusion.10
  93.8 2.1 %collective-permute-start.16 = (bf16[512,256]{1,0:T(8,128)(2,1)S(1)}, bf16[512,256]{1,0:T(8,128)(2,1)S(1)}, u32[]{:S(2)}, u32[]{:S(2)}) collective-permute-start(bf16[512,256]{1,0:T(8,128)(2,1)S(1)} %get-tuple-element.77), channel_id=1, source_target_pairs={{0,32},{16,48},{32,64},{48,80},{64,96},{80,112},{96,0},{112,16},{1... | collective-permute-start | bytes 786440 | tf_op jit(solution)/shard_map/ppermute | solution.py:377
  96.0 0.6 collective-permute-done.13
  96.6 0.5 convert_add_fusion
  97.2 0.2 collective-permute-start.14
  97.4 3.2 %collective-permute-start.15 = (bf16[512,256]{1,0:T(8,128)(2,1)S(1)}, bf16[512,256]{1,0:T(8,128)(2,1)S(1)}, u32[]{:S(2)}, u32[]{:S(2)}) collective-permute-start(bf16[512,256]{1,0:T(8,128)(2,1)S(1)} %slice.113), channel_id=1, source_target_pairs={{0,32},{16,48},{32,64},{48,80},{64,96},{80,112},{96,0},{112,16},{1... | collective-permute-start | bytes 786440 | tf_op jit(solution)/shard_map/ppermute | solution.py:377
  100.6 2.5 %collective-permute-done.16 = bf16[512,256]{1,0:T(8,128)(2,1)S(1)} collective-permute-done((bf16[512,256]{1,0:T(8,128)(2,1)S(1)}, bf16[512,256]{1,0:T(8,128)(2,1)S(1)}, u32[]{:S(2)}, u32[]{:S(2)}) %collective-permute-start.16) | collective-permute-done | bytes 262176 | tf_op jit(solution)/shard_map/ppermute | solution.py:377
  103.1 3.3 %collective-permute-start.17 = (bf16[512,256]{1,0:T(8,128)(2,1)S(1)}, bf16[512,256]{1,0:T(8,128)(2,1)S(1)}, u32[]{:S(2)}, u32[]{:S(2)}) collective-permute-start(bf16[512,256]{1,0:T(8,128)(2,1)S(1)} %fusion.7), channel_id=1, source_target_pairs={{0,32},{16,48},{32,64},{48,80},{64,96},{80,112},{96,0},{112,16},{1... | collective-permute-start | bytes 786440 | tf_op jit(solution)/shard_map/ppermute | solution.py:377
  106.4 0.1 collective-permute-start.19
  106.5 5.4 %collective-permute-done.14 = bf16[512,256]{1,0:T(8,128)(2,1)S(1)} collective-permute-done((bf16[512,256]{1,0:T(8,128)(2,1)S(1)}, bf16[512,256]{1,0:T(8,128)(2,1)S(1)}, u32[]{:S(2)}, u32[]{:S(2)}) %collective-permute-start.14) | collective-permute-done | bytes 262176 | tf_op jit(solution)/shard_map/ppermute | solution.py:377
  111.9 0.1 slice_add_fusion.2
  112.0 1.7 %collective-permute-done.17 = bf16[512,256]{1,0:T(8,128)(2,1)S(1)} collective-permute-done((bf16[512,256]{1,0:T(8,128)(2,1)S(1)}, bf16[512,256]{1,0:T(8,128)(2,1)S(1)}, u32[]{:S(2)}, u32[]{:S(2)}) %collective-permute-start.17) | collective-permute-done | bytes 262176 | tf_op jit(solution)/shard_map/ppermute | solution.py:377
  113.8 2.9 %collective-permute-done.19 = bf16[512,256]{1,0:T(8,128)(2,1)S(1)} collective-permute-done((bf16[512,256]{1,0:T(8,128)(2,1)S(1)}, bf16[512,256]{1,0:T(8,128)(2,1)S(1)}, u32[]{:S(2)}, u32[]{:S(2)}) %collective-permute-start.19) | collective-permute-done | bytes 262176 | tf_op jit(solution)/shard_map/ppermute | solution.py:377
  116.7 1.2 fusion.2
  (44 shorter events, 0.8 us)
Async XLA Ops:
  0.0 93.3 %copy-start = (bf16[256,256]{1,0:T(8,128)(2,1)S(1)}, bf16[256,256]{1,0:T(8,128)(2,1)}, u32[]{:S(2)}) copy-start(bf16[256,256]{1,0:T(8,128)(2,1)} %param.17) | copy-start | bytes 393220
  0.0 1.1 copy-start.1
  1.1 0.7 copy-start.4
  1.8 37.1 %copy-start.2 = (s32[1,1,704]{2,1,0:T(1,128)S(1)}, s32[1,1,704]{2,1,0:T(1,128)}, u32[]{:S(2)}) copy-start(s32[1,1,704]{2,1,0:T(1,128)} %param.13) | copy-start | bytes 8452
  1.8 37.1 %copy-start.3 = (s32[1,1,704]{2,1,0:T(1,128)S(1)}, s32[1,1,704]{2,1,0:T(1,128)}, u32[]{:S(2)}) copy-start(s32[1,1,704]{2,1,0:T(1,128)} %param.14) | copy-start | bytes 8452
  34.8 10.5 %collective-permute-start = (bf16[1024,256]{1,0:T(8,128)(2,1)S(1)}, bf16[1024,256]{1,0:T(8,128)(2,1)S(1)}, u32[]{:S(2)}, u32[]{:S(2)}) collective-permute-start(bf16[1024,256]{1,0:T(8,128)(2,1)S(1)} %unpack.1), channel_id=1, source_target_pairs={{0,1},{1,2},{2,3},{3,0},{4,5},{5,6},{6,7},{7,4},{8,9},{9,10},{10,1... | collective-permute-start | bytes 1572872 | tf_op jit(solution)/shard_map/ppermute | solution.py:350
  35.5 9.8 %collective-permute-start.1 = (bf16[1024,256]{1,0:T(8,128)(2,1)S(1)}, bf16[1024,256]{1,0:T(8,128)(2,1)S(1)}, u32[]{:S(2)}, u32[]{:S(2)}) collective-permute-start(bf16[1024,256]{1,0:T(8,128)(2,1)S(1)} %unpack.1), channel_id=1, source_target_pairs={{0,3},{1,0},{2,1},{3,2},{4,7},{5,4},{6,5},{7,6},{8,11},{9,8},{10,9... | collective-permute-start | bytes 1572872 | tf_op jit(solution)/shard_map/ppermute | solution.py:350
  45.3 9.6 %collective-permute-start.4 = (bf16[512,256]{1,0:T(8,128)(2,1)S(1)}, bf16[512,256]{1,0:T(8,128)(2,1)S(1)}, u32[]{:S(2)}, u32[]{:S(2)}) collective-permute-start(bf16[512,256]{1,0:T(8,128)(2,1)S(1)} %slice.65), channel_id=1, source_target_pairs={{0,1},{1,2},{2,3},{3,0},{4,5},{5,6},{6,7},{7,4},{8,9},{9,10},{10,1... | collective-permute-start | bytes 786440 | tf_op jit(solution)/shard_map/ppermute | solution.py:350
  45.4 9.6 %collective-permute-start.5 = (bf16[512,256]{1,0:T(8,128)(2,1)S(1)}, bf16[512,256]{1,0:T(8,128)(2,1)S(1)}, u32[]{:S(2)}, u32[]{:S(2)}) collective-permute-start(bf16[512,256]{1,0:T(8,128)(2,1)S(1)} %slice.66), channel_id=1, source_target_pairs={{0,3},{1,0},{2,1},{3,2},{4,7},{5,4},{6,5},{7,6},{8,11},{9,8},{10,9... | collective-permute-start | bytes 786440 | tf_op jit(solution)/shard_map/ppermute | solution.py:350
  48.7 16.1 %collective-permute-start.2 = (bf16[2048,256]{1,0:T(8,128)(2,1)S(1)}, bf16[2048,256]{1,0:T(8,128)(2,1)S(1)}, u32[]{:S(2)}, u32[]{:S(2)}) collective-permute-start(bf16[2048,256]{1,0:T(8,128)(2,1)S(1)} %pad_maximum_fusion), channel_id=1, source_target_pairs={{0,4},{1,5},{2,6},{3,7},{4,8},{5,9},{6,10},{7,11},{8,12},{9,13},{1... | collective-permute-start | bytes 3145736 | tf_op jit(solution)/shard_map/ppermute | solution.py:350
  49.6 15.2 %collective-permute-start.3 = (bf16[2048,256]{1,0:T(8,128)(2,1)S(1)}, bf16[2048,256]{1,0:T(8,128)(2,1)S(1)}, u32[]{:S(2)}, u32[]{:S(2)}) collective-permute-start(bf16[2048,256]{1,0:T(8,128)(2,1)S(1)} %pad_maximum_fusion), channel_id=1, source_target_pairs={{0,12},{1,13},{2,14},{3,15},{4,0},{5,1},{6,2},{7,3},{8,4},{9,5},{1... | collective-permute-start | bytes 3145736 | tf_op jit(solution)/shard_map/ppermute | solution.py:350
  55.0 21.1 %collective-permute-start.8 = (bf16[2048,256]{1,0:T(8,128)(2,1)S(1)}, bf16[2048,256]{1,0:T(8,128)(2,1)S(1)}, u32[]{:S(2)}, u32[]{:S(2)}) collective-permute-start(bf16[2048,256]{1,0:T(8,128)(2,1)S(1)} %constant_dynamic-update-slice_fusion), channel_id=1, source_target_pairs={{0,4},{1,5},{2,6},{3,7},{4,8},{5,9},{6,10},{7,11},{8,12},{9,13},{1... | collective-permute-start | bytes 3145736 | tf_op jit(solution)/shard_map/ppermute | solution.py:350
  56.7 19.4 %collective-permute-start.9 = (bf16[2048,256]{1,0:T(8,128)(2,1)S(1)}, bf16[2048,256]{1,0:T(8,128)(2,1)S(1)}, u32[]{:S(2)}, u32[]{:S(2)}) collective-permute-start(bf16[2048,256]{1,0:T(8,128)(2,1)S(1)} %constant_dynamic-update-slice_fusion), channel_id=1, source_target_pairs={{0,12},{1,13},{2,14},{3,15},{4,0},{5,1},{6,2},{7,3},{8,4},{9,5},{1... | collective-permute-start | bytes 3145736 | tf_op jit(solution)/shard_map/ppermute | solution.py:350
  64.9 18.1 %collective-permute-start.6 = (bf16[1024,256]{1,0:T(8,128)(2,1)S(1)}, bf16[1024,256]{1,0:T(8,128)(2,1)S(1)}, u32[]{:S(2)}, u32[]{:S(2)}) collective-permute-start(bf16[1024,256]{1,0:T(8,128)(2,1)S(1)} %slice.67), channel_id=1, source_target_pairs={{0,4},{1,5},{2,6},{3,7},{4,8},{5,9},{6,10},{7,11},{8,12},{9,13},{1... | collective-permute-start | bytes 1572872 | tf_op jit(solution)/shard_map/ppermute | solution.py:350
  65.0 18.0 %collective-permute-start.7 = (bf16[1024,256]{1,0:T(8,128)(2,1)S(1)}, bf16[1024,256]{1,0:T(8,128)(2,1)S(1)}, u32[]{:S(2)}, u32[]{:S(2)}) collective-permute-start(bf16[1024,256]{1,0:T(8,128)(2,1)S(1)} %slice.68), channel_id=1, source_target_pairs={{0,12},{1,13},{2,14},{3,15},{4,0},{5,1},{6,2},{7,3},{8,4},{9,5},{1... | collective-permute-start | bytes 1572872 | tf_op jit(solution)/shard_map/ppermute | solution.py:350
  76.1 11.2 %collective-permute-start.10 = (bf16[1024,256]{1,0:T(8,128)(2,1)S(1)}, bf16[1024,256]{1,0:T(8,128)(2,1)S(1)}, u32[]{:S(2)}, u32[]{:S(2)}) collective-permute-start(bf16[1024,256]{1,0:T(8,128)(2,1)S(1)} %slice.69), channel_id=1, source_target_pairs={{0,4},{1,5},{2,6},{3,7},{4,8},{5,9},{6,10},{7,11},{8,12},{9,13},{1... | collective-permute-start | bytes 1572872 | tf_op jit(solution)/shard_map/ppermute | solution.py:350
  76.2 11.1 %collective-permute-start.11 = (bf16[1024,256]{1,0:T(8,128)(2,1)S(1)}, bf16[1024,256]{1,0:T(8,128)(2,1)S(1)}, u32[]{:S(2)}, u32[]{:S(2)}) collective-permute-start(bf16[1024,256]{1,0:T(8,128)(2,1)S(1)} %slice.70), channel_id=1, source_target_pairs={{0,12},{1,13},{2,14},{3,15},{4,0},{5,1},{6,2},{7,3},{8,4},{9,5},{1... | collective-permute-start | bytes 1572872 | tf_op jit(solution)/shard_map/ppermute | solution.py:350
  87.3 6.0 %copy-start.5 = (s32[1024]{0:T(1024)S(1)}, s32[1024]{0:T(1024)}, u32[]{:S(2)}) copy-start(s32[1024]{0:T(1024)} %param.12) | copy-start | bytes 12292
  87.3 6.0 %copy-start.7 = (bf16[256]{0:T(256)(128)(2,1)S(1)}, bf16[256]{0:T(256)(128)(2,1)}, u32[]{:S(2)}) copy-start(bf16[256]{0:T(256)(128)(2,1)} %param.19) | copy-start | bytes 1540
  90.9 2.0 %collective-permute-start.12 = (bf16[1024,256]{1,0:T(8,128)(2,1)S(1)}, bf16[1024,256]{1,0:T(8,128)(2,1)S(1)}, u32[]{:S(2)}, u32[]{:S(2)}) collective-permute-start(bf16[1024,256]{1,0:T(8,128)(2,1)S(1)} %bitcast.76), channel_id=1, source_target_pairs={{0,16},{16,0},{32,48},{48,32},{64,80},{80,64},{96,112},{112,96},{1... | collective-permute-start | bytes 1572872 | tf_op jit(solution)/shard_map/ppermute | solution.py:377
  93.1 3.5 %collective-permute-start.13 = (bf16[3,1024,256]{2,1,0:T(8,128)(2,1)S(1)}, bf16[3,1024,256]{2,1,0:T(8,128)(2,1)S(1)}, u32[]{:S(2)}, u32[]{:S(2)}) collective-permute-start(bf16[3,1024,256]{2,1,0:T(8,128)(2,1)S(1)} %bitcast.75), channel_id=1, source_target_pairs={{0,16},{16,0},{32,48},{48,32},{64,80},{80,64},{96,112},{112,96},{1... | collective-permute-start | bytes 4718600 | tf_op jit(solution)/shard_map/ppermute | solution.py:377
  93.8 9.2 %collective-permute-start.16 = (bf16[512,256]{1,0:T(8,128)(2,1)S(1)}, bf16[512,256]{1,0:T(8,128)(2,1)S(1)}, u32[]{:S(2)}, u32[]{:S(2)}) collective-permute-start(bf16[512,256]{1,0:T(8,128)(2,1)S(1)} %get-tuple-element.77), channel_id=1, source_target_pairs={{0,32},{16,48},{32,64},{48,80},{64,96},{80,112},{96,0},{112,16},{1... | collective-permute-start | bytes 786440 | tf_op jit(solution)/shard_map/ppermute | solution.py:377
  95.9 10.5 %collective-permute-start.18 = (bf16[512,256]{1,0:T(8,128)(2,1)S(1)}, bf16[512,256]{1,0:T(8,128)(2,1)S(1)}, u32[]{:S(2)}, u32[]{:S(2)}) collective-permute-start(bf16[512,256]{1,0:T(8,128)(2,1)S(1)} %get-tuple-element.78), channel_id=1, source_target_pairs={{0,96},{16,112},{32,0},{48,16},{64,32},{80,48},{96,64},{112,80},{1... | collective-permute-start | bytes 786440 | tf_op jit(solution)/shard_map/ppermute | solution.py:377
  97.1 19.6 %copy-start.6 = (bf16[256,256]{1,0:T(8,128)(2,1)S(1)}, bf16[256,256]{1,0:T(8,128)(2,1)}, u32[]{:S(2)}) copy-start(bf16[256,256]{1,0:T(8,128)(2,1)} %param.18) | copy-start | bytes 393220
  97.2 14.7 %collective-permute-start.14 = (bf16[512,256]{1,0:T(8,128)(2,1)S(1)}, bf16[512,256]{1,0:T(8,128)(2,1)S(1)}, u32[]{:S(2)}, u32[]{:S(2)}) collective-permute-start(bf16[512,256]{1,0:T(8,128)(2,1)S(1)} %slice.114), channel_id=1, source_target_pairs={{0,96},{16,112},{32,0},{48,16},{64,32},{80,48},{96,64},{112,80},{1... | collective-permute-start | bytes 786440 | tf_op jit(solution)/shard_map/ppermute | solution.py:377
  97.4 14.5 %collective-permute-start.15 = (bf16[512,256]{1,0:T(8,128)(2,1)S(1)}, bf16[512,256]{1,0:T(8,128)(2,1)S(1)}, u32[]{:S(2)}, u32[]{:S(2)}) collective-permute-start(bf16[512,256]{1,0:T(8,128)(2,1)S(1)} %slice.113), channel_id=1, source_target_pairs={{0,32},{16,48},{32,64},{48,80},{64,96},{80,112},{96,0},{112,16},{1... | collective-permute-start | bytes 786440 | tf_op jit(solution)/shard_map/ppermute | solution.py:377
  103.1 10.6 %collective-permute-start.17 = (bf16[512,256]{1,0:T(8,128)(2,1)S(1)}, bf16[512,256]{1,0:T(8,128)(2,1)S(1)}, u32[]{:S(2)}, u32[]{:S(2)}) collective-permute-start(bf16[512,256]{1,0:T(8,128)(2,1)S(1)} %fusion.7), channel_id=1, source_target_pairs={{0,32},{16,48},{32,64},{48,80},{64,96},{80,112},{96,0},{112,16},{1... | collective-permute-start | bytes 786440 | tf_op jit(solution)/shard_map/ppermute | solution.py:377
  106.4 10.2 %collective-permute-start.19 = (bf16[512,256]{1,0:T(8,128)(2,1)S(1)}, bf16[512,256]{1,0:T(8,128)(2,1)S(1)}, u32[]{:S(2)}, u32[]{:S(2)}) collective-permute-start(bf16[512,256]{1,0:T(8,128)(2,1)S(1)} %fusion.6), channel_id=1, source_target_pairs={{0,96},{16,112},{32,0},{48,16},{64,32},{80,48},{96,64},{112,80},{1... | collective-permute-start | bytes 786440 | tf_op jit(solution)/shard_map/ppermute | solution.py:377

commit v7 on v6

--- a/solution.py
+++ b/solution.py
@@ -27,7 +27,12 @@
     return jnp.where(mask, 1.0, 0.0).astype(jnp.bfloat16)
 
 
-def pack_kernel(home_ref, table_ref, out_ref):
+def pack_kernel(home_hbm, table_hbm, out_ref, home_ref, table_ref, sem):
+    home_copy = pltpu.make_async_copy(home_hbm, home_ref, sem.at[0])
+    table_copy = pltpu.make_async_copy(table_hbm, table_ref, sem.at[1])
+    home_copy.start()
+    table_copy.start()
+    home_copy.wait()
     rows = table_ref.shape[0]
     blocks = home_ref.shape[1]
     home = home_ref[...]
@@ -48,6 +53,7 @@
     place = dest * SLOT_ROWS + rank
     outs = out_ref.shape[0]
     spread = onehot(iota((outs, rows), 0) == place)
+    table_copy.wait()
     data = jnp.dot(spread, table_ref[...], preferred_element_type=jnp.float32)
     lane = iota((256, rows), 0)
     high = jnp.broadcast_to((parts[2:3] + 1).astype(jnp.float32), (256, rows))
@@ -220,6 +226,29 @@
         pl.when((last + i < total) & (last + i >= fetched))(
             functools.partial(arrive, last + i, weights, wbuf, wsem)
         )
+
+
+def round_kernel(outs, acc, *out_refs):
+    for out, (lo, n) in zip(out_refs, outs):
+
+        def give(i, _, out=out, lo=lo):
+            out[i] = acc[lo + i].astype(out.dtype)
+            return 0
+
+        lax.fori_loop(0, n, give, 0)
+
+
+def round_rows(acc, outs):
+    vmem = pl.BlockSpec(memory_space=pltpu.VMEM)
+    return pl.pallas_call(
+        functools.partial(round_kernel, outs),
+        out_shape=[pltpu.VMEM((n, *acc.shape[1:]), jnp.bfloat16) for _, n in outs],
+        in_specs=[vmem],
+        out_specs=[vmem] * len(outs),
+        compiler_params=pltpu.CompilerParams(vmem_limit_bytes=VMEM_TILES),
+        cost_estimate=pl.CostEstimate(flops=1 << 22, bytes_accessed=12 * MB, transcendentals=0),
+        name="round_rows",
+    )(acc)
 
 
 def open_tiles(code, start, weights, width):
@@ -309,9 +338,14 @@
     outgoing = pl.pallas_call(
         pack_kernel,
         out_shape=jax.ShapeDtypeStruct((devices * SLOT_ROWS, width), jnp.bfloat16),
-        in_specs=[vmem, vmem],
+        in_specs=[pl.BlockSpec(memory_space=pl.ANY)] * 2,
         out_specs=vmem,
-        compiler_params=big,
+        scratch_shapes=[
+            pltpu.VMEM((1, home.shape[0]), jnp.int32),
+            pltpu.VMEM(table.shape, jnp.bfloat16),
+            pltpu.SemaphoreType.DMA((2,)),
+        ],
+        compiler_params=pltpu.CompilerParams(vmem_limit_bytes=60 * MB),
         name="pack",
     )(home.reshape(1, -1), table)
     incoming = lax.all_to_all(
@@ -367,9 +401,10 @@
     hi_p, hi_m, *state = lax.optimization_barrier((hi_p, hi_m, *state))
     far_hi = [send(hi_p[:rows], 1, 1), send(hi_m[rows:], 1, -1)]
     state = run_tiles(2, *lists, [hi_p, hi_m], state)
-    *_, other_far, mine_far, other_rest, mine_rest = run_tiles(
-        3, *lists, far_lo + far_hi, state, ((0, 8), (8, 8), (16, 24), (40, 24))
-    )
+    sums, _, other_far, mine_far = run_tiles(
+        3, *lists, far_lo + far_hi, state, ((0, 8), (8, 8))
+    )
+    other_rest, mine_rest = round_rows(sums, ((16, 24), (40, 24)))
 
     f32 = jnp.float32
 

time: 119 us -> 120 us (level)
  local copies, waits for them, and re-layouts: 2.27 us -> 0.48 us
  Pallas kernels: 24 us -> 25.6 us
    pallas_call x1, Pallas kernels: 2.54 us -> 5.34 us  [per_device(): pl.pallas_call(pack_kernel, out_shape=jax.ShapeDtypeStruct((devices * SLO...]
    unnamed x18 -> x14, local copies, waits for them, and re-layouts: 1.84 us -> 0.08 us
    pallas_call x4, Pallas kernels: 13.8 us -> 12.1 us  [run_tiles(): pl.pallas_call(functools.partial(tiles_kernel, stage, n, outs), out_shape...]
  transfers between devices with their start and end apart: 20 -> 20, of which waited for: 12 -> 11; matrix products, arithmetic and copies ran while one was open for 1% -> 1% of each run, Pallas kernels for 13% -> 13%
where the time goes in v7:
time: 120 us; the launch traced here: 119 us
  starting transfers between devices  30.5 us (25%)
  waiting for transfers between devices  30.1 us (25%)
  blocking collectives  28.6 us (24%)
  Pallas kernels  25.6 us (21%)
  matrix products  1.47 us (1%)
  other arithmetic  1.24 us (1%)
    all_to_all x1, blocking collectives, per_device(): lax.all_to_all(outgoing.reshape(devices, SLOT_ROWS, width), ('row', 'col'...  28.6 us
    ppermute x12, starting transfers between devices, send(): return lax.ppermute(v, ('row', 'col'), panel_perm(turn, step))  20.2 us
    ppermute x12, waiting for transfers between devices, send(): return lax.ppermute(v, ('row', 'col'), panel_perm(turn, step))  16.1 us
    ppermute x8, waiting for transfers between devices, over(): return lax.ppermute(v, 'row', row_perm(dx, flip))  14 us
    pallas_call x4, Pallas kernels, run_tiles(): pl.pallas_call(functools.partial(tiles_kernel, stage, n, outs), out_shape...  12.1 us
    ppermute x8, starting transfers between devices, over(): return lax.ppermute(v, 'row', row_perm(dx, flip))  10.3 us
    pallas_call x1, Pallas kernels, per_device(): pl.pallas_call(pack_kernel, out_shape=jax.ShapeDtypeStruct((devices * SLO...  5.34 us
    pallas_call x1, Pallas kernels, open_tiles(): pl.pallas_call(open_kernel, out_shape=[pltpu.VMEM((64, t, width), jnp.flo...  3.75 us
  transfers between devices with their start and end apart: 20, of which 11 were waited for; matrix products, arithmetic and copies ran while one was open for 1% of the time, Pallas kernels for 13%

profile of v7, /device:TPU:6, one launch (start us, length us, event | category | flops | bytes accessed | tf_op | source)
XLA Modules:
  0.0 119.0 jit_solution(6206817568895769905)
XLA Ops:
  0.0 5.3 %pack.1 = bf16[2048,256]{1,0:T(8,128)(2,1)} custom-call(s32[1,512]{1,0:T(1,128)} %bitcast.81, bf16[1024,256]{1,0:T(8,128)(2,1)} %table_hbm.1), custom_call_target="tpu_custom_call" | custom-call | tf_op jit(solution)/shard_map/pack/pallas_call | solution.py:338
  5.4 28.6 %all_to_all.5 = bf16[128,16,256]{2,1,0:T(8,128)(2,1)S(1)} all-to-all(bf16[128,16,256]{2,1,0:T(8,128)(2,1)} %bitcast.80), channel_id=1, replica_groups=mesh['row'=8,'col'=16] {'row','col'}, dimensions={0} | all-to-all | bytes 2097152 | tf_op jit(solution)/shard_map/all_to_all | solution.py:351
  34.0 2.1 %unpack.1 = bf16[1024,256]{1,0:T(8,128)(2,1)S(1)} custom-call(bf16[2048,256]{1,0:T(8,128)(2,1)S(1)} %bitcast.56), custom_call_target="tpu_custom_call" | custom-call | tf_op jit(solution)/shard_map/unpack/pallas_call | solution.py:359
  36.0 0.7 collective-permute-start
  36.7 2.6 %collective-permute-start.1 = (bf16[1024,256]{1,0:T(8,128)(2,1)S(1)}, bf16[1024,256]{1,0:T(8,128)(2,1)S(1)}, u32[]{:S(2)}, u32[]{:S(2)}) collective-permute-start(bf16[1024,256]{1,0:T(8,128)(2,1)S(1)} %unpack.1), channel_id=1, source_target_pairs={{0,3},{1,0},{2,1},{3,2},{4,7},{5,4},{6,5},{7,6},{8,11},{9,8},{10,9... | collective-permute-start | bytes 1572872 | tf_op jit(solution)/shard_map/ppermute | solution.py:384
  40.0 0.1 pad_add_fusion.where_ref
  40.1 1.9 %plan.1 = (s32[1,1024]{1,0:T(1,128)S(1)}, s32[1,384]{1,0:T(1,128)S(1)}) custom-call(s32[4]{0:T(128)S(1)} %pad_add_fusion.where_ref, s32[1]{0:T(128)} %bitcast.54.count_ref, s32[1,704]{1,0:T(1,128)S(1)} %bitcast.71, s32[1,704]{1,0:T(1,128)S(1)} %bitcast.72), custom_call_target="tpu_custom_call" | custom-call | tf_op jit(solution)/shard_map/plan/pallas_call | solution.py:368
  42.0 3.7 %tiles_open.1 = (f32[64,128,256]{2,1,0:T(8,128)S(1)}, bf16[8,16,128,128]{3,2,1,0:T(8,128)(2,1)S(1)}) custom-call(s32[1024]{0:T(1024)S(1)} %bitcast.66, s32[384]{0:T(512)S(1)} %reduce.start_ref.refs_1_, bf16[704,128,128]{2,1,0:T(8,128)(2,1)} %bitcast.75), custom_call_target="tpu_custom_call" | custom-call | tf_op jit(solution)/shard_map/tiles_open/pallas_call | solution.py:258
  45.8 0.7 collective-permute-done
  46.5 0.1 collective-permute-start.4
  46.6 3.3 %collective-permute-start.5 = (bf16[512,256]{1,0:T(8,128)(2,1)S(1)}, bf16[512,256]{1,0:T(8,128)(2,1)S(1)}, u32[]{:S(2)}, u32[]{:S(2)}) collective-permute-start(bf16[512,256]{1,0:T(8,128)(2,1)S(1)} %slice.66), channel_id=1, source_target_pairs={{0,3},{1,0},{2,1},{3,2},{4,7},{5,4},{6,5},{7,6},{8,11},{9,8},{10,9... | collective-permute-start | bytes 786440 | tf_op jit(solution)/shard_map/ppermute | solution.py:384
  50.0 0.9 collective-permute-start.2
  50.9 2.4 %collective-permute-start.3 = (bf16[2048,256]{1,0:T(8,128)(2,1)S(1)}, bf16[2048,256]{1,0:T(8,128)(2,1)S(1)}, u32[]{:S(2)}, u32[]{:S(2)}) collective-permute-start(bf16[2048,256]{1,0:T(8,128)(2,1)S(1)} %pad_maximum_fusion), channel_id=1, source_target_pairs={{0,12},{1,13},{2,14},{3,15},{4,0},{5,1},{6,2},{7,3},{8,4},{9,5},{1... | collective-permute-start | bytes 3145736 | tf_op jit(solution)/shard_map/ppermute | solution.py:384
  53.4 2.8 %collective-permute-done.4 = bf16[512,256]{1,0:T(8,128)(2,1)S(1)} collective-permute-done((bf16[512,256]{1,0:T(8,128)(2,1)S(1)}, bf16[512,256]{1,0:T(8,128)(2,1)S(1)}, u32[]{:S(2)}, u32[]{:S(2)}) %collective-permute-start.4) | collective-permute-done | bytes 262176 | tf_op jit(solution)/shard_map/ppermute | solution.py:384
  56.3 1.7 %collective-permute-start.8 = (bf16[2048,256]{1,0:T(8,128)(2,1)S(1)}, bf16[2048,256]{1,0:T(8,128)(2,1)S(1)}, u32[]{:S(2)}, u32[]{:S(2)}) collective-permute-start(bf16[2048,256]{1,0:T(8,128)(2,1)S(1)} %constant_dynamic-update-slice_fusion), channel_id=1, source_target_pairs={{0,4},{1,5},{2,6},{3,7},{4,8},{5,9},{6,10},{7,11},{8,12},{9,13},{1... | collective-permute-start | bytes 3145736 | tf_op jit(solution)/shard_map/ppermute | solution.py:384
  57.9 1.6 %collective-permute-start.9 = (bf16[2048,256]{1,0:T(8,128)(2,1)S(1)}, bf16[2048,256]{1,0:T(8,128)(2,1)S(1)}, u32[]{:S(2)}, u32[]{:S(2)}) collective-permute-start(bf16[2048,256]{1,0:T(8,128)(2,1)S(1)} %constant_dynamic-update-slice_fusion), channel_id=1, source_target_pairs={{0,12},{1,13},{2,14},{3,15},{4,0},{5,1},{6,2},{7,3},{8,4},{9,5},{1... | collective-permute-start | bytes 3145736 | tf_op jit(solution)/shard_map/ppermute | solution.py:384
  59.6 3.5 %tiles_0.1 = (f32[64,128,256]{2,1,0:T(8,128)S(1)}, bf16[8,16,128,128]{3,2,1,0:T(8,128)(2,1)S(1)}) custom-call(s32[1024]{0:T(1024)S(1)} %bitcast.67, s32[384]{0:T(512)S(1)} %reduce.start_ref.refs_1_, bf16[704,128,128]{2,1,0:T(8,128)(2,1)} %bitcast.76, bf16[16,128,256]{2,1,0:T(8,128)(2,1)S(1)} %bitcast.55, ...), custom_call_target="tpu_custom_call", output_to_operand_aliasing={{0}: (5, {}), {1}: (6, {})} | custom-call | flops 1476395008 | bytes 5767168 | tf_op jit(solution)/shard_map/tiles_0/pallas_call | solution.py:289
  63.1 3.0 %collective-permute-done.2 = bf16[2048,256]{1,0:T(8,128)(2,1)S(1)} collective-permute-done((bf16[2048,256]{1,0:T(8,128)(2,1)S(1)}, bf16[2048,256]{1,0:T(8,128)(2,1)S(1)}, u32[]{:S(2)}, u32[]{:S(2)}) %collective-permute-start.2) | collective-permute-done | bytes 1048608 | tf_op jit(solution)/shard_map/ppermute | solution.py:384
  66.1 0.1 collective-permute-start.6
  66.3 3.5 %collective-permute-start.7 = (bf16[1024,256]{1,0:T(8,128)(2,1)S(1)}, bf16[1024,256]{1,0:T(8,128)(2,1)S(1)}, u32[]{:S(2)}, u32[]{:S(2)}) collective-permute-start(bf16[1024,256]{1,0:T(8,128)(2,1)S(1)} %slice.68), channel_id=1, source_target_pairs={{0,12},{1,13},{2,14},{3,15},{4,0},{5,1},{6,2},{7,3},{8,4},{9,5},{1... | collective-permute-start | bytes 1572872 | tf_op jit(solution)/shard_map/ppermute | solution.py:384
  69.7 3.0 %tiles_1.1 = (f32[64,128,256]{2,1,0:T(8,128)S(1)}, bf16[8,16,128,128]{3,2,1,0:T(8,128)(2,1)S(1)}) custom-call(s32[1024]{0:T(1024)S(1)} %bitcast.68, s32[384]{0:T(512)S(1)} %reduce.start_ref.refs_1_, bf16[704,128,128]{2,1,0:T(8,128)(2,1)} %bitcast.77, bf16[16,128,256]{2,1,0:T(8,128)(2,1)S(1)} %bitcast.58, ...), custom_call_target="tpu_custom_call", output_to_operand_aliasing={{0}: (5, {}), {1}: (6, {})} | custom-call | flops 1476395008 | bytes 5767168 | tf_op jit(solution)/shard_map/tiles_1/pallas_call | solution.py:289
  72.8 4.5 %collective-permute-done.8 = bf16[2048,256]{1,0:T(8,128)(2,1)S(1)} collective-permute-done((bf16[2048,256]{1,0:T(8,128)(2,1)S(1)}, bf16[2048,256]{1,0:T(8,128)(2,1)S(1)}, u32[]{:S(2)}, u32[]{:S(2)}) %collective-permute-start.8) | collective-permute-done | bytes 1048608 | tf_op jit(solution)/shard_map/ppermute | solution.py:384
  77.4 0.1 collective-permute-start.10
  77.5 3.3 %collective-permute-start.11 = (bf16[1024,256]{1,0:T(8,128)(2,1)S(1)}, bf16[1024,256]{1,0:T(8,128)(2,1)S(1)}, u32[]{:S(2)}, u32[]{:S(2)}) collective-permute-start(bf16[1024,256]{1,0:T(8,128)(2,1)S(1)} %slice.70), channel_id=1, source_target_pairs={{0,12},{1,13},{2,14},{3,15},{4,0},{5,1},{6,2},{7,3},{8,4},{9,5},{1... | collective-permute-start | bytes 1572872 | tf_op jit(solution)/shard_map/ppermute | solution.py:384
  80.8 2.8 %tiles_2.1 = (f32[64,128,256]{2,1,0:T(8,128)S(1)}, bf16[8,16,128,128]{3,2,1,0:T(8,128)(2,1)S(1)}) custom-call(s32[1024]{0:T(1024)S(1)} %bitcast.69, s32[384]{0:T(512)S(1)} %reduce.start_ref.refs_1_, bf16[704,128,128]{2,1,0:T(8,128)(2,1)} %bitcast.78, bf16[16,128,256]{2,1,0:T(8,128)(2,1)S(1)} %bitcast.57, ...), custom_call_target="tpu_custom_call", output_to_operand_aliasing={{0}: (5, {}), {1}: (6, {})} | custom-call | flops 1476395008 | bytes 5767168 | tf_op jit(solution)/shard_map/tiles_2/pallas_call | solution.py:289
  83.6 5.0 %collective-permute-done.10 = bf16[1024,256]{1,0:T(8,128)(2,1)S(1)} collective-permute-done((bf16[1024,256]{1,0:T(8,128)(2,1)S(1)}, bf16[1024,256]{1,0:T(8,128)(2,1)S(1)}, u32[]{:S(2)}, u32[]{:S(2)}) %collective-permute-start.10) | collective-permute-done | bytes 524320 | tf_op jit(solution)/shard_map/ppermute | solution.py:384
  88.6 2.8 %tiles_3.1 = (f32[64,128,256]{2,1,0:T(8,128)S(1)}, bf16[8,16,128,128]{3,2,1,0:T(8,128)(2,1)S(1)}, bf16[8,128,256]{2,1,0:T(8,128)(2,1)S(1)}, bf16[8,128,256]{2,1,0:T(8,128)(2,1)S(1)}) custom-call(s32[1024]{0:T(1024)S(1)} %bitcast.70, s32[384]{0:T(512)S(1)} %reduce.start_ref.refs_1_, ...), custom_call_target="tpu_custom_call", output_to_operand_aliasing={{0}: (7, {}), {1}: (8, {})} | custom-call | flops 1476395008 | bytes 5767168 | tf_op jit(solution)/shard_map/tiles_3/pallas_call | solution.py:289
  91.3 0.1 collective-permute-start.12
  91.5 0.4 round_rows.1
  91.9 1.4 %collective-permute-done.12 = bf16[1024,256]{1,0:T(8,128)(2,1)S(1)} collective-permute-done((bf16[1024,256]{1,0:T(8,128)(2,1)S(1)}, bf16[1024,256]{1,0:T(8,128)(2,1)S(1)}, u32[]{:S(2)}, u32[]{:S(2)}) %collective-permute-start.12) | collective-permute-done | bytes 524320 | tf_op jit(solution)/shard_map/ppermute | solution.py:412
  93.3 0.2 fusion.4
  93.5 0.2 collective-permute-start.13
  93.7 0.3 fusion.12
  94.0 0.1 fusion.10
  94.2 2.8 %collective-permute-start.16 = (bf16[512,256]{1,0:T(8,128)(2,1)S(1)}, bf16[512,256]{1,0:T(8,128)(2,1)S(1)}, u32[]{:S(2)}, u32[]{:S(2)}) collective-permute-start(bf16[512,256]{1,0:T(8,128)(2,1)S(1)} %get-tuple-element.79), channel_id=1, source_target_pairs={{0,32},{16,48},{32,64},{48,80},{64,96},{80,112},{96,0},{112,16},{1... | collective-permute-start | bytes 786440 | tf_op jit(solution)/shard_map/ppermute | solution.py:412
  97.0 0.5 convert_add_fusion
  97.6 0.1 collective-permute-start.14
  97.7 3.3 %collective-permute-start.15 = (bf16[512,256]{1,0:T(8,128)(2,1)S(1)}, bf16[512,256]{1,0:T(8,128)(2,1)S(1)}, u32[]{:S(2)}, u32[]{:S(2)}) collective-permute-start(bf16[512,256]{1,0:T(8,128)(2,1)S(1)} %slice.113), channel_id=1, source_target_pairs={{0,32},{16,48},{32,64},{48,80},{64,96},{80,112},{96,0},{112,16},{1... | collective-permute-start | bytes 786440 | tf_op jit(solution)/shard_map/ppermute | solution.py:412
  101.0 2.6 %collective-permute-done.16 = bf16[512,256]{1,0:T(8,128)(2,1)S(1)} collective-permute-done((bf16[512,256]{1,0:T(8,128)(2,1)S(1)}, bf16[512,256]{1,0:T(8,128)(2,1)S(1)}, u32[]{:S(2)}, u32[]{:S(2)}) %collective-permute-start.16) | collective-permute-done | bytes 262176 | tf_op jit(solution)/shard_map/ppermute | solution.py:412
  103.7 3.8 %collective-permute-start.17 = (bf16[512,256]{1,0:T(8,128)(2,1)S(1)}, bf16[512,256]{1,0:T(8,128)(2,1)S(1)}, u32[]{:S(2)}, u32[]{:S(2)}) collective-permute-start(bf16[512,256]{1,0:T(8,128)(2,1)S(1)} %fusion.7), channel_id=1, source_target_pairs={{0,32},{16,48},{32,64},{48,80},{64,96},{80,112},{96,0},{112,16},{1... | collective-permute-start | bytes 786440 | tf_op jit(solution)/shard_map/ppermute | solution.py:412
  107.5 0.1 collective-permute-start.19
  107.6 5.4 %collective-permute-done.14 = bf16[512,256]{1,0:T(8,128)(2,1)S(1)} collective-permute-done((bf16[512,256]{1,0:T(8,128)(2,1)S(1)}, bf16[512,256]{1,0:T(8,128)(2,1)S(1)}, u32[]{:S(2)}, u32[]{:S(2)}) %collective-permute-start.14) | collective-permute-done | bytes 262176 | tf_op jit(solution)/shard_map/ppermute | solution.py:412
  113.0 0.1 slice_add_fusion.2
  113.1 1.2 %collective-permute-done.17 = bf16[512,256]{1,0:T(8,128)(2,1)S(1)} collective-permute-done((bf16[512,256]{1,0:T(8,128)(2,1)S(1)}, bf16[512,256]{1,0:T(8,128)(2,1)S(1)}, u32[]{:S(2)}, u32[]{:S(2)}) %collective-permute-start.17) | collective-permute-done | bytes 262176 | tf_op jit(solution)/shard_map/ppermute | solution.py:412
  114.3 0.1 convert_add_fusion.5
  114.4 3.3 %collective-permute-done.19 = bf16[512,256]{1,0:T(8,128)(2,1)S(1)} collective-permute-done((bf16[512,256]{1,0:T(8,128)(2,1)S(1)}, bf16[512,256]{1,0:T(8,128)(2,1)S(1)}, u32[]{:S(2)}, u32[]{:S(2)}) %collective-permute-start.19) | collective-permute-done | bytes 262176 | tf_op jit(solution)/shard_map/ppermute | solution.py:412
  117.7 0.1 convert_add_fusion.4
  117.8 1.2 fusion.2
  (41 shorter events, 0.7 us)
Async XLA Ops:
  0.0 93.7 %copy-start = (bf16[256,256]{1,0:T(8,128)(2,1)S(1)}, bf16[256,256]{1,0:T(8,128)(2,1)}, u32[]{:S(2)}) copy-start(bf16[256,256]{1,0:T(8,128)(2,1)} %param.17) | copy-start | bytes 393220
  0.0 40.1 %copy-start.1 = (s32[1,1,704]{2,1,0:T(1,128)S(1)}, s32[1,1,704]{2,1,0:T(1,128)}, u32[]{:S(2)}) copy-start(s32[1,1,704]{2,1,0:T(1,128)} %param.13) | copy-start | bytes 8452
  0.0 40.1 %copy-start.2 = (s32[1,1,704]{2,1,0:T(1,128)S(1)}, s32[1,1,704]{2,1,0:T(1,128)}, u32[]{:S(2)}) copy-start(s32[1,1,704]{2,1,0:T(1,128)} %param.14) | copy-start | bytes 8452
  36.0 10.5 %collective-permute-start = (bf16[1024,256]{1,0:T(8,128)(2,1)S(1)}, bf16[1024,256]{1,0:T(8,128)(2,1)S(1)}, u32[]{:S(2)}, u32[]{:S(2)}) collective-permute-start(bf16[1024,256]{1,0:T(8,128)(2,1)S(1)} %unpack.1), channel_id=1, source_target_pairs={{0,1},{1,2},{2,3},{3,0},{4,5},{5,6},{6,7},{7,4},{8,9},{9,10},{10,1... | collective-permute-start | bytes 1572872 | tf_op jit(solution)/shard_map/ppermute | solution.py:384
  36.7 9.8 %collective-permute-start.1 = (bf16[1024,256]{1,0:T(8,128)(2,1)S(1)}, bf16[1024,256]{1,0:T(8,128)(2,1)S(1)}, u32[]{:S(2)}, u32[]{:S(2)}) collective-permute-start(bf16[1024,256]{1,0:T(8,128)(2,1)S(1)} %unpack.1), channel_id=1, source_target_pairs={{0,3},{1,0},{2,1},{3,2},{4,7},{5,4},{6,5},{7,6},{8,11},{9,8},{10,9... | collective-permute-start | bytes 1572872 | tf_op jit(solution)/shard_map/ppermute | solution.py:384
  46.5 9.6 %collective-permute-start.4 = (bf16[512,256]{1,0:T(8,128)(2,1)S(1)}, bf16[512,256]{1,0:T(8,128)(2,1)S(1)}, u32[]{:S(2)}, u32[]{:S(2)}) collective-permute-start(bf16[512,256]{1,0:T(8,128)(2,1)S(1)} %slice.65), channel_id=1, source_target_pairs={{0,1},{1,2},{2,3},{3,0},{4,5},{5,6},{6,7},{7,4},{8,9},{9,10},{10,1... | collective-permute-start | bytes 786440 | tf_op jit(solution)/shard_map/ppermute | solution.py:384
  46.6 9.6 %collective-permute-start.5 = (bf16[512,256]{1,0:T(8,128)(2,1)S(1)}, bf16[512,256]{1,0:T(8,128)(2,1)S(1)}, u32[]{:S(2)}, u32[]{:S(2)}) collective-permute-start(bf16[512,256]{1,0:T(8,128)(2,1)S(1)} %slice.66), channel_id=1, source_target_pairs={{0,3},{1,0},{2,1},{3,2},{4,7},{5,4},{6,5},{7,6},{8,11},{9,8},{10,9... | collective-permute-start | bytes 786440 | tf_op jit(solution)/shard_map/ppermute | solution.py:384
  50.0 16.1 %collective-permute-start.2 = (bf16[2048,256]{1,0:T(8,128)(2,1)S(1)}, bf16[2048,256]{1,0:T(8,128)(2,1)S(1)}, u32[]{:S(2)}, u32[]{:S(2)}) collective-permute-start(bf16[2048,256]{1,0:T(8,128)(2,1)S(1)} %pad_maximum_fusion), channel_id=1, source_target_pairs={{0,4},{1,5},{2,6},{3,7},{4,8},{5,9},{6,10},{7,11},{8,12},{9,13},{1... | collective-permute-start | bytes 3145736 | tf_op jit(solution)/shard_map/ppermute | solution.py:384
  50.9 15.2 %collective-permute-start.3 = (bf16[2048,256]{1,0:T(8,128)(2,1)S(1)}, bf16[2048,256]{1,0:T(8,128)(2,1)S(1)}, u32[]{:S(2)}, u32[]{:S(2)}) collective-permute-start(bf16[2048,256]{1,0:T(8,128)(2,1)S(1)} %pad_maximum_fusion), channel_id=1, source_target_pairs={{0,12},{1,13},{2,14},{3,15},{4,0},{5,1},{6,2},{7,3},{8,4},{9,5},{1... | collective-permute-start | bytes 3145736 | tf_op jit(solution)/shard_map/ppermute | solution.py:384
  56.3 21.1 %collective-permute-start.8 = (bf16[2048,256]{1,0:T(8,128)(2,1)S(1)}, bf16[2048,256]{1,0:T(8,128)(2,1)S(1)}, u32[]{:S(2)}, u32[]{:S(2)}) collective-permute-start(bf16[2048,256]{1,0:T(8,128)(2,1)S(1)} %constant_dynamic-update-slice_fusion), channel_id=1, source_target_pairs={{0,4},{1,5},{2,6},{3,7},{4,8},{5,9},{6,10},{7,11},{8,12},{9,13},{1... | collective-permute-start | bytes 3145736 | tf_op jit(solution)/shard_map/ppermute | solution.py:384
  57.9 19.4 %collective-permute-start.9 = (bf16[2048,256]{1,0:T(8,128)(2,1)S(1)}, bf16[2048,256]{1,0:T(8,128)(2,1)S(1)}, u32[]{:S(2)}, u32[]{:S(2)}) collective-permute-start(bf16[2048,256]{1,0:T(8,128)(2,1)S(1)} %constant_dynamic-update-slice_fusion), channel_id=1, source_target_pairs={{0,12},{1,13},{2,14},{3,15},{4,0},{5,1},{6,2},{7,3},{8,4},{9,5},{1... | collective-permute-start | bytes 3145736 | tf_op jit(solution)/shard_map/ppermute | solution.py:384
  66.1 17.4 %collective-permute-start.6 = (bf16[1024,256]{1,0:T(8,128)(2,1)S(1)}, bf16[1024,256]{1,0:T(8,128)(2,1)S(1)}, u32[]{:S(2)}, u32[]{:S(2)}) collective-permute-start(bf16[1024,256]{1,0:T(8,128)(2,1)S(1)} %slice.67), channel_id=1, source_target_pairs={{0,4},{1,5},{2,6},{3,7},{4,8},{5,9},{6,10},{7,11},{8,12},{9,13},{1... | collective-permute-start | bytes 1572872 | tf_op jit(solution)/shard_map/ppermute | solution.py:384
  66.3 17.3 %collective-permute-start.7 = (bf16[1024,256]{1,0:T(8,128)(2,1)S(1)}, bf16[1024,256]{1,0:T(8,128)(2,1)S(1)}, u32[]{:S(2)}, u32[]{:S(2)}) collective-permute-start(bf16[1024,256]{1,0:T(8,128)(2,1)S(1)} %slice.68), channel_id=1, source_target_pairs={{0,12},{1,13},{2,14},{3,15},{4,0},{5,1},{6,2},{7,3},{8,4},{9,5},{1... | collective-permute-start | bytes 1572872 | tf_op jit(solution)/shard_map/ppermute | solution.py:384
  77.4 11.2 %collective-permute-start.10 = (bf16[1024,256]{1,0:T(8,128)(2,1)S(1)}, bf16[1024,256]{1,0:T(8,128)(2,1)S(1)}, u32[]{:S(2)}, u32[]{:S(2)}) collective-permute-start(bf16[1024,256]{1,0:T(8,128)(2,1)S(1)} %slice.69), channel_id=1, source_target_pairs={{0,4},{1,5},{2,6},{3,7},{4,8},{5,9},{6,10},{7,11},{8,12},{9,13},{1... | collective-permute-start | bytes 1572872 | tf_op jit(solution)/shard_map/ppermute | solution.py:384
  77.5 11.1 %collective-permute-start.11 = (bf16[1024,256]{1,0:T(8,128)(2,1)S(1)}, bf16[1024,256]{1,0:T(8,128)(2,1)S(1)}, u32[]{:S(2)}, u32[]{:S(2)}) collective-permute-start(bf16[1024,256]{1,0:T(8,128)(2,1)S(1)} %slice.70), channel_id=1, source_target_pairs={{0,12},{1,13},{2,14},{3,15},{4,0},{5,1},{6,2},{7,3},{8,4},{9,5},{1... | collective-permute-start | bytes 1572872 | tf_op jit(solution)/shard_map/ppermute | solution.py:384
  91.3 2.0 %collective-permute-start.12 = (bf16[1024,256]{1,0:T(8,128)(2,1)S(1)}, bf16[1024,256]{1,0:T(8,128)(2,1)S(1)}, u32[]{:S(2)}, u32[]{:S(2)}) collective-permute-start(bf16[1024,256]{1,0:T(8,128)(2,1)S(1)} %bitcast.74), channel_id=1, source_target_pairs={{0,16},{16,0},{32,48},{48,32},{64,80},{80,64},{96,112},{112,96},{1... | collective-permute-start | bytes 1572872 | tf_op jit(solution)/shard_map/ppermute | solution.py:412
  91.4 2.3 %copy-start.3 = (s32[1024]{0:T(1024)S(1)}, s32[1024]{0:T(1024)}, u32[]{:S(2)}) copy-start(s32[1024]{0:T(1024)} %param.12) | copy-start | bytes 12292
  91.4 2.3 %copy-start.5 = (bf16[256]{0:T(256)(128)(2,1)S(1)}, bf16[256]{0:T(256)(128)(2,1)}, u32[]{:S(2)}) copy-start(bf16[256]{0:T(256)(128)(2,1)} %param.19) | copy-start | bytes 1540
  93.5 3.5 %collective-permute-start.13 = (bf16[3,1024,256]{2,1,0:T(8,128)(2,1)S(1)}, bf16[3,1024,256]{2,1,0:T(8,128)(2,1)S(1)}, u32[]{:S(2)}, u32[]{:S(2)}) collective-permute-start(bf16[3,1024,256]{2,1,0:T(8,128)(2,1)S(1)} %bitcast.73), channel_id=1, source_target_pairs={{0,16},{16,0},{32,48},{48,32},{64,80},{80,64},{96,112},{112,96},{1... | collective-permute-start | bytes 4718600 | tf_op jit(solution)/shard_map/ppermute | solution.py:412
  94.2 9.4 %collective-permute-start.16 = (bf16[512,256]{1,0:T(8,128)(2,1)S(1)}, bf16[512,256]{1,0:T(8,128)(2,1)S(1)}, u32[]{:S(2)}, u32[]{:S(2)}) collective-permute-start(bf16[512,256]{1,0:T(8,128)(2,1)S(1)} %get-tuple-element.79), channel_id=1, source_target_pairs={{0,32},{16,48},{32,64},{48,80},{64,96},{80,112},{96,0},{112,16},{1... | collective-permute-start | bytes 786440 | tf_op jit(solution)/shard_map/ppermute | solution.py:412
  97.0 10.5 %collective-permute-start.18 = (bf16[512,256]{1,0:T(8,128)(2,1)S(1)}, bf16[512,256]{1,0:T(8,128)(2,1)S(1)}, u32[]{:S(2)}, u32[]{:S(2)}) collective-permute-start(bf16[512,256]{1,0:T(8,128)(2,1)S(1)} %get-tuple-element.80), channel_id=1, source_target_pairs={{0,96},{16,112},{32,0},{48,16},{64,32},{80,48},{96,64},{112,80},{1... | collective-permute-start | bytes 786440 | tf_op jit(solution)/shard_map/ppermute | solution.py:412
  97.5 20.3 %copy-start.4 = (bf16[256,256]{1,0:T(8,128)(2,1)S(1)}, bf16[256,256]{1,0:T(8,128)(2,1)}, u32[]{:S(2)}) copy-start(bf16[256,256]{1,0:T(8,128)(2,1)} %param.18) | copy-start | bytes 393220
  97.6 15.4 %collective-permute-start.14 = (bf16[512,256]{1,0:T(8,128)(2,1)S(1)}, bf16[512,256]{1,0:T(8,128)(2,1)S(1)}, u32[]{:S(2)}, u32[]{:S(2)}) collective-permute-start(bf16[512,256]{1,0:T(8,128)(2,1)S(1)} %slice.114), channel_id=1, source_target_pairs={{0,96},{16,112},{32,0},{48,16},{64,32},{80,48},{96,64},{112,80},{1... | collective-permute-start | bytes 786440 | tf_op jit(solution)/shard_map/ppermute | solution.py:412
  97.7 15.3 %collective-permute-start.15 = (bf16[512,256]{1,0:T(8,128)(2,1)S(1)}, bf16[512,256]{1,0:T(8,128)(2,1)S(1)}, u32[]{:S(2)}, u32[]{:S(2)}) collective-permute-start(bf16[512,256]{1,0:T(8,128)(2,1)S(1)} %slice.113), channel_id=1, source_target_pairs={{0,32},{16,48},{32,64},{48,80},{64,96},{80,112},{96,0},{112,16},{1... | collective-permute-start | bytes 786440 | tf_op jit(solution)/shard_map/ppermute | solution.py:412
  103.7 10.6 %collective-permute-start.17 = (bf16[512,256]{1,0:T(8,128)(2,1)S(1)}, bf16[512,256]{1,0:T(8,128)(2,1)S(1)}, u32[]{:S(2)}, u32[]{:S(2)}) collective-permute-start(bf16[512,256]{1,0:T(8,128)(2,1)S(1)} %fusion.7), channel_id=1, source_target_pairs={{0,32},{16,48},{32,64},{48,80},{64,96},{80,112},{96,0},{112,16},{1... | collective-permute-start | bytes 786440 | tf_op jit(solution)/shard_map/ppermute | solution.py:412
  107.5 10.2 %collective-permute-start.19 = (bf16[512,256]{1,0:T(8,128)(2,1)S(1)}, bf16[512,256]{1,0:T(8,128)(2,1)S(1)}, u32[]{:S(2)}, u32[]{:S(2)}) collective-permute-start(bf16[512,256]{1,0:T(8,128)(2,1)S(1)} %fusion.6), channel_id=1, source_target_pairs={{0,96},{16,112},{32,0},{48,16},{64,32},{80,48},{96,64},{112,80},{1... | collective-permute-start | bytes 786440 | tf_op jit(solution)/shard_map/ppermute | solution.py:412

commit v8 on v7

--- a/solution.py
+++ b/solution.py
@@ -27,12 +27,7 @@
     return jnp.where(mask, 1.0, 0.0).astype(jnp.bfloat16)
 
 
-def pack_kernel(home_hbm, table_hbm, out_ref, home_ref, table_ref, sem):
-    home_copy = pltpu.make_async_copy(home_hbm, home_ref, sem.at[0])
-    table_copy = pltpu.make_async_copy(table_hbm, table_ref, sem.at[1])
-    home_copy.start()
-    table_copy.start()
-    home_copy.wait()
+def pack_kernel(home_ref, table_ref, out_ref):
     rows = table_ref.shape[0]
     blocks = home_ref.shape[1]
     home = home_ref[...]
@@ -53,7 +48,6 @@
     place = dest * SLOT_ROWS + rank
     outs = out_ref.shape[0]
     spread = onehot(iota((outs, rows), 0) == place)
-    table_copy.wait()
     data = jnp.dot(spread, table_ref[...], preferred_element_type=jnp.float32)
     lane = iota((256, rows), 0)
     high = jnp.broadcast_to((parts[2:3] + 1).astype(jnp.float32), (256, rows))
@@ -338,14 +332,9 @@
     outgoing = pl.pallas_call(
         pack_kernel,
         out_shape=jax.ShapeDtypeStruct((devices * SLOT_ROWS, width), jnp.bfloat16),
-        in_specs=[pl.BlockSpec(memory_space=pl.ANY)] * 2,
+        in_specs=[vmem, vmem],
         out_specs=vmem,
-        scratch_shapes=[
-            pltpu.VMEM((1, home.shape[0]), jnp.int32),
-            pltpu.VMEM(table.shape, jnp.bfloat16),
-            pltpu.SemaphoreType.DMA((2,)),
-        ],
-        compiler_params=pltpu.CompilerParams(vmem_limit_bytes=60 * MB),
+        compiler_params=big,
         name="pack",
     )(home.reshape(1, -1), table)
     incoming = lax.all_to_all(

time: 120 us -> 119 us (level)
  Pallas kernels: 25.6 us -> 21.6 us
  local copies, waits for them, and re-layouts: 0.48 us -> 2.23 us
    pallas_call x1, Pallas kernels: 5.34 us -> 2.54 us  [per_device(): pl.pallas_call(pack_kernel, out_shape=jax.ShapeDtypeStruct((devices * SLO...]
    unnamed x14 -> x18, local copies, waits for them, and re-layouts: 0.08 us -> 1.84 us
  transfers between devices with their start and end apart: 20 -> 20, of which waited for: 11 -> 12; matrix products, arithmetic and copies ran while one was open for 1% -> 1% of each run, Pallas kernels for 13% -> 13%
where the time goes in v8:
time: 119 us; the launch traced here: 118 us
  starting transfers between devices  31.1 us (26%)
  waiting for transfers between devices  30.8 us (26%)
  blocking collectives  28.4 us (24%)
  Pallas kernels  21.6 us (18%)
  local copies, waits for them, and re-layouts  2.23 us (2%)
  matrix products  1.47 us (1%)
  other arithmetic  1.24 us (1%)
    all_to_all x1, blocking collectives, per_device(): lax.all_to_all(outgoing.reshape(devices, SLOT_ROWS, width), ('row', 'col'...  28.4 us
    ppermute x12, starting transfers between devices, send(): return lax.ppermute(v, ('row', 'col'), panel_perm(turn, step))  20.2 us
    ppermute x12, waiting for transfers between devices, send(): return lax.ppermute(v, ('row', 'col'), panel_perm(turn, step))  16.6 us
    ppermute x8, waiting for transfers between devices, over(): return lax.ppermute(v, 'row', row_perm(dx, flip))  14.2 us
    pallas_call x4, Pallas kernels, run_tiles(): pl.pallas_call(functools.partial(tiles_kernel, stage, n, outs), out_shape...  10.9 us
    ppermute x8, starting transfers between devices, over(): return lax.ppermute(v, 'row', row_perm(dx, flip))  10.8 us
    pallas_call x1, Pallas kernels, open_tiles(): pl.pallas_call(open_kernel, out_shape=[pltpu.VMEM((64, t, width), jnp.flo...  3.74 us
    pallas_call x1, Pallas kernels, per_device(): pl.pallas_call(pack_kernel, out_shape=jax.ShapeDtypeStruct((devices * SLO...  2.54 us
  transfers between devices with their start and end apart: 20, of which 12 were waited for; matrix products, arithmetic and copies ran while one was open for 1% of the time, Pallas kernels for 13%

profile of v8, /device:TPU:6, one launch (start us, length us, event | category | flops | bytes accessed | tf_op | source)
XLA Modules:
  0.0 117.7 jit_solution(2288440526307409398)
XLA Ops:
  0.0 1.1 copy-done.1
  1.1 0.7 copy-done.4
  1.8 2.5 %pack.1 = bf16[2048,256]{1,0:T(8,128)(2,1)S(1)} custom-call(s32[1,512]{1,0:T(1,128)S(1)} %bitcast.74, bf16[1024,256]{1,0:T(8,128)(2,1)S(1)} %copy-done.1), custom_call_target="tpu_custom_call" | custom-call | tf_op jit(solution)/shard_map/pack/pallas_call | solution.py:332
  4.3 28.4 %all_to_all.5 = bf16[128,16,256]{2,1,0:T(8,128)(2,1)S(1)} all-to-all(bf16[128,16,256]{2,1,0:T(8,128)(2,1)S(1)} %bitcast.57), channel_id=1, replica_groups=mesh['row'=8,'col'=16] {'row','col'}, dimensions={0} | all-to-all | bytes 2097152 | tf_op jit(solution)/shard_map/all_to_all | solution.py:340
  32.7 2.1 %unpack.1 = bf16[1024,256]{1,0:T(8,128)(2,1)S(1)} custom-call(bf16[2048,256]{1,0:T(8,128)(2,1)S(1)} %bitcast.56), custom_call_target="tpu_custom_call" | custom-call | tf_op jit(solution)/shard_map/unpack/pallas_call | solution.py:348
  34.8 0.7 collective-permute-start
  35.5 2.6 %collective-permute-start.1 = (bf16[1024,256]{1,0:T(8,128)(2,1)S(1)}, bf16[1024,256]{1,0:T(8,128)(2,1)S(1)}, u32[]{:S(2)}, u32[]{:S(2)}) collective-permute-start(bf16[1024,256]{1,0:T(8,128)(2,1)S(1)} %unpack.1), channel_id=1, source_target_pairs={{0,3},{1,0},{2,1},{3,2},{4,7},{5,4},{6,5},{7,6},{8,11},{9,8},{10,9... | collective-permute-start | bytes 1572872 | tf_op jit(solution)/shard_map/ppermute | solution.py:373
  38.7 0.1 pad_add_fusion.where_ref
  38.8 1.9 %plan.1 = (s32[1,1024]{1,0:T(1,128)S(1)}, s32[1,384]{1,0:T(1,128)S(1)}) custom-call(s32[4]{0:T(128)S(1)} %pad_add_fusion.where_ref, s32[1]{0:T(128)} %bitcast.54.count_ref, s32[1,704]{1,0:T(1,128)S(1)} %bitcast.72, s32[1,704]{1,0:T(1,128)S(1)} %bitcast.73), custom_call_target="tpu_custom_call" | custom-call | tf_op jit(solution)/shard_map/plan/pallas_call | solution.py:357
  40.7 3.7 %tiles_open.1 = (f32[64,128,256]{2,1,0:T(8,128)S(1)}, bf16[8,16,128,128]{3,2,1,0:T(8,128)(2,1)S(1)}) custom-call(s32[1024]{0:T(1024)S(1)} %bitcast.67, s32[384]{0:T(512)S(1)} %reduce.start_ref.refs_1_, bf16[704,128,128]{2,1,0:T(8,128)(2,1)} %bitcast.77), custom_call_target="tpu_custom_call" | custom-call | tf_op jit(solution)/shard_map/tiles_open/pallas_call | solution.py:252
  44.5 0.8 collective-permute-done
  45.4 3.3 %collective-permute-start.5 = (bf16[512,256]{1,0:T(8,128)(2,1)S(1)}, bf16[512,256]{1,0:T(8,128)(2,1)S(1)}, u32[]{:S(2)}, u32[]{:S(2)}) collective-permute-start(bf16[512,256]{1,0:T(8,128)(2,1)S(1)} %slice.66), channel_id=1, source_target_pairs={{0,3},{1,0},{2,1},{3,2},{4,7},{5,4},{6,5},{7,6},{8,11},{9,8},{10,9... | collective-permute-start | bytes 786440 | tf_op jit(solution)/shard_map/ppermute | solution.py:373
  48.7 0.9 collective-permute-start.2
  49.6 2.4 %collective-permute-start.3 = (bf16[2048,256]{1,0:T(8,128)(2,1)S(1)}, bf16[2048,256]{1,0:T(8,128)(2,1)S(1)}, u32[]{:S(2)}, u32[]{:S(2)}) collective-permute-start(bf16[2048,256]{1,0:T(8,128)(2,1)S(1)} %pad_maximum_fusion), channel_id=1, source_target_pairs={{0,12},{1,13},{2,14},{3,15},{4,0},{5,1},{6,2},{7,3},{8,4},{9,5},{1... | collective-permute-start | bytes 3145736 | tf_op jit(solution)/shard_map/ppermute | solution.py:373
  52.1 2.8 %collective-permute-done.4 = bf16[512,256]{1,0:T(8,128)(2,1)S(1)} collective-permute-done((bf16[512,256]{1,0:T(8,128)(2,1)S(1)}, bf16[512,256]{1,0:T(8,128)(2,1)S(1)}, u32[]{:S(2)}, u32[]{:S(2)}) %collective-permute-start.4) | collective-permute-done | bytes 262176 | tf_op jit(solution)/shard_map/ppermute | solution.py:373
  55.0 1.7 %collective-permute-start.8 = (bf16[2048,256]{1,0:T(8,128)(2,1)S(1)}, bf16[2048,256]{1,0:T(8,128)(2,1)S(1)}, u32[]{:S(2)}, u32[]{:S(2)}) collective-permute-start(bf16[2048,256]{1,0:T(8,128)(2,1)S(1)} %constant_dynamic-update-slice_fusion), channel_id=1, source_target_pairs={{0,4},{1,5},{2,6},{3,7},{4,8},{5,9},{6,10},{7,11},{8,12},{9,13},{1... | collective-permute-start | bytes 3145736 | tf_op jit(solution)/shard_map/ppermute | solution.py:373
  56.7 1.6 %collective-permute-start.9 = (bf16[2048,256]{1,0:T(8,128)(2,1)S(1)}, bf16[2048,256]{1,0:T(8,128)(2,1)S(1)}, u32[]{:S(2)}, u32[]{:S(2)}) collective-permute-start(bf16[2048,256]{1,0:T(8,128)(2,1)S(1)} %constant_dynamic-update-slice_fusion), channel_id=1, source_target_pairs={{0,12},{1,13},{2,14},{3,15},{4,0},{5,1},{6,2},{7,3},{8,4},{9,5},{1... | collective-permute-start | bytes 3145736 | tf_op jit(solution)/shard_map/ppermute | solution.py:373
  58.3 3.5 %tiles_0.1 = (f32[64,128,256]{2,1,0:T(8,128)S(1)}, bf16[8,16,128,128]{3,2,1,0:T(8,128)(2,1)S(1)}) custom-call(s32[1024]{0:T(1024)S(1)} %bitcast.68, s32[384]{0:T(512)S(1)} %reduce.start_ref.refs_1_, bf16[704,128,128]{2,1,0:T(8,128)(2,1)} %bitcast.78, bf16[16,128,256]{2,1,0:T(8,128)(2,1)S(1)} %bitcast.55, ...), custom_call_target="tpu_custom_call", output_to_operand_aliasing={{0}: (5, {}), {1}: (6, {})} | custom-call | flops 1476395008 | bytes 5767168 | tf_op jit(solution)/shard_map/tiles_0/pallas_call | solution.py:283
  61.8 3.0 %collective-permute-done.2 = bf16[2048,256]{1,0:T(8,128)(2,1)S(1)} collective-permute-done((bf16[2048,256]{1,0:T(8,128)(2,1)S(1)}, bf16[2048,256]{1,0:T(8,128)(2,1)S(1)}, u32[]{:S(2)}, u32[]{:S(2)}) %collective-permute-start.2) | collective-permute-done | bytes 1048608 | tf_op jit(solution)/shard_map/ppermute | solution.py:373
  65.0 3.3 %collective-permute-start.7 = (bf16[1024,256]{1,0:T(8,128)(2,1)S(1)}, bf16[1024,256]{1,0:T(8,128)(2,1)S(1)}, u32[]{:S(2)}, u32[]{:S(2)}) collective-permute-start(bf16[1024,256]{1,0:T(8,128)(2,1)S(1)} %slice.68), channel_id=1, source_target_pairs={{0,12},{1,13},{2,14},{3,15},{4,0},{5,1},{6,2},{7,3},{8,4},{9,5},{1... | collective-permute-start | bytes 1572872 | tf_op jit(solution)/shard_map/ppermute | solution.py:373
  68.3 3.1 %tiles_1.1 = (f32[64,128,256]{2,1,0:T(8,128)S(1)}, bf16[8,16,128,128]{3,2,1,0:T(8,128)(2,1)S(1)}) custom-call(s32[1024]{0:T(1024)S(1)} %bitcast.69, s32[384]{0:T(512)S(1)} %reduce.start_ref.refs_1_, bf16[704,128,128]{2,1,0:T(8,128)(2,1)} %bitcast.79, bf16[16,128,256]{2,1,0:T(8,128)(2,1)S(1)} %bitcast.59, ...), custom_call_target="tpu_custom_call", output_to_operand_aliasing={{0}: (5, {}), {1}: (6, {})} | custom-call | flops 1476395008 | bytes 5767168 | tf_op jit(solution)/shard_map/tiles_1/pallas_call | solution.py:283
  71.4 4.6 %collective-permute-done.8 = bf16[2048,256]{1,0:T(8,128)(2,1)S(1)} collective-permute-done((bf16[2048,256]{1,0:T(8,128)(2,1)S(1)}, bf16[2048,256]{1,0:T(8,128)(2,1)S(1)}, u32[]{:S(2)}, u32[]{:S(2)}) %collective-permute-start.8) | collective-permute-done | bytes 1048608 | tf_op jit(solution)/shard_map/ppermute | solution.py:373
  76.1 0.1 collective-permute-start.10
  76.2 3.5 %collective-permute-start.11 = (bf16[1024,256]{1,0:T(8,128)(2,1)S(1)}, bf16[1024,256]{1,0:T(8,128)(2,1)S(1)}, u32[]{:S(2)}, u32[]{:S(2)}) collective-permute-start(bf16[1024,256]{1,0:T(8,128)(2,1)S(1)} %slice.70), channel_id=1, source_target_pairs={{0,12},{1,13},{2,14},{3,15},{4,0},{5,1},{6,2},{7,3},{8,4},{9,5},{1... | collective-permute-start | bytes 1572872 | tf_op jit(solution)/shard_map/ppermute | solution.py:373
  79.7 2.2 %tiles_2.1 = (f32[64,128,256]{2,1,0:T(8,128)S(1)}, bf16[8,16,128,128]{3,2,1,0:T(8,128)(2,1)S(1)}) custom-call(s32[1024]{0:T(1024)S(1)} %bitcast.70, s32[384]{0:T(512)S(1)} %reduce.start_ref.refs_1_, bf16[704,128,128]{2,1,0:T(8,128)(2,1)} %bitcast.80, bf16[16,128,256]{2,1,0:T(8,128)(2,1)S(1)} %bitcast.58, ...), custom_call_target="tpu_custom_call", output_to_operand_aliasing={{0}: (5, {}), {1}: (6, {})} | custom-call | flops 1476395008 | bytes 5767168 | tf_op jit(solution)/shard_map/tiles_2/pallas_call | solution.py:283
  82.0 5.3 %collective-permute-done.10 = bf16[1024,256]{1,0:T(8,128)(2,1)S(1)} collective-permute-done((bf16[1024,256]{1,0:T(8,128)(2,1)S(1)}, bf16[1024,256]{1,0:T(8,128)(2,1)S(1)}, u32[]{:S(2)}, u32[]{:S(2)}) %collective-permute-start.10) | collective-permute-done | bytes 524320 | tf_op jit(solution)/shard_map/ppermute | solution.py:373
  87.3 2.1 %tiles_3.1 = (f32[64,128,256]{2,1,0:T(8,128)S(1)}, bf16[8,16,128,128]{3,2,1,0:T(8,128)(2,1)S(1)}, bf16[8,128,256]{2,1,0:T(8,128)(2,1)S(1)}, bf16[8,128,256]{2,1,0:T(8,128)(2,1)S(1)}) custom-call(s32[1024]{0:T(1024)S(1)} %bitcast.71, s32[384]{0:T(512)S(1)} %reduce.start_ref.refs_1_, ...), custom_call_target="tpu_custom_call", output_to_operand_aliasing={{0}: (7, {}), {1}: (8, {})} | custom-call | flops 1476395008 | bytes 5767168 | tf_op jit(solution)/shard_map/tiles_3/pallas_call | solution.py:283
  89.4 1.6 %collective-permute-start.12 = (bf16[1024,256]{1,0:T(8,128)(2,1)S(1)}, bf16[1024,256]{1,0:T(8,128)(2,1)S(1)}, u32[]{:S(2)}, u32[]{:S(2)}) collective-permute-start(bf16[1024,256]{1,0:T(8,128)(2,1)S(1)} %bitcast.76), channel_id=1, source_target_pairs={{0,16},{16,0},{32,48},{48,32},{64,80},{80,64},{96,112},{112,96},{1... | collective-permute-start | bytes 1572872 | tf_op jit(solution)/shard_map/ppermute | solution.py:401
  91.0 0.4 round_rows.1
  91.5 1.1 collective-permute-done.12
  92.6 0.2 fusion.4
  92.7 0.5 collective-permute-start.13
  93.2 0.3 fusion.12
  93.5 0.1 fusion.10
  93.7 2.0 %collective-permute-start.16 = (bf16[512,256]{1,0:T(8,128)(2,1)S(1)}, bf16[512,256]{1,0:T(8,128)(2,1)S(1)}, u32[]{:S(2)}, u32[]{:S(2)}) collective-permute-start(bf16[512,256]{1,0:T(8,128)(2,1)S(1)} %get-tuple-element.79), channel_id=1, source_target_pairs={{0,32},{16,48},{32,64},{48,80},{64,96},{80,112},{96,0},{112,16},{1... | collective-permute-start | bytes 786440 | tf_op jit(solution)/shard_map/ppermute | solution.py:401
  95.8 0.5 collective-permute-done.13
  96.2 0.5 convert_add_fusion
  96.8 0.2 collective-permute-start.14
  97.0 3.2 %collective-permute-start.15 = (bf16[512,256]{1,0:T(8,128)(2,1)S(1)}, bf16[512,256]{1,0:T(8,128)(2,1)S(1)}, u32[]{:S(2)}, u32[]{:S(2)}) collective-permute-start(bf16[512,256]{1,0:T(8,128)(2,1)S(1)} %slice.113), channel_id=1, source_target_pairs={{0,32},{16,48},{32,64},{48,80},{64,96},{80,112},{96,0},{112,16},{1... | collective-permute-start | bytes 786440 | tf_op jit(solution)/shard_map/ppermute | solution.py:401
  100.2 2.7 %collective-permute-done.16 = bf16[512,256]{1,0:T(8,128)(2,1)S(1)} collective-permute-done((bf16[512,256]{1,0:T(8,128)(2,1)S(1)}, bf16[512,256]{1,0:T(8,128)(2,1)S(1)}, u32[]{:S(2)}, u32[]{:S(2)}) %collective-permute-start.16) | collective-permute-done | bytes 262176 | tf_op jit(solution)/shard_map/ppermute | solution.py:401
  102.9 3.2 %collective-permute-start.17 = (bf16[512,256]{1,0:T(8,128)(2,1)S(1)}, bf16[512,256]{1,0:T(8,128)(2,1)S(1)}, u32[]{:S(2)}, u32[]{:S(2)}) collective-permute-start(bf16[512,256]{1,0:T(8,128)(2,1)S(1)} %fusion.7), channel_id=1, source_target_pairs={{0,32},{16,48},{32,64},{48,80},{64,96},{80,112},{96,0},{112,16},{1... | collective-permute-start | bytes 786440 | tf_op jit(solution)/shard_map/ppermute | solution.py:401
  106.3 5.4 %collective-permute-done.14 = bf16[512,256]{1,0:T(8,128)(2,1)S(1)} collective-permute-done((bf16[512,256]{1,0:T(8,128)(2,1)S(1)}, bf16[512,256]{1,0:T(8,128)(2,1)S(1)}, u32[]{:S(2)}, u32[]{:S(2)}) %collective-permute-start.14) | collective-permute-done | bytes 262176 | tf_op jit(solution)/shard_map/ppermute | solution.py:401
  111.7 0.1 slice_add_fusion.2
  111.8 1.5 %collective-permute-done.17 = bf16[512,256]{1,0:T(8,128)(2,1)S(1)} collective-permute-done((bf16[512,256]{1,0:T(8,128)(2,1)S(1)}, bf16[512,256]{1,0:T(8,128)(2,1)S(1)}, u32[]{:S(2)}, u32[]{:S(2)}) %collective-permute-start.17) | collective-permute-done | bytes 262176 | tf_op jit(solution)/shard_map/ppermute | solution.py:401
  113.3 0.1 convert_add_fusion.5
  113.4 3.0 %collective-permute-done.19 = bf16[512,256]{1,0:T(8,128)(2,1)S(1)} collective-permute-done((bf16[512,256]{1,0:T(8,128)(2,1)S(1)}, bf16[512,256]{1,0:T(8,128)(2,1)S(1)}, u32[]{:S(2)}, u32[]{:S(2)}) %collective-permute-start.19) | collective-permute-done | bytes 262176 | tf_op jit(solution)/shard_map/ppermute | solution.py:401
  116.4 0.1 convert_add_fusion.4
  116.5 1.2 fusion.2
  (45 shorter events, 1.0 us)
Async XLA Ops:
  0.0 93.2 %copy-start = (bf16[256,256]{1,0:T(8,128)(2,1)S(1)}, bf16[256,256]{1,0:T(8,128)(2,1)}, u32[]{:S(2)}) copy-start(bf16[256,256]{1,0:T(8,128)(2,1)} %param.17) | copy-start | bytes 393220
  0.0 1.1 copy-start.1
  1.1 0.7 copy-start.4
  1.8 37.1 %copy-start.2 = (s32[1,1,704]{2,1,0:T(1,128)S(1)}, s32[1,1,704]{2,1,0:T(1,128)}, u32[]{:S(2)}) copy-start(s32[1,1,704]{2,1,0:T(1,128)} %param.13) | copy-start | bytes 8452
  1.8 37.1 %copy-start.3 = (s32[1,1,704]{2,1,0:T(1,128)S(1)}, s32[1,1,704]{2,1,0:T(1,128)}, u32[]{:S(2)}) copy-start(s32[1,1,704]{2,1,0:T(1,128)} %param.14) | copy-start | bytes 8452
  34.8 10.5 %collective-permute-start = (bf16[1024,256]{1,0:T(8,128)(2,1)S(1)}, bf16[1024,256]{1,0:T(8,128)(2,1)S(1)}, u32[]{:S(2)}, u32[]{:S(2)}) collective-permute-start(bf16[1024,256]{1,0:T(8,128)(2,1)S(1)} %unpack.1), channel_id=1, source_target_pairs={{0,1},{1,2},{2,3},{3,0},{4,5},{5,6},{6,7},{7,4},{8,9},{9,10},{10,1... | collective-permute-start | bytes 1572872 | tf_op jit(solution)/shard_map/ppermute | solution.py:373
  35.5 9.8 %collective-permute-start.1 = (bf16[1024,256]{1,0:T(8,128)(2,1)S(1)}, bf16[1024,256]{1,0:T(8,128)(2,1)S(1)}, u32[]{:S(2)}, u32[]{:S(2)}) collective-permute-start(bf16[1024,256]{1,0:T(8,128)(2,1)S(1)} %unpack.1), channel_id=1, source_target_pairs={{0,3},{1,0},{2,1},{3,2},{4,7},{5,4},{6,5},{7,6},{8,11},{9,8},{10,9... | collective-permute-start | bytes 1572872 | tf_op jit(solution)/shard_map/ppermute | solution.py:373
  45.3 9.6 %collective-permute-start.4 = (bf16[512,256]{1,0:T(8,128)(2,1)S(1)}, bf16[512,256]{1,0:T(8,128)(2,1)S(1)}, u32[]{:S(2)}, u32[]{:S(2)}) collective-permute-start(bf16[512,256]{1,0:T(8,128)(2,1)S(1)} %slice.65), channel_id=1, source_target_pairs={{0,1},{1,2},{2,3},{3,0},{4,5},{5,6},{6,7},{7,4},{8,9},{9,10},{10,1... | collective-permute-start | bytes 786440 | tf_op jit(solution)/shard_map/ppermute | solution.py:373
  45.4 9.6 %collective-permute-start.5 = (bf16[512,256]{1,0:T(8,128)(2,1)S(1)}, bf16[512,256]{1,0:T(8,128)(2,1)S(1)}, u32[]{:S(2)}, u32[]{:S(2)}) collective-permute-start(bf16[512,256]{1,0:T(8,128)(2,1)S(1)} %slice.66), channel_id=1, source_target_pairs={{0,3},{1,0},{2,1},{3,2},{4,7},{5,4},{6,5},{7,6},{8,11},{9,8},{10,9... | collective-permute-start | bytes 786440 | tf_op jit(solution)/shard_map/ppermute | solution.py:373
  48.7 16.1 %collective-permute-start.2 = (bf16[2048,256]{1,0:T(8,128)(2,1)S(1)}, bf16[2048,256]{1,0:T(8,128)(2,1)S(1)}, u32[]{:S(2)}, u32[]{:S(2)}) collective-permute-start(bf16[2048,256]{1,0:T(8,128)(2,1)S(1)} %pad_maximum_fusion), channel_id=1, source_target_pairs={{0,4},{1,5},{2,6},{3,7},{4,8},{5,9},{6,10},{7,11},{8,12},{9,13},{1... | collective-permute-start | bytes 3145736 | tf_op jit(solution)/shard_map/ppermute | solution.py:373
  49.6 15.2 %collective-permute-start.3 = (bf16[2048,256]{1,0:T(8,128)(2,1)S(1)}, bf16[2048,256]{1,0:T(8,128)(2,1)S(1)}, u32[]{:S(2)}, u32[]{:S(2)}) collective-permute-start(bf16[2048,256]{1,0:T(8,128)(2,1)S(1)} %pad_maximum_fusion), channel_id=1, source_target_pairs={{0,12},{1,13},{2,14},{3,15},{4,0},{5,1},{6,2},{7,3},{8,4},{9,5},{1... | collective-permute-start | bytes 3145736 | tf_op jit(solution)/shard_map/ppermute | solution.py:373
  55.0 21.1 %collective-permute-start.8 = (bf16[2048,256]{1,0:T(8,128)(2,1)S(1)}, bf16[2048,256]{1,0:T(8,128)(2,1)S(1)}, u32[]{:S(2)}, u32[]{:S(2)}) collective-permute-start(bf16[2048,256]{1,0:T(8,128)(2,1)S(1)} %constant_dynamic-update-slice_fusion), channel_id=1, source_target_pairs={{0,4},{1,5},{2,6},{3,7},{4,8},{5,9},{6,10},{7,11},{8,12},{9,13},{1... | collective-permute-start | bytes 3145736 | tf_op jit(solution)/shard_map/ppermute | solution.py:373
  56.7 19.4 %collective-permute-start.9 = (bf16[2048,256]{1,0:T(8,128)(2,1)S(1)}, bf16[2048,256]{1,0:T(8,128)(2,1)S(1)}, u32[]{:S(2)}, u32[]{:S(2)}) collective-permute-start(bf16[2048,256]{1,0:T(8,128)(2,1)S(1)} %constant_dynamic-update-slice_fusion), channel_id=1, source_target_pairs={{0,12},{1,13},{2,14},{3,15},{4,0},{5,1},{6,2},{7,3},{8,4},{9,5},{1... | collective-permute-start | bytes 3145736 | tf_op jit(solution)/shard_map/ppermute | solution.py:373
  64.9 17.1 %collective-permute-start.6 = (bf16[1024,256]{1,0:T(8,128)(2,1)S(1)}, bf16[1024,256]{1,0:T(8,128)(2,1)S(1)}, u32[]{:S(2)}, u32[]{:S(2)}) collective-permute-start(bf16[1024,256]{1,0:T(8,128)(2,1)S(1)} %slice.67), channel_id=1, source_target_pairs={{0,4},{1,5},{2,6},{3,7},{4,8},{5,9},{6,10},{7,11},{8,12},{9,13},{1... | collective-permute-start | bytes 1572872 | tf_op jit(solution)/shard_map/ppermute | solution.py:373
  65.0 17.0 %collective-permute-start.7 = (bf16[1024,256]{1,0:T(8,128)(2,1)S(1)}, bf16[1024,256]{1,0:T(8,128)(2,1)S(1)}, u32[]{:S(2)}, u32[]{:S(2)}) collective-permute-start(bf16[1024,256]{1,0:T(8,128)(2,1)S(1)} %slice.68), channel_id=1, source_target_pairs={{0,12},{1,13},{2,14},{3,15},{4,0},{5,1},{6,2},{7,3},{8,4},{9,5},{1... | collective-permute-start | bytes 1572872 | tf_op jit(solution)/shard_map/ppermute | solution.py:373
  76.1 11.2 %collective-permute-start.10 = (bf16[1024,256]{1,0:T(8,128)(2,1)S(1)}, bf16[1024,256]{1,0:T(8,128)(2,1)S(1)}, u32[]{:S(2)}, u32[]{:S(2)}) collective-permute-start(bf16[1024,256]{1,0:T(8,128)(2,1)S(1)} %slice.69), channel_id=1, source_target_pairs={{0,4},{1,5},{2,6},{3,7},{4,8},{5,9},{6,10},{7,11},{8,12},{9,13},{1... | collective-permute-start | bytes 1572872 | tf_op jit(solution)/shard_map/ppermute | solution.py:373
  76.2 11.1 %collective-permute-start.11 = (bf16[1024,256]{1,0:T(8,128)(2,1)S(1)}, bf16[1024,256]{1,0:T(8,128)(2,1)S(1)}, u32[]{:S(2)}, u32[]{:S(2)}) collective-permute-start(bf16[1024,256]{1,0:T(8,128)(2,1)S(1)} %slice.70), channel_id=1, source_target_pairs={{0,12},{1,13},{2,14},{3,15},{4,0},{5,1},{6,2},{7,3},{8,4},{9,5},{1... | collective-permute-start | bytes 1572872 | tf_op jit(solution)/shard_map/ppermute | solution.py:373
  89.4 3.2 %collective-permute-start.12 = (bf16[1024,256]{1,0:T(8,128)(2,1)S(1)}, bf16[1024,256]{1,0:T(8,128)(2,1)S(1)}, u32[]{:S(2)}, u32[]{:S(2)}) collective-permute-start(bf16[1024,256]{1,0:T(8,128)(2,1)S(1)} %bitcast.76), channel_id=1, source_target_pairs={{0,16},{16,0},{32,48},{48,32},{64,80},{80,64},{96,112},{112,96},{1... | collective-permute-start | bytes 1572872 | tf_op jit(solution)/shard_map/ppermute | solution.py:401
  91.0 2.2 %copy-start.5 = (s32[1024]{0:T(1024)S(1)}, s32[1024]{0:T(1024)}, u32[]{:S(2)}) copy-start(s32[1024]{0:T(1024)} %param.12) | copy-start | bytes 12292
  91.0 2.2 %copy-start.7 = (bf16[256]{0:T(256)(128)(2,1)S(1)}, bf16[256]{0:T(256)(128)(2,1)}, u32[]{:S(2)}) copy-start(bf16[256]{0:T(256)(128)(2,1)} %param.19) | copy-start | bytes 1540
  92.7 3.5 %collective-permute-start.13 = (bf16[3,1024,256]{2,1,0:T(8,128)(2,1)S(1)}, bf16[3,1024,256]{2,1,0:T(8,128)(2,1)S(1)}, u32[]{:S(2)}, u32[]{:S(2)}) collective-permute-start(bf16[3,1024,256]{2,1,0:T(8,128)(2,1)S(1)} %bitcast.75), channel_id=1, source_target_pairs={{0,16},{16,0},{32,48},{48,32},{64,80},{80,64},{96,112},{112,96},{1... | collective-permute-start | bytes 4718600 | tf_op jit(solution)/shard_map/ppermute | solution.py:401
  93.7 9.2 %collective-permute-start.16 = (bf16[512,256]{1,0:T(8,128)(2,1)S(1)}, bf16[512,256]{1,0:T(8,128)(2,1)S(1)}, u32[]{:S(2)}, u32[]{:S(2)}) collective-permute-start(bf16[512,256]{1,0:T(8,128)(2,1)S(1)} %get-tuple-element.79), channel_id=1, source_target_pairs={{0,32},{16,48},{32,64},{48,80},{64,96},{80,112},{96,0},{112,16},{1... | collective-permute-start | bytes 786440 | tf_op jit(solution)/shard_map/ppermute | solution.py:401
  95.7 10.5 %collective-permute-start.18 = (bf16[512,256]{1,0:T(8,128)(2,1)S(1)}, bf16[512,256]{1,0:T(8,128)(2,1)S(1)}, u32[]{:S(2)}, u32[]{:S(2)}) collective-permute-start(bf16[512,256]{1,0:T(8,128)(2,1)S(1)} %get-tuple-element.80), channel_id=1, source_target_pairs={{0,96},{16,112},{32,0},{48,16},{64,32},{80,48},{96,64},{112,80},{1... | collective-permute-start | bytes 786440 | tf_op jit(solution)/shard_map/ppermute | solution.py:401
  96.7 19.8 %copy-start.6 = (bf16[256,256]{1,0:T(8,128)(2,1)S(1)}, bf16[256,256]{1,0:T(8,128)(2,1)}, u32[]{:S(2)}) copy-start(bf16[256,256]{1,0:T(8,128)(2,1)} %param.18) | copy-start | bytes 393220
  96.8 14.9 %collective-permute-start.14 = (bf16[512,256]{1,0:T(8,128)(2,1)S(1)}, bf16[512,256]{1,0:T(8,128)(2,1)S(1)}, u32[]{:S(2)}, u32[]{:S(2)}) collective-permute-start(bf16[512,256]{1,0:T(8,128)(2,1)S(1)} %slice.114), channel_id=1, source_target_pairs={{0,96},{16,112},{32,0},{48,16},{64,32},{80,48},{96,64},{112,80},{1... | collective-permute-start | bytes 786440 | tf_op jit(solution)/shard_map/ppermute | solution.py:401
  97.0 14.7 %collective-permute-start.15 = (bf16[512,256]{1,0:T(8,128)(2,1)S(1)}, bf16[512,256]{1,0:T(8,128)(2,1)S(1)}, u32[]{:S(2)}, u32[]{:S(2)}) collective-permute-start(bf16[512,256]{1,0:T(8,128)(2,1)S(1)} %slice.113), channel_id=1, source_target_pairs={{0,32},{16,48},{32,64},{48,80},{64,96},{80,112},{96,0},{112,16},{1... | collective-permute-start | bytes 786440 | tf_op jit(solution)/shard_map/ppermute | solution.py:401
  102.9 10.4 %collective-permute-start.17 = (bf16[512,256]{1,0:T(8,128)(2,1)S(1)}, bf16[512,256]{1,0:T(8,128)(2,1)S(1)}, u32[]{:S(2)}, u32[]{:S(2)}) collective-permute-start(bf16[512,256]{1,0:T(8,128)(2,1)S(1)} %fusion.7), channel_id=1, source_target_pairs={{0,32},{16,48},{32,64},{48,80},{64,96},{80,112},{96,0},{112,16},{1... | collective-permute-start | bytes 786440 | tf_op jit(solution)/shard_map/ppermute | solution.py:401
  106.2 10.2 %collective-permute-start.19 = (bf16[512,256]{1,0:T(8,128)(2,1)S(1)}, bf16[512,256]{1,0:T(8,128)(2,1)S(1)}, u32[]{:S(2)}, u32[]{:S(2)}) collective-permute-start(bf16[512,256]{1,0:T(8,128)(2,1)S(1)} %fusion.6), channel_id=1, source_target_pairs={{0,96},{16,112},{32,0},{48,16},{64,32},{80,48},{96,64},{112,80},{1... | collective-permute-start | bytes 786440 | tf_op jit(solution)/shard_map/ppermute | solution.py:401
